TPU v7x, 512 devices: a whole 4x8x8 slice. The times are simulated.
512 devices in a mesh: dp: 16 (over y, core), expert: 8 (over z), tensor: 4 (over x).
Axes of the slice: x: 4, y: 8, z: 8, core: 2. Of those that a mesh axis runs over, the one named last changes fastest.
Arguments:
- queries: bfloat16 [8192, 4096], P(('dp', 'expert'), 'tensor'), may hold values from -6 to 6
- keys: bfloat16 [8192, 512], P(('dp', 'expert'), 'tensor'), may hold values from -6 to 6
- values: bfloat16 [8192, 512], P(('dp', 'expert'), 'tensor'), may hold values from -6 to 6
- image_start: int32 [16, 4], P('dp'), may hold values from 0 to 448, as said below
- norm_gain: bfloat16 [4096], P('tensor'), may hold values from 0.099609375 to 1.8984375
- expert_ids: int32 [8192, 8], P(('dp', 'expert')), may hold values from 0 to 127, all different within a row; in each aligned block of 64 rows (0 to 63, 64 to 127, ...) at most 8 rows name the same one
- gate_values: float32 [8192, 8], P(('dp', 'expert')), may hold values from 0.03 to 0.3
- gate_weight: bfloat16 [128, 4096, 768], P(('dp', 'expert'), 'tensor'), may hold values from -0.09375 to 0.09375
- up_weight: bfloat16 [128, 4096, 768], P(('dp', 'expert'), 'tensor'), may hold values from -0.09375 to 0.09375
- down_weight: bfloat16 [128, 768, 4096], P(('dp', 'expert'), None, 'tensor'), may hold values from -0.21875 to 0.21875
Outputs:
- mixed: bfloat16 [8192, 4096], P(('dp', 'expert'), 'tensor')
Inputs may be any that keep to these rules, and one draw needn't show every extreme that they name: The images of a rollout are in order and disjoint; image k covers 64 positions from image_start and lies within positions 2 * k * 64 to 2 * (k + 1) * 64 - 1. `expert_ids`: among the rows of one device, no expert is named by more than 8 rows.
All inputs are finite; a program needn't handle non-finite values.
Results may differ from a plain program's by a relative error of at most 0.029.
Values may be sent and summed in bfloat16 or wider, within the bound.
No kernel may reach another device: no remote copies, remote signals or barrier semaphores. Data moves between devices by JAX's collectives and lax.ppermute only.
A program may use at most 64 MiB of HBM per device.

v0:
```python
import math

import jax
import jax.numpy as jnp
from jax import lax
from jax.sharding import PartitionSpec as P

D = 4096


def per_device(
    queries,
    keys,
    values,
    image_start,
    norm_gain,
    expert_ids,
    gate_values,
    gate_weight,
    up_weight,
    down_weight,
):
    tok_rows = queries.shape[0]
    head_size = keys.shape[1]
    heads_here = queries.shape[1] // head_size
    block_index = lax.axis_index("expert")
    query_pos = block_index * tok_rows + jnp.arange(tok_rows, dtype=jnp.int32)
    starts = image_start[0]
    inside = (query_pos[:, None] >= starts[None, :]) & (
        query_pos[:, None] < starts[None, :] + tok_rows
    )
    span_ends = jnp.broadcast_to(starts[None, :] + tok_rows - 1, inside.shape)
    visible_end = jnp.max(jnp.where(inside, span_ends, query_pos[:, None]), axis=1)
    grouped = queries.reshape(tok_rows, heads_here, head_size)
    score_scale = 1.0 / math.sqrt(head_size)
    running_max = jnp.full((heads_here, tok_rows), -1e30, jnp.float32)
    key_piece = lax.all_gather(keys, "expert", axis=0, tiled=True)
    value_piece = lax.all_gather(values, "expert", axis=0, tiled=True)
    piece_rows = key_piece.shape[0]
    scores = (
        jnp.einsum("thd,nd->htn", grouped, key_piece, preferred_element_type=jnp.float32)
        * score_scale
    )
    key_pos = jnp.arange(piece_rows, dtype=jnp.int32)
    visible = (key_pos[None, :] <= visible_end[:, None])[None]
    masked = jnp.where(visible, scores, -1e30)
    new_max = jnp.maximum(running_max, jnp.max(masked, axis=2))
    weights = jnp.where(visible, jnp.exp(scores - new_max[:, :, None]), 0.0)
    row_total = jnp.sum(weights, axis=2)
    update = jnp.einsum(
        "htn,nd->htd", weights.astype(jnp.bfloat16), value_piece, preferred_element_type=jnp.float32
    )
    weighted_sum = update
    running_max, row_total, weighted_sum = (new_max, row_total, weighted_sum)
    result = weighted_sum / row_total[:, :, None]
    attended = (
        jnp.transpose(result, (1, 0, 2))
        .reshape(tok_rows, heads_here * head_size)
        .astype(jnp.bfloat16)
    )
    wide = attended.astype(jnp.float32)
    square_total = lax.psum(jnp.sum(wide * wide, axis=1), "tensor")
    mean_square = square_total / D
    normed = (
        wide * lax.rsqrt(mean_square + 1e-06)[:, None] * norm_gain.astype(jnp.float32)
    ).astype(jnp.bfloat16)
    feat_dev = normed.shape[1]
    experts_all = lax.axis_size("dp") * lax.axis_size("expert")
    route_width = expert_ids.shape[1]
    capacity = min(tok_rows, 2 * tok_rows * route_width // experts_all)
    flat_ids = expert_ids.reshape(-1)
    routes = flat_ids.shape[0]
    onehot = (flat_ids[:, None] == jnp.arange(experts_all, dtype=jnp.int32)[None, :]).astype(
        jnp.bfloat16
    )
    earlier = (jnp.arange(routes)[:, None] > jnp.arange(routes)[None, :]).astype(jnp.bfloat16)
    before = jnp.dot(earlier, onehot, preferred_element_type=jnp.float32)
    slot_index = jnp.sum(before * onehot.astype(jnp.float32), axis=1).astype(jnp.int32)
    target = flat_ids * capacity + slot_index
    slot_ids = jnp.arange(experts_all * capacity, dtype=jnp.int32)
    dispatch_mat = jnp.any(
        slot_ids[:, None, None] == target.reshape(tok_rows, route_width)[None], axis=2
    ).astype(jnp.bfloat16)
    outgoing = jnp.dot(dispatch_mat, normed, preferred_element_type=jnp.float32).astype(
        jnp.bfloat16
    )
    outgoing = outgoing.reshape(experts_all, capacity, feat_dev)
    arrived = lax.all_to_all(outgoing, ("dp", "expert"), split_axis=0, concat_axis=0, tiled=True)
    slot_rows = arrived.reshape(experts_all * capacity, feat_dev)
    gate_rows = gate_weight[0]
    up_rows = up_weight[0]
    gate_part = jnp.dot(slot_rows, gate_rows, preferred_element_type=jnp.float32)
    up_part = jnp.dot(slot_rows, up_rows, preferred_element_type=jnp.float32)
    gate_sum, up_sum = (
        lax.psum(gate_part.astype(jnp.bfloat16), "tensor").astype(jnp.float32),
        lax.psum(up_part.astype(jnp.bfloat16), "tensor").astype(jnp.float32),
    )
    hidden = (jax.nn.silu(gate_sum) * up_sum).astype(jnp.bfloat16)
    produced = jnp.dot(hidden, down_weight[0], preferred_element_type=jnp.float32).astype(
        jnp.bfloat16
    )
    produced = produced.reshape(experts_all, capacity, feat_dev)
    returned = lax.all_to_all(produced, ("dp", "expert"), split_axis=0, concat_axis=0, tiled=True)
    picked = returned.reshape(experts_all * capacity, feat_dev)[target].reshape(
        tok_rows, route_width, feat_dev
    )
    expert_mix = jnp.sum(gate_values[:, :, None] * picked.astype(jnp.float32), axis=1)
    return (wide + expert_mix).astype(jnp.bfloat16)


def solution(mesh):
    return jax.shard_map(
        per_device,
        mesh=mesh,
        in_specs=(
            P(("dp", "expert"), "tensor"),
            P(("dp", "expert"), "tensor"),
            P(("dp", "expert"), "tensor"),
            P("dp", None),
            P("tensor"),
            P(("dp", "expert"), None),
            P(("dp", "expert"), None),
            P(("dp", "expert"), "tensor", None),
            P(("dp", "expert"), "tensor", None),
            P(("dp", "expert"), None, "tensor"),
        ),
        out_specs=P(("dp", "expert"), "tensor"),
        check_vma=False,
    )
```

profile of v0, /device:TPU:1, one launch (start us, length us, event | category | flops | bytes accessed | tf_op | source)
XLA Modules:
  0.0 315.1 jit_solution(14604552703327720750)
XLA Ops:
  6.5 0.0 copy-start
  6.5 0.0 all-reduce.3.cloned.1.call-start
  6.5 0.8 add_bitcast_fusion.1
  7.3 0.7 select_reduce_fusion.1
  8.1 0.1 iota_compare_fusion.5
  8.2 25.9 %all_gather.6 = bf16[512,128]{1,0:T(8,128)(2,1)S(1)} all-gather(bf16[64,128]{1,0:T(8,128)(2,1)} %param.11), channel_id=1, replica_groups=mesh['dp'=16,'expert'=8,'tensor'=4] {'expert'}, dimensions={0}, use_global_device_ids=true | all-gather | bytes 147456 | tf_op jit(solution)/shard_map/all_gather | solution.py:37
  34.1 1.3 select_reduce_fusion
  35.3 0.0 copy-start.1
  35.4 18.5 %all_gather.7 = bf16[512,128]{1,0:T(8,128)(2,1)S(1)} all-gather(bf16[64,128]{1,0:T(8,128)(2,1)} %param.12), channel_id=1, replica_groups=mesh['dp'=16,'expert'=8,'tensor'=4] {'expert'}, dimensions={0}, use_global_device_ids=true | all-gather | bytes 147456 | tf_op jit(solution)/shard_map/all_gather | solution.py:38
  53.9 0.0 copy-start.3
  53.9 0.4 fusion.27
  54.3 0.5 multiply_reduce_fusion
  54.7 8.5 %psum.21 = f32[64]{0:T(128)S(1)} all-reduce(f32[64]{0:T(128)S(1)} %get-tuple-element.13), channel_id=1, replica_groups=mesh['dp'=16,'expert'=8,'tensor'=4] {'tensor'}, use_global_device_ids=true, to_apply=%region_6.7 | all-reduce | flops 64 | bytes 512 | tf_op jit(solution)/shard_map/psum | solution.py:62
  63.2 0.0 copy-done.1
  63.2 0.1 copy.22
  63.3 0.1 eq.29
  63.4 0.3 fusion.26
  63.7 0.1 convert_element_type.86
  63.8 0.7 fusion.10
  64.5 0.0 copy-done.3
  64.5 0.8 convert_bitcast_fusion.1
  65.3 0.0 copy-start.4
  65.3 79.8 %all_to_all.10 = bf16[128,8,1024]{2,1,0:T(8,128)(2,1)S(1)} all-to-all(bf16[128,8,1024]{2,1,0:T(8,128)(2,1)S(1)} %convert_bitcast_fusion.1), channel_id=1, replica_groups=mesh['dp'=16,'expert'=8,'tensor'=4] {'dp','expert'}, dimensions={0} | all-to-all | bytes 4194304 | tf_op jit(solution)/shard_map/all_to_all | solution.py:88
  145.1 0.0 copy-done.4
  145.1 0.0 copy-start.5
  145.1 3.0 fusion.11
  148.1 0.0 copy-done.5
  148.1 2.9 fusion.14
  151.0 0.0 all-reduce.3.cloned.1.call-update
  151.1 77.2 %all-reduce.3.cloned.1.call-done = (bf16[1024,768]{1,0:T(8,128)(2,1)}, bf16[1024,768]{1,0:T(8,128)(2,1)}) async-done(((bf16[1024,768]{1,0:T(8,128)(2,1)}, bf16[1024,768]{1,0:T(8,128)(2,1)}), (bf16[1024,768]{1,0:T(8,128)(2,1)}, bf16[1024,768]{1,0:T(8,128)(2,1)})) %all-reduce.3.cloned.1.call-update) | async-done | bytes 3145744 | tf_op jit(solution)/shard_map/psum | solution.py:96
  228.2 0.0 copy-done
  228.2 5.3 %convert_bitcast_fusion = bf16[128,8,1024]{2,1,0:T(8,128)(2,1)} fusion(bf16[1024,768]{1,0:T(8,128)(2,1)} %get-tuple-element.5, bf16[1024,768]{1,0:T(8,128)(2,1)} %get-tuple-element.6, bf16[1,768,1024]{2,1,0:T(8,128)(2,1)S(1)} %copy-done), kind=kOutput, calls=%fused_computation.14 | convolution fusion | flops 1617952768 | bytes 6815744 | tf_op jit(solution)/shard_map/dot_general | solution.py:99
  233.5 0.0 copy-start.2
  233.5 14.9 %all-to-all-start.1 = ((bf16[128,8,1024]{2,1,0:T(8,128)(2,1)}), bf16[128,8,1024]{2,1,0:T(8,128)(2,1)}, u32[]{:S(2)}, u32[]{:S(2)}) async-start(bf16[128,8,1024]{2,1,0:T(8,128)(2,1)} %convert_bitcast_fusion), calls=%async_computation.1 | async-start | bytes 4194304 | tf_op jit(solution)/shard_map/all_to_all | solution.py:103
  248.4 0.1 mul.83
  248.5 0.0 copy-done.2
  248.5 0.1 copy.21
  248.6 53.6 %all-to-all-done.1 = bf16[128,8,1024]{2,1,0:T(8,128)(2,1)} async-done(((bf16[128,8,1024]{2,1,0:T(8,128)(2,1)}), bf16[128,8,1024]{2,1,0:T(8,128)(2,1)}, u32[]{:S(2)}, u32[]{:S(2)}) %all-to-all-start.1) | async-done | bytes 2097184 | tf_op jit(solution)/shard_map/all_to_all | solution.py:103
  302.2 4.6 %gather_fusion = bf16[512,1024]{1,0:T(8,128)(2,1)S(1)} fusion(bf16[1024,1024]{1,0:T(8,128)(2,1)} %bitcast.14, s32[1024]{0:T(1024)S(1)} %pad_clamp_fusion), kind=kCustom, calls=%fused_computation | custom fusion | bytes 2099200 | tf_op jit(solution)/shard_map/gather | solution.py:104
  306.8 0.7 fusion.5
  307.5 0.7 fusion.35
  (8 shorter events, 0.0 us)
Async XLA Ops:
  6.5 221.7 %copy-start = (bf16[1,768,1024]{2,1,0:T(8,128)(2,1)S(1)}, bf16[1,768,1024]{2,1,0:T(8,128)(2,1)}, u32[]{:S(2)}) copy-start(bf16[1,768,1024]{2,1,0:T(8,128)(2,1)} %param.19) | copy-start | bytes 4718596
  6.5 221.7 %all-reduce.3.cloned.1.call-start = ((), (), s32[]{:S(2)}) async-start(), calls=%async_computation.2 | async-start | bytes 6291456 | tf_op jit(solution)/shard_map/psum | solution.py:96
  35.3 27.9 %copy-start.1 = (s32[64,8]{0,1:T(8,128)S(1)}, s32[64,8]{0,1:T(8,128)}, u32[]{:S(2)}) copy-start(s32[64,8]{0,1:T(8,128)} %param.15) | copy-start | bytes 6148
  53.9 10.6 %copy-start.3 = (bf16[1024]{0:T(1024)(128)(2,1)S(1)}, bf16[1024]{0:T(1024)(128)(2,1)}, u32[]{:S(2)}) copy-start(bf16[1024]{0:T(1024)(128)(2,1)} %param.14) | copy-start | bytes 6148
  65.3 79.8 %copy-start.4 = (bf16[1,1024,768]{2,1,0:T(8,128)(2,1)S(1)}, bf16[1,1024,768]{2,1,0:T(8,128)(2,1)}, u32[]{:S(2)}) copy-start(bf16[1,1024,768]{2,1,0:T(8,128)(2,1)} %param.17) | copy-start | bytes 4718596
  145.1 3.0 copy-start.5
  233.5 15.0 %copy-start.2 = (f32[64,8]{0,1:T(8,128)S(1)}, f32[64,8]{0,1:T(8,128)}, u32[]{:S(2)}) copy-start(f32[64,8]{0,1:T(8,128)} %param.16) | copy-start | bytes 6148
  233.5 68.7 %all-to-all-start.1 = ((bf16[128,8,1024]{2,1,0:T(8,128)(2,1)}), bf16[128,8,1024]{2,1,0:T(8,128)(2,1)}, u32[]{:S(2)}, u32[]{:S(2)}) async-start(bf16[128,8,1024]{2,1,0:T(8,128)(2,1)} %convert_bitcast_fusion), calls=%async_computation.1 | async-start | bytes 4194304 | tf_op jit(solution)/shard_map/all_to_all | solution.py:103
Sparse Core Ops, SparseCore 0:
  151.2 76.9 all-reduce.2
where the time goes:
time: 315 us
  blocking collectives  133 us (42%)
  waiting for transfers between devices  131 us (42%)
  starting transfers between devices  14.9 us (5%)
  matrix products  14 us (4%)
  between operations  13.5 us (4%)
  local copies, waits for them, and re-layouts  5.05 us (2%)
  other arithmetic  4.09 us (1%)
    all_to_all x1, blocking collectives, per_device(): lax.all_to_all(outgoing, ('dp', 'expert'), split_axis=0, concat_axis=0, t...  79.8 us
    psum x1, waiting for transfers between devices, per_device(): lax.psum(up_part.astype(jnp.bfloat16), 'tensor').astype(jnp.float32)  77.2 us
    all_to_all x1, waiting for transfers between devices, per_device(): lax.all_to_all(produced, ('dp', 'expert'), split_axis=0, concat_axis=0, t...  53.6 us
    all_gather x1, blocking collectives, per_device(): key_piece = lax.all_gather(keys, 'expert', axis=0, tiled=True)  25.9 us
    all_gather x1, blocking collectives, per_device(): value_piece = lax.all_gather(values, 'expert', axis=0, tiled=True)  18.5 us
    all_to_all x1, starting transfers between devices, per_device(): lax.all_to_all(produced, ('dp', 'expert'), split_axis=0, concat_axis=0, t...  14.9 us
    psum x1, blocking collectives, per_device(): square_total = lax.psum(jnp.sum(wide * wide, axis=1), 'tensor')  8.47 us
  transfers between devices with their start and end apart: 2, of which 2 were waited for; matrix products, arithmetic and copies ran while one was open for 0% of the time, Pallas kernels for 0%

commit v1 on v0

v1 whole, which is shorter than its diff:
```python
import functools
import math

import jax
import jax.numpy as jnp
from jax import lax
from jax.experimental import pallas as pl
from jax.experimental.pallas import tpu as pltpu
from jax.sharding import Mesh
from jax.sharding import PartitionSpec as P

D = 4096
CAP = 8
LANES = 128
BF = jnp.bfloat16
F32 = jnp.float32
GROUP = ("y", "expert")


def ring(size, step):
    return [(i, (i + step) % size) for i in range(size)]


def whole(shape):
    return pl.BlockSpec(shape, lambda *_: (0,) * len(shape))


def attention(queries, keys, values, image_start):
    tok_rows, head_size = keys.shape
    heads_here = queries.shape[1] // head_size
    blocks = lax.axis_size("expert")
    query_pos = lax.axis_index("expert") * tok_rows + jnp.arange(tok_rows, dtype=jnp.int32)
    starts = image_start[0]
    inside = (query_pos[:, None] >= starts[None, :]) & (
        query_pos[:, None] < starts[None, :] + tok_rows
    )
    ends = jnp.broadcast_to(starts[None, :] + tok_rows - 1, inside.shape)
    visible_end = jnp.max(jnp.where(inside, ends, query_pos[:, None]), axis=1)
    grouped = queries.reshape(tok_rows, heads_here, head_size)
    own = jnp.concatenate([keys, values], axis=1)
    copies = jnp.broadcast_to(own[None], (blocks,) + own.shape)
    both = lax.all_to_all(copies, "expert", split_axis=0, concat_axis=0, tiled=True)
    both = both.reshape(blocks * tok_rows, 2 * head_size)
    all_keys, all_values = both[:, :head_size], both[:, head_size:]
    scores = jnp.einsum("thd,nd->htn", grouped, all_keys, preferred_element_type=F32)
    scores = scores * (1.0 / math.sqrt(head_size))
    key_pos = jnp.arange(all_keys.shape[0], dtype=jnp.int32)
    visible = (key_pos[None, :] <= visible_end[:, None])[None]
    row_max = jnp.max(jnp.where(visible, scores, -1e30), axis=2, keepdims=True)
    weights = jnp.where(visible, jnp.exp(scores - row_max), 0.0)
    row_total = jnp.sum(weights, axis=2)
    summed = jnp.einsum("htn,nd->htd", weights.astype(BF), all_values, preferred_element_type=F32)
    result = summed / row_total[:, :, None]
    return jnp.transpose(result, (1, 0, 2)).reshape(tok_rows, heads_here * head_size).astype(BF)


def gate_up_kernel(here, rows, gain, gate, up, *rest, size, waits):
    outs, scaled = rest[waits : waits + size], rest[waits + size]
    block = rows.shape[0] // size
    hidden = gate.shape[1]
    step = pl.program_id(0)

    @pl.when(step == 0)
    def _():
        lane = lax.broadcasted_iota(jnp.int32, (block, LANES), 1)
        for k in range(size):
            at = lax.rem(here[0] + k, size) * block
            wide = rows[pl.ds(pl.multiple_of(at, block), block), :].astype(F32)
            squares = jnp.sum(wide * wide, axis=1, keepdims=True)
            high = squares.astype(BF).astype(F32)
            extra = jnp.where(lane == 0, high, jnp.where(lane == 1, squares - high, 0.0))
            outs[k][:, 2 * hidden :] = extra.astype(BF)
            scaled[pl.ds(k * block, block), :] = (wide * gain[...].astype(F32)).astype(BF)

    def product(weight, low):
        part = jnp.dot(scaled[...], weight[...], preferred_element_type=F32).astype(BF)
        for k in range(size):
            outs[k][:, low : low + hidden] = part[k * block : (k + 1) * block, :]

    @pl.when(step == 0)
    def _():
        product(gate, 0)

    @pl.when(step == 1)
    def _():
        product(up, hidden)


def gate_up(here, rows, gain, gate, up, after):
    size = lax.axis_size("tensor")
    feat, hidden = gate.shape
    block = rows.shape[0] // size
    width = 2 * hidden + LANES
    kernel = functools.partial(gate_up_kernel, size=size, waits=len(after))
    return pl.pallas_call(
        kernel,
        grid_spec=pltpu.PrefetchScalarGridSpec(
            num_scalar_prefetch=1,
            grid=(2,),
            in_specs=[whole(rows.shape), whole((1, feat)), whole(gate.shape), whole(up.shape)]
            + [pl.BlockSpec(memory_space=pl.ANY)] * len(after),
            out_specs=[whole((block, width))] * size,
            scratch_shapes=[pltpu.VMEM(rows.shape, BF)],
        ),
        out_shape=[jax.ShapeDtypeStruct((block, width), BF)] * size,
        compiler_params=pltpu.CompilerParams(vmem_limit_bytes=32 * 1024 * 1024),
        cost_estimate=pl.CostEstimate(
            flops=4 * rows.shape[0] * feat * hidden,
            bytes_accessed=2 * (rows.size + 2 * gate.size + rows.shape[0] * width),
            transcendentals=0,
        ),
    )(here, rows, gain, gate, up, *after)


def down_kernel(here, *refs, size, waits):
    pieces, down = refs[:size], refs[size]
    made, hidden = refs[size + 1 + waits], refs[size + 2 + waits]
    block = pieces[0].shape[0]

    @pl.when(pl.program_id(0) == 0)
    def _():
        for k in range(size):
            at = lax.rem(here[0] + size - k, size) * block
            hidden[pl.ds(pl.multiple_of(at, block), block), :] = pieces[k][...]

    made[...] = jnp.dot(hidden[...], down[...], preferred_element_type=F32).astype(BF)


def down_product(here, pieces, down, after):
    size = len(pieces)
    block, hidden = pieces[0].shape
    feat = down.shape[1]
    half = feat // 2
    rows = size * block
    return pl.pallas_call(
        functools.partial(down_kernel, size=size, waits=len(after)),
        grid_spec=pltpu.PrefetchScalarGridSpec(
            num_scalar_prefetch=1,
            grid=(2,),
            in_specs=[whole((block, hidden))] * size
            + [pl.BlockSpec((hidden, half), lambda i, _: (0, i))]
            + [pl.BlockSpec(memory_space=pl.ANY)] * len(after),
            out_specs=pl.BlockSpec((rows, half), lambda i, _: (0, i)),
            scratch_shapes=[pltpu.VMEM((rows, hidden), BF)],
        ),
        out_shape=jax.ShapeDtypeStruct((rows, feat), BF),
        compiler_params=pltpu.CompilerParams(vmem_limit_bytes=32 * 1024 * 1024),
        cost_estimate=pl.CostEstimate(
            flops=2 * rows * hidden * feat,
            bytes_accessed=2 * (rows * hidden + hidden * feat + rows * feat),
            transcendentals=0,
        ),
    )(here, *pieces, down, *after)


def silu_product(parts, hidden):
    total = parts[0].astype(F32)
    for part in parts[1:]:
        total = total + part.astype(F32)
    squares = total[:, 2 * hidden : 2 * hidden + 1] + total[:, 2 * hidden + 1 : 2 * hidden + 2]
    scale = lax.rsqrt(squares / D + 1e-06)
    gate_sum = total[:, :hidden] * scale
    up_sum = total[:, hidden : 2 * hidden] * scale
    return (jax.nn.silu(gate_sum) * up_sum).astype(BF)


def exchange(block):
    return lax.all_to_all(block, GROUP, split_axis=0, concat_axis=0, tiled=True)


def swap(block):
    return lax.ppermute(block, "core", [(0, 1), (1, 0)])


def per_device(
    queries,
    keys,
    values,
    image_start,
    norm_gain,
    expert_ids,
    gate_values,
    gate_weight,
    up_weight,
    down_weight,
):
    tok_rows, feat = queries.shape
    hidden_size = gate_weight.shape[2]
    size = lax.axis_size("tensor")
    zs = lax.axis_size("expert")
    peers = lax.axis_size("y") * zs
    rows = peers * CAP
    core = lax.axis_index("core")
    here = lax.axis_index("tensor").astype(jnp.int32)[None]
    gain = norm_gain[None]
    gate_rows, up_rows, down_rows = gate_weight[0], up_weight[0], down_weight[0]

    token = jnp.arange(tok_rows, dtype=jnp.int32)
    earlier = (token[:, None] < token[None, :]).astype(BF)
    level = jnp.arange(CAP, dtype=jnp.int32)[None, :, None]
    peer = jnp.arange(peers, dtype=jnp.int32)

    def plan(side):
        experts = (peer // zs * 2 + side) * zs + peer % zs
        named = expert_ids.T[:, None, :] == experts[None, :, None]
        member = jnp.any(named, axis=0)
        gate_of = jnp.sum(jnp.where(named, gate_values.T[:, None, :], 0.0), axis=0)
        rank = jnp.dot(member.astype(BF), earlier, preferred_element_type=F32)
        place = jnp.where(member, rank.astype(jnp.int32), -1)
        hit = place[:, None, :] == level
        high = lax.reduce_precision(gate_of, 8, 7)
        gates = jnp.concatenate([high, gate_of - high], axis=1)
        mix = jnp.where(jnp.concatenate([hit, hit], axis=2), gates[:, None, :], 0.0)
        pick = hit.astype(BF).reshape(rows, tok_rows)
        return pick, mix.astype(BF).reshape(rows, 2 * tok_rows)

    pick_near, mix_near = plan(core)
    pick_far, mix_far = plan(1 - core)
    attended = attention(queries, keys, values, image_start)

    def outgoing(pick):
        return jnp.dot(pick, attended, preferred_element_type=F32).astype(BF)

    def blocks(flat):
        return flat.reshape(peers, CAP, feat)

    def reduce_parts(parts):
        got = [parts[0]]
        for step in range(1, size):
            got.append(lax.ppermute(parts[step], "tensor", ring(size, step)))
        return silu_product(got, hidden_size)

    def spread(piece):
        return [piece] + [lax.ppermute(piece, "tensor", ring(size, k)) for k in range(1, size)]

    def combine(mix, returned):
        both = lax.dot_general(
            mix,
            returned.reshape(rows, feat),
            (((0,), (0,)), ((), ())),
            preferred_element_type=F32,
        )
        return both[:tok_rows] + both[tok_rows:]

    near = exchange(blocks(outgoing(pick_near))).reshape(rows, feat)
    far = exchange(blocks(swap(outgoing(pick_far)))).reshape(rows, feat)

    near_parts = gate_up(here, near, gain, gate_rows, up_rows, [])
    near_hidden = reduce_parts(near_parts)
    far_parts = gate_up(here, far, gain, gate_rows, up_rows, [near_hidden])
    near_made = down_product(here, spread(near_hidden), down_rows, [far_parts[0]])
    near_back = exchange(blocks(near_made))
    far_hidden = reduce_parts(far_parts)
    far_made = down_product(here, spread(far_hidden), down_rows, [])
    far_back = exchange(blocks(swap(far_made)))

    mixed = attended.astype(F32) + combine(mix_near, near_back) + combine(mix_far, far_back)
    return mixed.astype(BF)


def solution(mesh):
    dp, expert, tensor = mesh.devices.shape
    split = Mesh(
        mesh.devices.reshape(dp // 2, 2, expert, tensor), ("y", "core", "expert", "tensor")
    )
    both = ("y", "core", "expert")
    return jax.shard_map(
        per_device,
        mesh=split,
        in_specs=(
            P(both, "tensor"),
            P(both, "tensor"),
            P(both, "tensor"),
            P(("y", "core"), None),
            P("tensor"),
            P(both, None),
            P(both, None),
            P(both, "tensor", None),
            P(both, "tensor", None),
            P(both, None, "tensor"),
        ),
        out_specs=P(both, "tensor"),
        check_vma=False,
    )
```

time: 315 us -> 230 us (0.73); the launches traced: 315 us -> 226 us
  blocking collectives: 133 us -> 0 us
  starting transfers between devices: 14.9 us -> 98.9 us
  waiting for transfers between devices: 131 us -> 99.5 us
  between operations: 13.5 us -> 0.42 us
  matrix products: 14 us -> 3.63 us
  Pallas kernels: 0 us -> 9.73 us
    all_to_all x1 -> x0, blocking collectives: 79.8 us -> none  [per_device(): lax.all_to_all(outgoing, ('dp', 'expert'), split_axis=0, concat_axis=0, t...]
    psum x1 -> x0, waiting for transfers between devices: 77.2 us -> none  [per_device(): lax.psum(up_part.astype(jnp.bfloat16), 'tensor').astype(jnp.float32)]
    ppermute x0 -> x14, starting transfers between devices: none -> 45.4 us  [the longest x6 19.7 us: spread(): lax.ppermute(piece, 'tensor', ring(size, k))]
    ppermute x0 -> x14, waiting for transfers between devices: none -> 45.2 us  [the longest x6 21.1 us: spread(): lax.ppermute(piece, 'tensor', ring(size, k))]
    all_gather x2 -> x0, blocking collectives: 44.4 us -> none  [the longest x1 25.9 us: per_device(): key_piece = lax.all_gather(keys, 'expert', axis=0, tiled=True)]
    all_to_all x1 -> x5, starting transfers between devices: 14.9 us -> 53.4 us  [the longest x4 42.6 us: exchange(): return lax.all_to_all(block, GROUP, split_axis=0, concat_axis=0, tiled=True)]
    dot_general x7 -> x8, matrix products: 14 us -> 3.63 us  [the longest x2 1.83 us: outgoing(): return jnp.dot(pick, attended, preferred_element_type=F32).astype(BF)]
    pallas_call x0 -> x4, Pallas kernels: none -> 9.73 us  [the longest x2 5.22 us: gate_up(): pl.pallas_call(kernel, grid_spec=pltpu.PrefetchScalarGridSpec(num_scalar_...]
  transfers between devices with their start and end apart: 2 -> 19, of which waited for: 2 -> 12; matrix products, arithmetic and copies ran while one was open for 0% -> 3% of each run, Pallas kernels for 0% -> 4%
where the time goes in v1:
time: 230 us; the launch traced here: 226 us
  waiting for transfers between devices  99.5 us (43%)
  starting transfers between devices  98.9 us (43%)
  Pallas kernels  9.73 us (4%)
  other arithmetic  7.02 us (3%)
  local copies, waits for them, and re-layouts  6.37 us (3%)
  matrix products  3.63 us (2%)
    all_to_all x4, waiting for transfers between devices, exchange(): return lax.all_to_all(block, GROUP, split_axis=0, concat_axis=0, tiled=True)  46.5 us
    all_to_all x4, starting transfers between devices, exchange(): return lax.all_to_all(block, GROUP, split_axis=0, concat_axis=0, tiled=True)  42.6 us
    ppermute x6, waiting for transfers between devices, spread(): lax.ppermute(piece, 'tensor', ring(size, k))  21.1 us
    ppermute x6, starting transfers between devices, spread(): lax.ppermute(piece, 'tensor', ring(size, k))  19.7 us
    ppermute x6, waiting for transfers between devices, reduce_parts(): got.append(lax.ppermute(parts[step], 'tensor', ring(size, step)))  19.3 us
    ppermute x6, starting transfers between devices, reduce_parts(): got.append(lax.ppermute(parts[step], 'tensor', ring(size, step)))  18.3 us
    all_to_all x1, starting transfers between devices, attention(): lax.all_to_all(copies, 'expert', split_axis=0, concat_axis=0, tiled=True)  10.9 us
    all_to_all x1, waiting for transfers between devices, attention(): lax.all_to_all(copies, 'expert', split_axis=0, concat_axis=0, tiled=True)  7.9 us
  transfers between devices with their start and end apart: 19, of which 12 were waited for; matrix products, arithmetic and copies ran while one was open for 3% of the time, Pallas kernels for 4%

profile of v1, /device:TPU:1, one launch (start us, length us, event | category | flops | bytes accessed | tf_op | source)
XLA Modules:
  0.0 225.6 jit_solution(17883752082821265626)
XLA Ops:
  0.0 0.8 pad_maximum_fusion
  0.8 0.7 broadcast_in_dim.106
  1.5 10.9 %all-to-all-start = ((bf16[8,64,256]{2,1,0:T(8,128)(2,1)}), bf16[8,64,256]{2,1,0:T(8,128)(2,1)S(1)}, u32[]{:S(2)}, u32[]{:S(2)}) async-start(bf16[8,64,256]{2,1,0:T(8,128)(2,1)} %broadcast_in_dim.106), calls=%async_computation | async-start | bytes 524288 | tf_op jit(solution)/shard_map/all_to_all | solution.py:42
  12.4 0.7 add_bitcast_fusion.1
  13.0 0.8 compare_reduce_fusion.1
  13.9 0.7 select_reduce_fusion.1
  14.6 0.1 iota_compare_fusion.2
  14.7 0.1 fusion.15
  14.8 7.9 %all-to-all-done = bf16[8,64,256]{2,1,0:T(8,128)(2,1)S(1)} async-done(((bf16[8,64,256]{2,1,0:T(8,128)(2,1)}), bf16[8,64,256]{2,1,0:T(8,128)(2,1)S(1)}, u32[]{:S(2)}, u32[]{:S(2)}) %all-to-all-start) | async-done | bytes 262176 | tf_op jit(solution)/shard_map/all_to_all | solution.py:42
  22.7 0.3 fusion.10
  23.0 0.4 fusion.56
  23.4 0.3 fusion.13
  23.7 1.4 fusion.1
  25.1 9.0 %all-to-all-start.1 = ((bf16[64,8,1024]{2,1,0:T(8,128)(2,1)}), bf16[64,8,1024]{2,1,0:T(8,128)(2,1)S(1)}, u32[]{:S(2)}, u32[]{:S(2)}) async-start(bf16[64,8,1024]{2,1,0:T(8,128)(2,1)} %fusion.1), calls=%async_computation.1 | async-start | bytes 2097152 | tf_op jit(solution)/shard_map/all_to_all | solution.py:168
  34.2 0.1 fusion.14
  34.3 0.4 convolution_convert_fusion
  34.7 3.5 %collective-permute-start.6 = (bf16[512,1024]{1,0:T(8,128)(2,1)S(1)}, bf16[512,1024]{1,0:T(8,128)(2,1)}, u32[]{:S(2)}, u32[]{:S(2)}) collective-permute-start(bf16[512,1024]{1,0:T(8,128)(2,1)S(1)} %convolution_convert_fusion), channel_id=1, source_target_pairs={{0,32},{32,0},{1,33},{33,1},{2,34},{34,2},{3,35},{35,3},{4,36},{36... | collective-permute-start | bytes 3145736 | tf_op jit(solution)/shard_map/ppermute | solution.py:172
  38.2 2.4 %collective-permute-done.6 = bf16[512,1024]{1,0:T(8,128)(2,1)} collective-permute-done((bf16[512,1024]{1,0:T(8,128)(2,1)S(1)}, bf16[512,1024]{1,0:T(8,128)(2,1)}, u32[]{:S(2)}, u32[]{:S(2)}) %collective-permute-start.6) | collective-permute-done | bytes 1048608 | tf_op jit(solution)/shard_map/ppermute | solution.py:172
  40.6 20.1 %all-to-all-done.1 = bf16[64,8,1024]{2,1,0:T(8,128)(2,1)S(1)} async-done(((bf16[64,8,1024]{2,1,0:T(8,128)(2,1)}), bf16[64,8,1024]{2,1,0:T(8,128)(2,1)S(1)}, u32[]{:S(2)}, u32[]{:S(2)}) %all-to-all-start.1) | async-done | bytes 1048608 | tf_op jit(solution)/shard_map/all_to_all | solution.py:168
  60.7 9.3 %all-to-all-start.2 = ((bf16[64,8,1024]{2,1,0:T(8,128)(2,1)}), bf16[64,8,1024]{2,1,0:T(8,128)(2,1)S(1)}, u32[]{:S(2)}, u32[]{:S(2)}) async-start(bf16[64,8,1024]{2,1,0:T(8,128)(2,1)} %bitcast.19), calls=%async_computation.2 | async-start | bytes 2097152 | tf_op jit(solution)/shard_map/all_to_all | solution.py:168
  70.1 1.4 copy-done.2
  71.5 1.4 copy-done.4
  72.9 2.1 shard_map.100
  74.9 4.4 %collective-permute-start.2 = (bf16[128,1664]{1,0:T(8,128)(2,1)S(1)}, bf16[128,1664]{1,0:T(8,128)(2,1)S(1)}, u32[]{:S(2)}, u32[]{:S(2)}) collective-permute-start(bf16[128,1664]{1,0:T(8,128)(2,1)S(1)} %get-tuple-element.16), channel_id=1, source_target_pairs={{0,3},{1,0},{2,1},{3,2},{4,7},{5,4},{6,5},{7,6},{8,11},{9,8},{10,9... | collective-permute-start | bytes 1277960 | tf_op jit(solution)/shard_map/ppermute | solution.py:230
  79.3 2.4 %collective-permute-start.1 = (bf16[128,1664]{1,0:T(8,128)(2,1)S(1)}, bf16[128,1664]{1,0:T(8,128)(2,1)S(1)}, u32[]{:S(2)}, u32[]{:S(2)}) collective-permute-start(bf16[128,1664]{1,0:T(8,128)(2,1)S(1)} %get-tuple-element.15), channel_id=1, source_target_pairs={{0,2},{1,3},{2,0},{3,1},{4,6},{5,7},{6,4},{7,5},{8,10},{9,11},{10,... | collective-permute-start | bytes 1277960 | tf_op jit(solution)/shard_map/ppermute | solution.py:230
  81.8 2.5 %collective-permute-start = (bf16[128,1664]{1,0:T(8,128)(2,1)S(1)}, bf16[128,1664]{1,0:T(8,128)(2,1)S(1)}, u32[]{:S(2)}, u32[]{:S(2)}) collective-permute-start(bf16[128,1664]{1,0:T(8,128)(2,1)S(1)} %get-tuple-element.14), channel_id=1, source_target_pairs={{0,1},{1,2},{2,3},{3,0},{4,5},{5,6},{6,7},{7,4},{8,9},{9,10},{10,1... | collective-permute-start | bytes 1277960 | tf_op jit(solution)/shard_map/ppermute | solution.py:230
  84.3 3.6 %collective-permute-done.2 = bf16[128,1664]{1,0:T(8,128)(2,1)S(1)} collective-permute-done((bf16[128,1664]{1,0:T(8,128)(2,1)S(1)}, bf16[128,1664]{1,0:T(8,128)(2,1)S(1)}, u32[]{:S(2)}, u32[]{:S(2)}) %collective-permute-start.2) | collective-permute-done | bytes 426016 | tf_op jit(solution)/shard_map/ppermute | solution.py:230
  87.9 4.6 %collective-permute-done.1 = bf16[128,1664]{1,0:T(8,128)(2,1)S(1)} collective-permute-done((bf16[128,1664]{1,0:T(8,128)(2,1)S(1)}, bf16[128,1664]{1,0:T(8,128)(2,1)S(1)}, u32[]{:S(2)}, u32[]{:S(2)}) %collective-permute-start.1) | collective-permute-done | bytes 426016 | tf_op jit(solution)/shard_map/ppermute | solution.py:230
  92.6 11.0 %collective-permute-done = bf16[128,1664]{1,0:T(8,128)(2,1)S(1)} collective-permute-done((bf16[128,1664]{1,0:T(8,128)(2,1)S(1)}, bf16[128,1664]{1,0:T(8,128)(2,1)S(1)}, u32[]{:S(2)}, u32[]{:S(2)}) %collective-permute-start) | collective-permute-done | bytes 426016 | tf_op jit(solution)/shard_map/ppermute | solution.py:230
  103.6 0.2 convert_add_fusion.1
  103.8 0.2 fusion.47
  104.0 0.2 fusion.22.rest_0_.refs_0_
  104.2 1.9 collective-permute-start.3
  106.1 1.4 copy-done.3
  107.5 1.4 copy-done.5
  108.9 3.1 %shard_map.101 = (bf16[128,1664]{1,0:T(8,128)(2,1)S(1)}, bf16[128,1664]{1,0:T(8,128)(2,1)}, bf16[128,1664]{1,0:T(8,128)(2,1)}, bf16[128,1664]{1,0:T(8,128)(2,1)}) custom-call(s32[1]{0:T(128)} %bitcast.11.here, bf16[512,1024]{1,0:T(8,128)(2,1)S(1)} %bitcast.68, bf16[1,1024]{1,0:T(2,128)(2,1)S(1)} %broadcast_in_dim.115.gain, bf16[1024,768]{1,0:T(8,128)(2,1)S(1)} %bitcast.71, ...), custom_call_target="tpu_custom_call" | custom-call | flops 1610612736 | bytes 5898240 | tf_op jit(solution)/shard_map/pallas_call | solution.py:95
  112.1 4.6 %collective-permute-start.9 = (bf16[128,1664]{1,0:T(8,128)(2,1)}, bf16[128,1664]{1,0:T(8,128)(2,1)}, u32[]{:S(2)}, u32[]{:S(2)}) collective-permute-start(bf16[128,1664]{1,0:T(8,128)(2,1)} %get-tuple-element.20), channel_id=1, source_target_pairs={{0,3},{1,0},{2,1},{3,2},{4,7},{5,4},{6,5},{7,6},{8,11},{9,8},{10,9... | collective-permute-start | bytes 1277960 | tf_op jit(solution)/shard_map/ppermute | solution.py:230
  116.7 1.9 collective-permute-start.8
  118.6 2.5 %collective-permute-start.7 = (bf16[128,1664]{1,0:T(8,128)(2,1)}, bf16[128,1664]{1,0:T(8,128)(2,1)}, u32[]{:S(2)}, u32[]{:S(2)}) collective-permute-start(bf16[128,1664]{1,0:T(8,128)(2,1)} %get-tuple-element.18), channel_id=1, source_target_pairs={{0,1},{1,2},{2,3},{3,0},{4,5},{5,6},{6,7},{7,4},{8,9},{9,10},{10,1... | collective-permute-start | bytes 1277960 | tf_op jit(solution)/shard_map/ppermute | solution.py:230
  121.1 4.3 %collective-permute-start.4 = (bf16[128,768]{1,0:T(8,128)(2,1)S(1)}, bf16[128,768]{1,0:T(8,128)(2,1)S(1)}, u32[]{:S(2)}, u32[]{:S(2)}) collective-permute-start(bf16[128,768]{1,0:T(8,128)(2,1)S(1)} %fusion.22.rest_0_.refs_0_), channel_id=1, source_target_pairs={{0,2},{1,3},{2,0},{3,1},{4,6},{5,7},{6,4},{7,5},{8,10},{9,11},{10,... | collective-permute-start | bytes 589832 | tf_op jit(solution)/shard_map/ppermute | solution.py:234
  125.4 4.0 %collective-permute-start.5 = (bf16[128,768]{1,0:T(8,128)(2,1)S(1)}, bf16[128,768]{1,0:T(8,128)(2,1)S(1)}, u32[]{:S(2)}, u32[]{:S(2)}) collective-permute-start(bf16[128,768]{1,0:T(8,128)(2,1)S(1)} %fusion.22.rest_0_.refs_0_), channel_id=1, source_target_pairs={{0,3},{1,0},{2,1},{3,2},{4,7},{5,4},{6,5},{7,6},{8,11},{9,8},{10,9... | collective-permute-start | bytes 589832 | tf_op jit(solution)/shard_map/ppermute | solution.py:234
  129.4 14.5 %collective-permute-done.4.refs_2_ = bf16[128,768]{1,0:T(8,128)(2,1)S(1)} collective-permute-done((bf16[128,768]{1,0:T(8,128)(2,1)S(1)}, bf16[128,768]{1,0:T(8,128)(2,1)S(1)}, u32[]{:S(2)}, u32[]{:S(2)}) %collective-permute-start.4) | collective-permute-done | bytes 196640 | tf_op jit(solution)/shard_map/ppermute | solution.py:234
  143.9 3.1 %shard_map.102 = bf16[512,1024]{1,0:T(8,128)(2,1)} custom-call(s32[1]{0:T(128)} %bitcast.11.here, bf16[128,768]{1,0:T(8,128)(2,1)S(1)} %fusion.22.rest_0_.refs_0_, bf16[128,768]{1,0:T(8,128)(2,1)} %collective-permute-done.3.refs_1_, bf16[128,768]{1,0:T(8,128)(2,1)S(1)} %collective-permute-done.4.refs_2_, ...), custom_call_target="tpu_custom_call" | custom-call | flops 805306368 | bytes 3407872 | tf_op jit(solution)/shard_map/pallas_call | solution.py:135
  147.0 12.2 %all-to-all-start.3 = ((bf16[64,8,1024]{2,1,0:T(8,128)(2,1)}), bf16[64,8,1024]{2,1,0:T(8,128)(2,1)S(1)}, u32[]{:S(2)}, u32[]{:S(2)}) async-start(bf16[64,8,1024]{2,1,0:T(8,128)(2,1)} %bitcast.21), calls=%async_computation.3 | async-start | bytes 2097152 | tf_op jit(solution)/shard_map/all_to_all | solution.py:168
  159.2 1.5 convert_add_fusion
  160.7 0.2 fusion.43
  160.9 0.2 fusion.20.refs_0_
  161.1 3.2 %collective-permute-start.10 = (bf16[128,768]{1,0:T(8,128)(2,1)S(1)}, bf16[128,768]{1,0:T(8,128)(2,1)S(1)}, u32[]{:S(2)}, u32[]{:S(2)}) collective-permute-start(bf16[128,768]{1,0:T(8,128)(2,1)S(1)} %fusion.20.refs_0_), channel_id=1, source_target_pairs={{0,1},{1,2},{2,3},{3,0},{4,5},{5,6},{6,7},{7,4},{8,9},{9,10},{10,1... | collective-permute-start | bytes 589832 | tf_op jit(solution)/shard_map/ppermute | solution.py:234
  164.3 4.0 %collective-permute-start.11 = (bf16[128,768]{1,0:T(8,128)(2,1)S(1)}, bf16[128,768]{1,0:T(8,128)(2,1)S(1)}, u32[]{:S(2)}, u32[]{:S(2)}) collective-permute-start(bf16[128,768]{1,0:T(8,128)(2,1)S(1)} %fusion.20.refs_0_), channel_id=1, source_target_pairs={{0,2},{1,3},{2,0},{3,1},{4,6},{5,7},{6,4},{7,5},{8,10},{9,11},{10,... | collective-permute-start | bytes 589832 | tf_op jit(solution)/shard_map/ppermute | solution.py:234
  168.3 2.2 collective-permute-start.12
  170.6 4.0 %collective-permute-done.11.refs_2_ = bf16[128,768]{1,0:T(8,128)(2,1)S(1)} collective-permute-done((bf16[128,768]{1,0:T(8,128)(2,1)S(1)}, bf16[128,768]{1,0:T(8,128)(2,1)S(1)}, u32[]{:S(2)}, u32[]{:S(2)}) %collective-permute-start.11) | collective-permute-done | bytes 196640 | tf_op jit(solution)/shard_map/ppermute | solution.py:234
  174.6 2.5 %collective-permute-done.12.refs_3_ = bf16[128,768]{1,0:T(8,128)(2,1)S(1)} collective-permute-done((bf16[128,768]{1,0:T(8,128)(2,1)S(1)}, bf16[128,768]{1,0:T(8,128)(2,1)S(1)}, u32[]{:S(2)}, u32[]{:S(2)}) %collective-permute-start.12) | collective-permute-done | bytes 196640 | tf_op jit(solution)/shard_map/ppermute | solution.py:234
  177.1 1.4 shard_map.103
  178.6 4.0 %collective-permute-start.13 = (bf16[512,1024]{1,0:T(8,128)(2,1)S(1)}, bf16[512,1024]{1,0:T(8,128)(2,1)}, u32[]{:S(2)}, u32[]{:S(2)}) collective-permute-start(bf16[512,1024]{1,0:T(8,128)(2,1)S(1)} %shard_map.103), channel_id=1, source_target_pairs={{0,32},{32,0},{1,33},{33,1},{2,34},{34,2},{3,35},{35,3},{4,36},{36... | collective-permute-start | bytes 3145736 | tf_op jit(solution)/shard_map/ppermute | solution.py:172
  182.6 2.4 %collective-permute-done.13 = bf16[512,1024]{1,0:T(8,128)(2,1)} collective-permute-done((bf16[512,1024]{1,0:T(8,128)(2,1)S(1)}, bf16[512,1024]{1,0:T(8,128)(2,1)}, u32[]{:S(2)}, u32[]{:S(2)}) %collective-permute-start.13) | collective-permute-done | bytes 1048608 | tf_op jit(solution)/shard_map/ppermute | solution.py:172
  185.0 0.3 all-to-all-done.3
  185.3 12.1 %all-to-all-start.4 = ((bf16[64,8,1024]{2,1,0:T(8,128)(2,1)}), bf16[64,8,1024]{2,1,0:T(8,128)(2,1)S(1)}, u32[]{:S(2)}, u32[]{:S(2)}) async-start(bf16[64,8,1024]{2,1,0:T(8,128)(2,1)} %bitcast.23), calls=%async_computation.4 | async-start | bytes 2097152 | tf_op jit(solution)/shard_map/all_to_all | solution.py:168
  197.4 0.1 fusion.23
  197.6 0.1 pad_maximum_fusion.2
  197.7 0.1 pad_maximum_fusion.1
  197.9 0.5 convolution_bitcast_fusion.1
  198.4 26.0 %all-to-all-done.4 = bf16[64,8,1024]{2,1,0:T(8,128)(2,1)S(1)} async-done(((bf16[64,8,1024]{2,1,0:T(8,128)(2,1)}), bf16[64,8,1024]{2,1,0:T(8,128)(2,1)S(1)}, u32[]{:S(2)}, u32[]{:S(2)}) %all-to-all-start.4) | async-done | bytes 1048608 | tf_op jit(solution)/shard_map/all_to_all | solution.py:168
  224.4 0.5 convolution_bitcast_fusion
  224.9 0.7 fusion.26
  (32 shorter events, 0.2 us)
Async XLA Ops:
  0.0 22.7 %copy-start = (bf16[64,1024]{1,0:T(8,128)(2,1)S(1)}, bf16[64,1024]{1,0:T(8,128)(2,1)}, u32[]{:S(2)}) copy-start(bf16[64,1024]{1,0:T(8,128)(2,1)} %param.10) | copy-start | bytes 393220
  1.5 21.2 %all-to-all-start = ((bf16[8,64,256]{2,1,0:T(8,128)(2,1)}), bf16[8,64,256]{2,1,0:T(8,128)(2,1)S(1)}, u32[]{:S(2)}, u32[]{:S(2)}) async-start(bf16[8,64,256]{2,1,0:T(8,128)(2,1)} %broadcast_in_dim.106), calls=%async_computation | async-start | bytes 524288 | tf_op jit(solution)/shard_map/all_to_all | solution.py:42
  25.1 35.6 %all-to-all-start.1 = ((bf16[64,8,1024]{2,1,0:T(8,128)(2,1)}), bf16[64,8,1024]{2,1,0:T(8,128)(2,1)S(1)}, u32[]{:S(2)}, u32[]{:S(2)}) async-start(bf16[64,8,1024]{2,1,0:T(8,128)(2,1)} %fusion.1), calls=%async_computation.1 | async-start | bytes 2097152 | tf_op jit(solution)/shard_map/all_to_all | solution.py:168
  34.3 26.4 %copy-start.6 = (s32[64,64]{1,0:T(8,128)}, s32[64,64]{1,0:T(8,128)S(1)}, u32[]{:S(2)}) copy-start(s32[64,64]{1,0:T(8,128)S(1)} %fusion.14) | copy-start | bytes 49156
  34.3 35.7 %copy-start.10 = (bf16[1024]{0:T(1024)(128)(2,1)S(1)}, bf16[1024]{0:T(1024)(128)(2,1)}, u32[]{:S(2)}) copy-start(bf16[1024]{0:T(1024)(128)(2,1)} %param.14) | copy-start | bytes 6148
  34.7 5.9 %collective-permute-start.6 = (bf16[512,1024]{1,0:T(8,128)(2,1)S(1)}, bf16[512,1024]{1,0:T(8,128)(2,1)}, u32[]{:S(2)}, u32[]{:S(2)}) collective-permute-start(bf16[512,1024]{1,0:T(8,128)(2,1)S(1)} %convolution_convert_fusion), channel_id=1, source_target_pairs={{0,32},{32,0},{1,33},{33,1},{2,34},{34,2},{3,35},{35,3},{4,36},{36... | collective-permute-start | bytes 3145736 | tf_op jit(solution)/shard_map/ppermute | solution.py:172
  60.7 45.4 %all-to-all-start.2 = ((bf16[64,8,1024]{2,1,0:T(8,128)(2,1)}), bf16[64,8,1024]{2,1,0:T(8,128)(2,1)S(1)}, u32[]{:S(2)}, u32[]{:S(2)}) async-start(bf16[64,8,1024]{2,1,0:T(8,128)(2,1)} %bitcast.19), calls=%async_computation.2 | async-start | bytes 2097152 | tf_op jit(solution)/shard_map/all_to_all | solution.py:168
  70.0 1.4 copy-start.2
  71.5 1.4 copy-start.4
  74.9 13.0 %collective-permute-start.2 = (bf16[128,1664]{1,0:T(8,128)(2,1)S(1)}, bf16[128,1664]{1,0:T(8,128)(2,1)S(1)}, u32[]{:S(2)}, u32[]{:S(2)}) collective-permute-start(bf16[128,1664]{1,0:T(8,128)(2,1)S(1)} %get-tuple-element.16), channel_id=1, source_target_pairs={{0,3},{1,0},{2,1},{3,2},{4,7},{5,4},{6,5},{7,6},{8,11},{9,8},{10,9... | collective-permute-start | bytes 1277960 | tf_op jit(solution)/shard_map/ppermute | solution.py:230
  79.3 13.2 %collective-permute-start.1 = (bf16[128,1664]{1,0:T(8,128)(2,1)S(1)}, bf16[128,1664]{1,0:T(8,128)(2,1)S(1)}, u32[]{:S(2)}, u32[]{:S(2)}) collective-permute-start(bf16[128,1664]{1,0:T(8,128)(2,1)S(1)} %get-tuple-element.15), channel_id=1, source_target_pairs={{0,2},{1,3},{2,0},{3,1},{4,6},{5,7},{6,4},{7,5},{8,10},{9,11},{10,... | collective-permute-start | bytes 1277960 | tf_op jit(solution)/shard_map/ppermute | solution.py:230
  81.8 21.8 %collective-permute-start = (bf16[128,1664]{1,0:T(8,128)(2,1)S(1)}, bf16[128,1664]{1,0:T(8,128)(2,1)S(1)}, u32[]{:S(2)}, u32[]{:S(2)}) collective-permute-start(bf16[128,1664]{1,0:T(8,128)(2,1)S(1)} %get-tuple-element.14), channel_id=1, source_target_pairs={{0,1},{1,2},{2,3},{3,0},{4,5},{5,6},{6,7},{7,4},{8,9},{9,10},{10,1... | collective-permute-start | bytes 1277960 | tf_op jit(solution)/shard_map/ppermute | solution.py:230
  104.2 21.2 %collective-permute-start.3 = (bf16[128,768]{1,0:T(8,128)(2,1)S(1)}, bf16[128,768]{1,0:T(8,128)(2,1)}, u32[]{:S(2)}, u32[]{:S(2)}) collective-permute-start(bf16[128,768]{1,0:T(8,128)(2,1)S(1)} %fusion.22.rest_0_.refs_0_), channel_id=1, source_target_pairs={{0,1},{1,2},{2,3},{3,0},{4,5},{5,6},{6,7},{7,4},{8,9},{9,10},{10,1... | collective-permute-start | bytes 589832 | tf_op jit(solution)/shard_map/ppermute | solution.py:234
  106.1 1.4 copy-start.3
  107.5 1.4 copy-start.5
  108.9 35.0 %copy-start.1 = (bf16[1,768,1024]{2,1,0:T(8,128)(2,1)S(1)}, bf16[1,768,1024]{2,1,0:T(8,128)(2,1)}, u32[]{:S(2)}) copy-start(bf16[1,768,1024]{2,1,0:T(8,128)(2,1)} %param.19) | copy-start | bytes 4718596
  112.1 47.1 %collective-permute-start.9 = (bf16[128,1664]{1,0:T(8,128)(2,1)}, bf16[128,1664]{1,0:T(8,128)(2,1)}, u32[]{:S(2)}, u32[]{:S(2)}) collective-permute-start(bf16[128,1664]{1,0:T(8,128)(2,1)} %get-tuple-element.20), channel_id=1, source_target_pairs={{0,3},{1,0},{2,1},{3,2},{4,7},{5,4},{6,5},{7,6},{8,11},{9,8},{10,9... | collective-permute-start | bytes 1277960 | tf_op jit(solution)/shard_map/ppermute | solution.py:230
  116.7 42.5 %collective-permute-start.8 = (bf16[128,1664]{1,0:T(8,128)(2,1)}, bf16[128,1664]{1,0:T(8,128)(2,1)}, u32[]{:S(2)}, u32[]{:S(2)}) collective-permute-start(bf16[128,1664]{1,0:T(8,128)(2,1)} %get-tuple-element.19), channel_id=1, source_target_pairs={{0,2},{1,3},{2,0},{3,1},{4,6},{5,7},{6,4},{7,5},{8,10},{9,11},{10,... | collective-permute-start | bytes 1277960 | tf_op jit(solution)/shard_map/ppermute | solution.py:230
  118.6 40.6 %collective-permute-start.7 = (bf16[128,1664]{1,0:T(8,128)(2,1)}, bf16[128,1664]{1,0:T(8,128)(2,1)}, u32[]{:S(2)}, u32[]{:S(2)}) collective-permute-start(bf16[128,1664]{1,0:T(8,128)(2,1)} %get-tuple-element.18), channel_id=1, source_target_pairs={{0,1},{1,2},{2,3},{3,0},{4,5},{5,6},{6,7},{7,4},{8,9},{9,10},{10,1... | collective-permute-start | bytes 1277960 | tf_op jit(solution)/shard_map/ppermute | solution.py:230
  121.1 22.8 %collective-permute-start.4 = (bf16[128,768]{1,0:T(8,128)(2,1)S(1)}, bf16[128,768]{1,0:T(8,128)(2,1)S(1)}, u32[]{:S(2)}, u32[]{:S(2)}) collective-permute-start(bf16[128,768]{1,0:T(8,128)(2,1)S(1)} %fusion.22.rest_0_.refs_0_), channel_id=1, source_target_pairs={{0,2},{1,3},{2,0},{3,1},{4,6},{5,7},{6,4},{7,5},{8,10},{9,11},{10,... | collective-permute-start | bytes 589832 | tf_op jit(solution)/shard_map/ppermute | solution.py:234
  125.4 18.5 %collective-permute-start.5 = (bf16[128,768]{1,0:T(8,128)(2,1)S(1)}, bf16[128,768]{1,0:T(8,128)(2,1)S(1)}, u32[]{:S(2)}, u32[]{:S(2)}) collective-permute-start(bf16[128,768]{1,0:T(8,128)(2,1)S(1)} %fusion.22.rest_0_.refs_0_), channel_id=1, source_target_pairs={{0,3},{1,0},{2,1},{3,2},{4,7},{5,4},{6,5},{7,6},{8,11},{9,8},{10,9... | collective-permute-start | bytes 589832 | tf_op jit(solution)/shard_map/ppermute | solution.py:234
  147.0 38.3 %all-to-all-start.3 = ((bf16[64,8,1024]{2,1,0:T(8,128)(2,1)}), bf16[64,8,1024]{2,1,0:T(8,128)(2,1)S(1)}, u32[]{:S(2)}, u32[]{:S(2)}) async-start(bf16[64,8,1024]{2,1,0:T(8,128)(2,1)} %bitcast.21), calls=%async_computation.3 | async-start | bytes 2097152 | tf_op jit(solution)/shard_map/all_to_all | solution.py:168
  161.1 9.5 %collective-permute-start.10 = (bf16[128,768]{1,0:T(8,128)(2,1)S(1)}, bf16[128,768]{1,0:T(8,128)(2,1)S(1)}, u32[]{:S(2)}, u32[]{:S(2)}) collective-permute-start(bf16[128,768]{1,0:T(8,128)(2,1)S(1)} %fusion.20.refs_0_), channel_id=1, source_target_pairs={{0,1},{1,2},{2,3},{3,0},{4,5},{5,6},{6,7},{7,4},{8,9},{9,10},{10,1... | collective-permute-start | bytes 589832 | tf_op jit(solution)/shard_map/ppermute | solution.py:234
  164.3 10.2 %collective-permute-start.11 = (bf16[128,768]{1,0:T(8,128)(2,1)S(1)}, bf16[128,768]{1,0:T(8,128)(2,1)S(1)}, u32[]{:S(2)}, u32[]{:S(2)}) collective-permute-start(bf16[128,768]{1,0:T(8,128)(2,1)S(1)} %fusion.20.refs_0_), channel_id=1, source_target_pairs={{0,2},{1,3},{2,0},{3,1},{4,6},{5,7},{6,4},{7,5},{8,10},{9,11},{10,... | collective-permute-start | bytes 589832 | tf_op jit(solution)/shard_map/ppermute | solution.py:234
  168.3 8.8 %collective-permute-start.12 = (bf16[128,768]{1,0:T(8,128)(2,1)S(1)}, bf16[128,768]{1,0:T(8,128)(2,1)S(1)}, u32[]{:S(2)}, u32[]{:S(2)}) collective-permute-start(bf16[128,768]{1,0:T(8,128)(2,1)S(1)} %fusion.20.refs_0_), channel_id=1, source_target_pairs={{0,3},{1,0},{2,1},{3,2},{4,7},{5,4},{6,5},{7,6},{8,11},{9,8},{10,9... | collective-permute-start | bytes 589832 | tf_op jit(solution)/shard_map/ppermute | solution.py:234
  178.5 18.9 %copy-start.8 = (s32[64,8]{0,1:T(8,128)S(1)}, s32[64,8]{0,1:T(8,128)}, u32[]{:S(2)}) copy-start(s32[64,8]{0,1:T(8,128)} %param.15) | copy-start | bytes 6148
  178.5 18.9 %copy-start.9 = (f32[64,8]{0,1:T(8,128)S(1)}, f32[64,8]{0,1:T(8,128)}, u32[]{:S(2)}) copy-start(f32[64,8]{0,1:T(8,128)} %param.16) | copy-start | bytes 6148
  178.5 19.2 %copy-start.7 = (s32[64,64]{1,0:T(8,128)S(1)}, s32[64,64]{1,0:T(8,128)}, u32[]{:S(2)}) copy-start(s32[64,64]{1,0:T(8,128)} %copy-done.6) | copy-start | bytes 49156
  178.6 6.4 %collective-permute-start.13 = (bf16[512,1024]{1,0:T(8,128)(2,1)S(1)}, bf16[512,1024]{1,0:T(8,128)(2,1)}, u32[]{:S(2)}, u32[]{:S(2)}) collective-permute-start(bf16[512,1024]{1,0:T(8,128)(2,1)S(1)} %shard_map.103), channel_id=1, source_target_pairs={{0,32},{32,0},{1,33},{33,1},{2,34},{34,2},{3,35},{35,3},{4,36},{36... | collective-permute-start | bytes 3145736 | tf_op jit(solution)/shard_map/ppermute | solution.py:172
  185.3 39.1 %all-to-all-start.4 = ((bf16[64,8,1024]{2,1,0:T(8,128)(2,1)}), bf16[64,8,1024]{2,1,0:T(8,128)(2,1)S(1)}, u32[]{:S(2)}, u32[]{:S(2)}) async-start(bf16[64,8,1024]{2,1,0:T(8,128)(2,1)} %bitcast.23), calls=%async_computation.4 | async-start | bytes 2097152 | tf_op jit(solution)/shard_map/all_to_all | solution.py:168

commit v2 on v1

--- a/solution.py
+++ b/solution.py
@@ -12,6 +12,7 @@
 D = 4096
 CAP = 8
 LANES = 128
+VMEM_LIMIT = 32 * 1024 * 1024
 BF = jnp.bfloat16
 F32 = jnp.float32
 GROUP = ("y", "expert")
@@ -103,7 +104,7 @@
             scratch_shapes=[pltpu.VMEM(rows.shape, BF)],
         ),
         out_shape=[jax.ShapeDtypeStruct((block, width), BF)] * size,
-        compiler_params=pltpu.CompilerParams(vmem_limit_bytes=32 * 1024 * 1024),
+        compiler_params=pltpu.CompilerParams(vmem_limit_bytes=VMEM_LIMIT),
         cost_estimate=pl.CostEstimate(
             flops=4 * rows.shape[0] * feat * hidden,
             bytes_accessed=2 * (rows.size + 2 * gate.size + rows.shape[0] * width),
@@ -144,7 +145,7 @@
             scratch_shapes=[pltpu.VMEM((rows, hidden), BF)],
         ),
         out_shape=jax.ShapeDtypeStruct((rows, feat), BF),
-        compiler_params=pltpu.CompilerParams(vmem_limit_bytes=32 * 1024 * 1024),
+        compiler_params=pltpu.CompilerParams(vmem_limit_bytes=VMEM_LIMIT),
         cost_estimate=pl.CostEstimate(
             flops=2 * rows * hidden * feat,
             bytes_accessed=2 * (rows * hidden + hidden * feat + rows * feat),
@@ -162,6 +163,40 @@
     gate_sum = total[:, :hidden] * scale
     up_sum = total[:, hidden : 2 * hidden] * scale
     return (jax.nn.silu(gate_sum) * up_sum).astype(BF)
+
+
+def silu_kernel(*refs):
+    parts, out = refs[:-1], refs[-1]
+    hidden = out.shape[1]
+
+    def total(low, width):
+        result = parts[0][:, low : low + width].astype(F32)
+        for part in parts[1:]:
+            result = result + part[:, low : low + width].astype(F32)
+        return result
+
+    extra = total(2 * hidden, LANES)
+    scale = lax.rsqrt((extra[:, :1] + extra[:, 1:2]) / D + 1e-06)
+    gate_sum = total(0, hidden) * scale
+    up_sum = total(hidden, hidden) * scale
+    out[...] = (gate_sum / (1.0 + jnp.exp(-gate_sum)) * up_sum).astype(BF)
+
+
+def silu_call(parts, hidden):
+    rows = parts[0].shape[0]
+    near = pl.BlockSpec(memory_space=pltpu.VMEM)
+    return pl.pallas_call(
+        silu_kernel,
+        in_specs=[near] * len(parts),
+        out_specs=near,
+        out_shape=jax.ShapeDtypeStruct((rows, hidden), BF),
+        compiler_params=pltpu.CompilerParams(vmem_limit_bytes=VMEM_LIMIT),
+        cost_estimate=pl.CostEstimate(
+            flops=16 * rows * hidden,
+            bytes_accessed=2 * rows * hidden * (2 * len(parts) + 1),
+            transcendentals=rows * hidden,
+        ),
+    )(*parts)
 
 
 def exchange(block):
@@ -224,11 +259,10 @@
     def blocks(flat):
         return flat.reshape(peers, CAP, feat)
 
-    def reduce_parts(parts):
-        got = [parts[0]]
-        for step in range(1, size):
-            got.append(lax.ppermute(parts[step], "tensor", ring(size, step)))
-        return silu_product(got, hidden_size)
+    def fetch_parts(parts):
+        return [parts[0]] + [
+            lax.ppermute(parts[step], "tensor", ring(size, step)) for step in range(1, size)
+        ]
 
     def spread(piece):
         return [piece] + [lax.ppermute(piece, "tensor", ring(size, k)) for k in range(1, size)]
@@ -246,12 +280,20 @@
     far = exchange(blocks(swap(outgoing(pick_far)))).reshape(rows, feat)
 
     near_parts = gate_up(here, near, gain, gate_rows, up_rows, [])
-    near_hidden = reduce_parts(near_parts)
-    far_parts = gate_up(here, far, gain, gate_rows, up_rows, [near_hidden])
-    near_made = down_product(here, spread(near_hidden), down_rows, [far_parts[0]])
+    near_got = fetch_parts(near_parts)
+    far_parts = gate_up(here, far, gain, gate_rows, up_rows, [near_got[size // 2]])
+    near_got, far_parts = lax.optimization_barrier((near_got, far_parts))
+    far_parts = list(far_parts)
+    near_pieces = spread(silu_call(near_got, hidden_size))
+    for step in range(1, size):
+        near_pieces[step], far_parts[step] = lax.optimization_barrier(
+            (near_pieces[step], far_parts[step])
+        )
+    near_made = down_product(here, near_pieces, down_rows, [far_parts[0]])
+    far_got = fetch_parts(far_parts)
     near_back = exchange(blocks(near_made))
-    far_hidden = reduce_parts(far_parts)
-    far_made = down_product(here, spread(far_hidden), down_rows, [])
+    far_pieces = spread(silu_product(far_got, hidden_size))
+    far_made = down_product(here, far_pieces, down_rows, [])
     far_back = exchange(blocks(swap(far_made)))
 
     mixed = attended.astype(F32) + combine(mix_near, near_back) + combine(mix_far, far_back)

time: 230 us -> 213 us (0.926)
  waiting for transfers between devices: 99.5 us -> 72.6 us
  starting transfers between devices: 98.9 us -> 108 us
    ppermute x6, waiting for transfers between devices: 21.1 us -> 4 us  [spread(): lax.ppermute(piece, 'tensor', ring(size, k))]
    ppermute x6, waiting for transfers between devices: 19.3 us -> 2.72 us  [fetch_parts(): lax.ppermute(parts[step], 'tensor', ring(size, step))]
    all_to_all x4, waiting for transfers between devices: 46.5 us -> 53.2 us  [exchange(): return lax.all_to_all(block, GROUP, split_axis=0, concat_axis=0, tiled=True)]
    all_to_all x4, starting transfers between devices: 42.6 us -> 47.7 us  [exchange(): return lax.all_to_all(block, GROUP, split_axis=0, concat_axis=0, tiled=True)]
    unnamed x22 -> x26, local copies, waits for them, and re-layouts: 5.66 us -> 5.67 us
  transfers between devices with their start and end apart: 19 -> 19, of which waited for: 12 -> 9; matrix products, arithmetic and copies ran while one was open for 3% -> 3% of each run, Pallas kernels for 4% -> 5%
where the time goes in v2:
time: 213 us; the launch traced here: 209 us
  starting transfers between devices  108 us (51%)
  waiting for transfers between devices  72.6 us (34%)
  Pallas kernels  11.3 us (5%)
  other arithmetic  6.45 us (3%)
  local copies, waits for them, and re-layouts  6.39 us (3%)
  matrix products  3.59 us (2%)
    all_to_all x4, waiting for transfers between devices, exchange(): return lax.all_to_all(block, GROUP, split_axis=0, concat_axis=0, tiled=True)  53.2 us
    all_to_all x4, starting transfers between devices, exchange(): return lax.all_to_all(block, GROUP, split_axis=0, concat_axis=0, tiled=True)  47.7 us
    ppermute x6, starting transfers between devices, fetch_parts(): lax.ppermute(parts[step], 'tensor', ring(size, step))  20.5 us
    ppermute x6, starting transfers between devices, spread(): lax.ppermute(piece, 'tensor', ring(size, k))  19.2 us
    all_to_all x1, starting transfers between devices, attention(): lax.all_to_all(copies, 'expert', split_axis=0, concat_axis=0, tiled=True)  10.9 us
    ppermute x2, starting transfers between devices, swap(): return lax.ppermute(block, 'core', [(0, 1), (1, 0)])  9.75 us
    all_to_all x1, waiting for transfers between devices, attention(): lax.all_to_all(copies, 'expert', split_axis=0, concat_axis=0, tiled=True)  7.9 us
    pallas_call x2, Pallas kernels, gate_up(): pl.pallas_call(kernel, grid_spec=pltpu.PrefetchScalarGridSpec(num_scalar_...  6.14 us
  transfers between devices with their start and end apart: 19, of which 9 were waited for; matrix products, arithmetic and copies ran while one was open for 3% of the time, Pallas kernels for 5%

profile of v2, /device:TPU:1, one launch (start us, length us, event | category | flops | bytes accessed | tf_op | source)
XLA Modules:
  0.0 208.8 jit_solution(2521290465736939719)
XLA Ops:
  0.0 0.8 pad_maximum_fusion
  0.8 0.7 broadcast_in_dim.106
  1.5 10.9 %all-to-all-start = ((bf16[8,64,256]{2,1,0:T(8,128)(2,1)}), bf16[8,64,256]{2,1,0:T(8,128)(2,1)S(1)}, u32[]{:S(2)}, u32[]{:S(2)}) async-start(bf16[8,64,256]{2,1,0:T(8,128)(2,1)} %broadcast_in_dim.106), calls=%async_computation | async-start | bytes 524288 | tf_op jit(solution)/shard_map/all_to_all | solution.py:43
  12.4 0.7 add_bitcast_fusion.1
  13.0 0.8 compare_reduce_fusion
  13.9 0.7 select_reduce_fusion.1
  14.6 0.1 iota_compare_fusion.2
  14.7 0.1 fusion.15
  14.8 7.9 %all-to-all-done = bf16[8,64,256]{2,1,0:T(8,128)(2,1)S(1)} async-done(((bf16[8,64,256]{2,1,0:T(8,128)(2,1)}), bf16[8,64,256]{2,1,0:T(8,128)(2,1)S(1)}, u32[]{:S(2)}, u32[]{:S(2)}) %all-to-all-start) | async-done | bytes 262176 | tf_op jit(solution)/shard_map/all_to_all | solution.py:43
  22.7 0.3 fusion.10
  23.0 0.4 fusion.50
  23.4 0.3 fusion.13
  23.7 0.0 copy-start.6
  23.7 1.4 fusion.1
  25.1 9.0 %all-to-all-start.1 = ((bf16[64,8,1024]{2,1,0:T(8,128)(2,1)}), bf16[64,8,1024]{2,1,0:T(8,128)(2,1)S(1)}, u32[]{:S(2)}, u32[]{:S(2)}) async-start(bf16[64,8,1024]{2,1,0:T(8,128)(2,1)} %fusion.1), calls=%async_computation.1 | async-start | bytes 2097152 | tf_op jit(solution)/shard_map/all_to_all | solution.py:203
  34.2 0.1 fusion.14
  34.3 0.0 copy-start.12
  34.3 0.4 convolution_convert_fusion
  34.7 3.5 %collective-permute-start.3 = (bf16[512,1024]{1,0:T(8,128)(2,1)S(1)}, bf16[512,1024]{1,0:T(8,128)(2,1)}, u32[]{:S(2)}, u32[]{:S(2)}) collective-permute-start(bf16[512,1024]{1,0:T(8,128)(2,1)S(1)} %convolution_convert_fusion), channel_id=1, source_target_pairs={{0,32},{32,0},{1,33},{33,1},{2,34},{34,2},{3,35},{35,3},{4,36},{36... | collective-permute-start | bytes 3145736 | tf_op jit(solution)/shard_map/ppermute | solution.py:207
  38.2 2.4 %collective-permute-done.3 = bf16[512,1024]{1,0:T(8,128)(2,1)} collective-permute-done((bf16[512,1024]{1,0:T(8,128)(2,1)S(1)}, bf16[512,1024]{1,0:T(8,128)(2,1)}, u32[]{:S(2)}, u32[]{:S(2)}) %collective-permute-start.3) | collective-permute-done | bytes 1048608 | tf_op jit(solution)/shard_map/ppermute | solution.py:207
  40.6 20.1 %all-to-all-done.1 = bf16[64,8,1024]{2,1,0:T(8,128)(2,1)S(1)} async-done(((bf16[64,8,1024]{2,1,0:T(8,128)(2,1)}), bf16[64,8,1024]{2,1,0:T(8,128)(2,1)S(1)}, u32[]{:S(2)}, u32[]{:S(2)}) %all-to-all-start.1) | async-done | bytes 1048608 | tf_op jit(solution)/shard_map/all_to_all | solution.py:203
  60.7 9.3 %all-to-all-start.2 = ((bf16[64,8,1024]{2,1,0:T(8,128)(2,1)}), bf16[64,8,1024]{2,1,0:T(8,128)(2,1)S(1)}, u32[]{:S(2)}, u32[]{:S(2)}) async-start(bf16[64,8,1024]{2,1,0:T(8,128)(2,1)} %bitcast.18), calls=%async_computation.2 | async-start | bytes 2097152 | tf_op jit(solution)/shard_map/all_to_all | solution.py:203
  70.0 0.0 copy-start.2
  70.0 1.4 copy-done.2
  71.4 1.4 copy-done.4
  72.9 3.0 %shard_map.100 = (bf16[128,1664]{1,0:T(8,128)(2,1)S(1)}, bf16[128,1664]{1,0:T(8,128)(2,1)}, bf16[128,1664]{1,0:T(8,128)(2,1)S(1)}, bf16[128,1664]{1,0:T(8,128)(2,1)}) custom-call(s32[1]{0:T(128)} %bitcast.11.here, bf16[512,1024]{1,0:T(8,128)(2,1)S(1)} %bitcast.69, bf16[1,1024]{1,0:T(2,128)(2,1)S(1)} %broadcast_in_dim.115.gain, ...), custom_call_target="tpu_custom_call" | custom-call | flops 1610612736 | bytes 5898240 | tf_op jit(solution)/shard_map/pallas_call | solution.py:96
  75.9 4.6 %collective-permute-start.1 = (bf16[128,1664]{1,0:T(8,128)(2,1)S(1)}, bf16[128,1664]{1,0:T(8,128)(2,1)S(1)}, u32[]{:S(2)}, u32[]{:S(2)}) collective-permute-start(bf16[128,1664]{1,0:T(8,128)(2,1)S(1)} %get-tuple-element.29), channel_id=1, source_target_pairs={{0,2},{1,3},{2,0},{3,1},{4,6},{5,7},{6,4},{7,5},{8,10},{9,11},{10,... | collective-permute-start | bytes 1277960 | tf_op jit(solution)/shard_map/ppermute | solution.py:264
  80.5 2.2 %collective-permute-start = (bf16[128,1664]{1,0:T(8,128)(2,1)}, bf16[128,1664]{1,0:T(8,128)(2,1)S(1)}, u32[]{:S(2)}, u32[]{:S(2)}) collective-permute-start(bf16[128,1664]{1,0:T(8,128)(2,1)} %get-tuple-element.28), channel_id=1, source_target_pairs={{0,1},{1,2},{2,3},{3,0},{4,5},{5,6},{6,7},{7,4},{8,9},{9,10},{10,1... | collective-permute-start | bytes 1277960 | tf_op jit(solution)/shard_map/ppermute | solution.py:264
  82.7 4.3 %collective-permute-start.2 = (bf16[128,1664]{1,0:T(8,128)(2,1)}, bf16[128,1664]{1,0:T(8,128)(2,1)}, u32[]{:S(2)}, u32[]{:S(2)}) collective-permute-start(bf16[128,1664]{1,0:T(8,128)(2,1)} %get-tuple-element.30), channel_id=1, source_target_pairs={{0,3},{1,0},{2,1},{3,2},{4,7},{5,4},{6,5},{7,6},{8,11},{9,8},{10,9... | collective-permute-start | bytes 1277960 | tf_op jit(solution)/shard_map/ppermute | solution.py:264
  87.0 2.3 %collective-permute-done.1.rest_0_.refs_2_ = bf16[128,1664]{1,0:T(8,128)(2,1)S(1)} collective-permute-done((bf16[128,1664]{1,0:T(8,128)(2,1)S(1)}, bf16[128,1664]{1,0:T(8,128)(2,1)S(1)}, u32[]{:S(2)}, u32[]{:S(2)}) %collective-permute-start.1) | collective-permute-done | bytes 426016 | tf_op jit(solution)/shard_map/ppermute | solution.py:264
  89.4 7.1 %all-to-all-done.2 = bf16[64,8,1024]{2,1,0:T(8,128)(2,1)S(1)} async-done(((bf16[64,8,1024]{2,1,0:T(8,128)(2,1)}), bf16[64,8,1024]{2,1,0:T(8,128)(2,1)S(1)}, u32[]{:S(2)}, u32[]{:S(2)}) %all-to-all-start.2) | async-done | bytes 1048608 | tf_op jit(solution)/shard_map/all_to_all | solution.py:203
  96.4 1.4 copy-done.3
  97.8 1.4 copy-done.5
  99.2 3.1 %shard_map.101 = (bf16[128,1664]{1,0:T(8,128)(2,1)S(1)}, bf16[128,1664]{1,0:T(8,128)(2,1)}, bf16[128,1664]{1,0:T(8,128)(2,1)}, bf16[128,1664]{1,0:T(8,128)(2,1)}) custom-call(s32[1]{0:T(128)} %bitcast.11.here, bf16[512,1024]{1,0:T(8,128)(2,1)S(1)} %bitcast.68, bf16[1,1024]{1,0:T(2,128)(2,1)S(1)} %broadcast_in_dim.115.gain, bf16[1024,768]{1,0:T(8,128)(2,1)S(1)} %bitcast.71, ...), custom_call_target="tpu_custom_call" | custom-call | flops 1610612736 | bytes 5898240 | tf_op jit(solution)/shard_map/pallas_call | solution.py:96
  102.4 1.5 shard_map.102.refs_0_
  103.9 4.4 %collective-permute-start.6 = (bf16[128,768]{1,0:T(8,128)(2,1)S(1)}, bf16[128,768]{1,0:T(8,128)(2,1)S(1)}, u32[]{:S(2)}, u32[]{:S(2)}) collective-permute-start(bf16[128,768]{1,0:T(8,128)(2,1)S(1)} %shard_map.102.refs_0_), channel_id=1, source_target_pairs={{0,3},{1,0},{2,1},{3,2},{4,7},{5,4},{6,5},{7,6},{8,11},{9,8},{10,9... | collective-permute-start | bytes 589832 | tf_op jit(solution)/shard_map/ppermute | solution.py:268
  108.3 2.5 %collective-permute-start.5 = (bf16[128,768]{1,0:T(8,128)(2,1)S(1)}, bf16[128,768]{1,0:T(8,128)(2,1)S(1)}, u32[]{:S(2)}, u32[]{:S(2)}) collective-permute-start(bf16[128,768]{1,0:T(8,128)(2,1)S(1)} %shard_map.102.refs_0_), channel_id=1, source_target_pairs={{0,2},{1,3},{2,0},{3,1},{4,6},{5,7},{6,4},{7,5},{8,10},{9,11},{10,... | collective-permute-start | bytes 589832 | tf_op jit(solution)/shard_map/ppermute | solution.py:268
  110.7 2.5 %collective-permute-start.4 = (bf16[128,768]{1,0:T(8,128)(2,1)S(1)}, bf16[128,768]{1,0:T(8,128)(2,1)S(1)}, u32[]{:S(2)}, u32[]{:S(2)}) collective-permute-start(bf16[128,768]{1,0:T(8,128)(2,1)S(1)} %shard_map.102.refs_0_), channel_id=1, source_target_pairs={{0,1},{1,2},{2,3},{3,0},{4,5},{5,6},{6,7},{7,4},{8,9},{9,10},{10,1... | collective-permute-start | bytes 589832 | tf_op jit(solution)/shard_map/ppermute | solution.py:268
  113.3 4.0 %collective-permute-start.9 = (bf16[128,1664]{1,0:T(8,128)(2,1)}, bf16[128,1664]{1,0:T(8,128)(2,1)}, u32[]{:S(2)}, u32[]{:S(2)}) collective-permute-start(bf16[128,1664]{1,0:T(8,128)(2,1)} %get-tuple-element.48), channel_id=1, source_target_pairs={{0,3},{1,0},{2,1},{3,2},{4,7},{5,4},{6,5},{7,6},{8,11},{9,8},{10,9... | collective-permute-start | bytes 1277960 | tf_op jit(solution)/shard_map/ppermute | solution.py:264
  117.3 3.1 %collective-permute-start.8 = (bf16[128,1664]{1,0:T(8,128)(2,1)}, bf16[128,1664]{1,0:T(8,128)(2,1)}, u32[]{:S(2)}, u32[]{:S(2)}) collective-permute-start(bf16[128,1664]{1,0:T(8,128)(2,1)} %get-tuple-element.47), channel_id=1, source_target_pairs={{0,2},{1,3},{2,0},{3,1},{4,6},{5,7},{6,4},{7,5},{8,10},{9,11},{10,... | collective-permute-start | bytes 1277960 | tf_op jit(solution)/shard_map/ppermute | solution.py:264
  120.4 2.3 %collective-permute-start.7 = (bf16[128,1664]{1,0:T(8,128)(2,1)}, bf16[128,1664]{1,0:T(8,128)(2,1)}, u32[]{:S(2)}, u32[]{:S(2)}) collective-permute-start(bf16[128,1664]{1,0:T(8,128)(2,1)} %get-tuple-element.46), channel_id=1, source_target_pairs={{0,1},{1,2},{2,3},{3,0},{4,5},{5,6},{6,7},{7,4},{8,9},{9,10},{10,1... | collective-permute-start | bytes 1277960 | tf_op jit(solution)/shard_map/ppermute | solution.py:264
  122.7 2.2 %shard_map.103 = bf16[512,1024]{1,0:T(8,128)(2,1)} custom-call(s32[1]{0:T(128)} %bitcast.11.here, bf16[128,768]{1,0:T(8,128)(2,1)S(1)} %shard_map.102.refs_0_, bf16[128,768]{1,0:T(8,128)(2,1)S(1)} %collective-permute-done.4.refs_1_, bf16[128,768]{1,0:T(8,128)(2,1)S(1)} %collective-permute-done.5.refs_2_, ...), custom_call_target="tpu_custom_call" | custom-call | flops 805306368 | bytes 3407872 | tf_op jit(solution)/shard_map/pallas_call | solution.py:136
  124.9 12.9 %all-to-all-start.3 = ((bf16[64,8,1024]{2,1,0:T(8,128)(2,1)}), bf16[64,8,1024]{2,1,0:T(8,128)(2,1)S(1)}, u32[]{:S(2)}, u32[]{:S(2)}) async-start(bf16[64,8,1024]{2,1,0:T(8,128)(2,1)} %bitcast.21), calls=%async_computation.3 | async-start | bytes 2097152 | tf_op jit(solution)/shard_map/all_to_all | solution.py:203
  137.9 0.4 collective-permute-done.7
  138.2 1.5 convert_add_fusion
  139.7 0.2 fusion.41
  139.9 0.2 fusion.20.refs_0_
  140.1 3.6 %collective-permute-start.10 = (bf16[128,768]{1,0:T(8,128)(2,1)S(1)}, bf16[128,768]{1,0:T(8,128)(2,1)S(1)}, u32[]{:S(2)}, u32[]{:S(2)}) collective-permute-start(bf16[128,768]{1,0:T(8,128)(2,1)S(1)} %fusion.20.refs_0_), channel_id=1, source_target_pairs={{0,1},{1,2},{2,3},{3,0},{4,5},{5,6},{6,7},{7,4},{8,9},{9,10},{10,1... | collective-permute-start | bytes 589832 | tf_op jit(solution)/shard_map/ppermute | solution.py:268
  143.7 3.1 %collective-permute-start.11 = (bf16[128,768]{1,0:T(8,128)(2,1)S(1)}, bf16[128,768]{1,0:T(8,128)(2,1)S(1)}, u32[]{:S(2)}, u32[]{:S(2)}) collective-permute-start(bf16[128,768]{1,0:T(8,128)(2,1)S(1)} %fusion.20.refs_0_), channel_id=1, source_target_pairs={{0,2},{1,3},{2,0},{3,1},{4,6},{5,7},{6,4},{7,5},{8,10},{9,11},{10,... | collective-permute-start | bytes 589832 | tf_op jit(solution)/shard_map/ppermute | solution.py:268
  146.8 3.1 %collective-permute-start.12 = (bf16[128,768]{1,0:T(8,128)(2,1)S(1)}, bf16[128,768]{1,0:T(8,128)(2,1)S(1)}, u32[]{:S(2)}, u32[]{:S(2)}) collective-permute-start(bf16[128,768]{1,0:T(8,128)(2,1)S(1)} %fusion.20.refs_0_), channel_id=1, source_target_pairs={{0,3},{1,0},{2,1},{3,2},{4,7},{5,4},{6,5},{7,6},{8,11},{9,8},{10,9... | collective-permute-start | bytes 589832 | tf_op jit(solution)/shard_map/ppermute | solution.py:268
  149.9 4.0 %collective-permute-done.11.refs_2_ = bf16[128,768]{1,0:T(8,128)(2,1)S(1)} collective-permute-done((bf16[128,768]{1,0:T(8,128)(2,1)S(1)}, bf16[128,768]{1,0:T(8,128)(2,1)S(1)}, u32[]{:S(2)}, u32[]{:S(2)}) %collective-permute-start.11) | collective-permute-done | bytes 196640 | tf_op jit(solution)/shard_map/ppermute | solution.py:268
  153.9 1.4 shard_map.104
  155.3 0.0 copy-start.10
  155.4 0.0 copy-start.11
  155.4 6.3 %collective-permute-start.13 = (bf16[512,1024]{1,0:T(8,128)(2,1)S(1)}, bf16[512,1024]{1,0:T(8,128)(2,1)}, u32[]{:S(2)}, u32[]{:S(2)}) collective-permute-start(bf16[512,1024]{1,0:T(8,128)(2,1)S(1)} %shard_map.104), channel_id=1, source_target_pairs={{0,32},{32,0},{1,33},{33,1},{2,34},{34,2},{3,35},{35,3},{4,36},{36... | collective-permute-start | bytes 3145736 | tf_op jit(solution)/shard_map/ppermute | solution.py:207
  161.7 2.4 %collective-permute-done.13 = bf16[512,1024]{1,0:T(8,128)(2,1)} collective-permute-done((bf16[512,1024]{1,0:T(8,128)(2,1)S(1)}, bf16[512,1024]{1,0:T(8,128)(2,1)}, u32[]{:S(2)}, u32[]{:S(2)}) %collective-permute-start.13) | collective-permute-done | bytes 1048608 | tf_op jit(solution)/shard_map/ppermute | solution.py:207
  164.1 16.5 %all-to-all-start.4 = ((bf16[64,8,1024]{2,1,0:T(8,128)(2,1)}), bf16[64,8,1024]{2,1,0:T(8,128)(2,1)S(1)}, u32[]{:S(2)}, u32[]{:S(2)}) async-start(bf16[64,8,1024]{2,1,0:T(8,128)(2,1)} %bitcast.23), calls=%async_computation.4 | async-start | bytes 2097152 | tf_op jit(solution)/shard_map/all_to_all | solution.py:203
  180.7 0.1 fusion.21
  180.8 0.1 pad_maximum_fusion.2
  180.9 0.1 pad_maximum_fusion.1
  181.1 0.5 convolution_bitcast_fusion.1
  181.6 26.0 %all-to-all-done.4 = bf16[64,8,1024]{2,1,0:T(8,128)(2,1)S(1)} async-done(((bf16[64,8,1024]{2,1,0:T(8,128)(2,1)}), bf16[64,8,1024]{2,1,0:T(8,128)(2,1)S(1)}, u32[]{:S(2)}, u32[]{:S(2)}) %all-to-all-start.4) | async-done | bytes 1048608 | tf_op jit(solution)/shard_map/all_to_all | solution.py:203
  207.6 0.5 convolution_bitcast_fusion
  208.1 0.7 fusion.24
  (34 shorter events, 0.2 us)
Async XLA Ops:
  0.0 22.7 %copy-start = (bf16[64,1024]{1,0:T(8,128)(2,1)S(1)}, bf16[64,1024]{1,0:T(8,128)(2,1)}, u32[]{:S(2)}) copy-start(bf16[64,1024]{1,0:T(8,128)(2,1)} %param.10) | copy-start | bytes 393220
  1.5 21.2 %all-to-all-start = ((bf16[8,64,256]{2,1,0:T(8,128)(2,1)}), bf16[8,64,256]{2,1,0:T(8,128)(2,1)S(1)}, u32[]{:S(2)}, u32[]{:S(2)}) async-start(bf16[8,64,256]{2,1,0:T(8,128)(2,1)} %broadcast_in_dim.106), calls=%async_computation | async-start | bytes 524288 | tf_op jit(solution)/shard_map/all_to_all | solution.py:43
  23.7 10.6 %copy-start.6 = (bf16[8,8,8,128]{3,2,1,0:T(8,128)(2,1)}, bf16[8,8,8,128]{3,2,1,0:T(8,128)(2,1)S(1)}, u32[]{:S(2)}) copy-start(bf16[8,8,8,128]{3,2,1,0:T(8,128)(2,1)S(1)} %fusion.13) | copy-start | bytes 393220
  25.1 35.6 %all-to-all-start.1 = ((bf16[64,8,1024]{2,1,0:T(8,128)(2,1)}), bf16[64,8,1024]{2,1,0:T(8,128)(2,1)S(1)}, u32[]{:S(2)}, u32[]{:S(2)}) async-start(bf16[64,8,1024]{2,1,0:T(8,128)(2,1)} %fusion.1), calls=%async_computation.1 | async-start | bytes 2097152 | tf_op jit(solution)/shard_map/all_to_all | solution.py:203
  34.3 26.4 %copy-start.8 = (s32[64,64]{1,0:T(8,128)}, s32[64,64]{1,0:T(8,128)S(1)}, u32[]{:S(2)}) copy-start(s32[64,64]{1,0:T(8,128)S(1)} %fusion.14) | copy-start | bytes 49156
  34.3 35.7 %copy-start.12 = (bf16[1024]{0:T(1024)(128)(2,1)S(1)}, bf16[1024]{0:T(1024)(128)(2,1)}, u32[]{:S(2)}) copy-start(bf16[1024]{0:T(1024)(128)(2,1)} %param.14) | copy-start | bytes 6148
  34.7 5.9 %collective-permute-start.3 = (bf16[512,1024]{1,0:T(8,128)(2,1)S(1)}, bf16[512,1024]{1,0:T(8,128)(2,1)}, u32[]{:S(2)}, u32[]{:S(2)}) collective-permute-start(bf16[512,1024]{1,0:T(8,128)(2,1)S(1)} %convolution_convert_fusion), channel_id=1, source_target_pairs={{0,32},{32,0},{1,33},{33,1},{2,34},{34,2},{3,35},{35,3},{4,36},{36... | collective-permute-start | bytes 3145736 | tf_op jit(solution)/shard_map/ppermute | solution.py:207
  60.7 35.7 %all-to-all-start.2 = ((bf16[64,8,1024]{2,1,0:T(8,128)(2,1)}), bf16[64,8,1024]{2,1,0:T(8,128)(2,1)S(1)}, u32[]{:S(2)}, u32[]{:S(2)}) async-start(bf16[64,8,1024]{2,1,0:T(8,128)(2,1)} %bitcast.18), calls=%async_computation.2 | async-start | bytes 2097152 | tf_op jit(solution)/shard_map/all_to_all | solution.py:203
  70.0 1.4 copy-start.2
  71.4 1.4 copy-start.4
  75.9 13.5 %collective-permute-start.1 = (bf16[128,1664]{1,0:T(8,128)(2,1)S(1)}, bf16[128,1664]{1,0:T(8,128)(2,1)S(1)}, u32[]{:S(2)}, u32[]{:S(2)}) collective-permute-start(bf16[128,1664]{1,0:T(8,128)(2,1)S(1)} %get-tuple-element.29), channel_id=1, source_target_pairs={{0,2},{1,3},{2,0},{3,1},{4,6},{5,7},{6,4},{7,5},{8,10},{9,11},{10,... | collective-permute-start | bytes 1277960 | tf_op jit(solution)/shard_map/ppermute | solution.py:264
  80.5 21.9 %collective-permute-start = (bf16[128,1664]{1,0:T(8,128)(2,1)}, bf16[128,1664]{1,0:T(8,128)(2,1)S(1)}, u32[]{:S(2)}, u32[]{:S(2)}) collective-permute-start(bf16[128,1664]{1,0:T(8,128)(2,1)} %get-tuple-element.28), channel_id=1, source_target_pairs={{0,1},{1,2},{2,3},{3,0},{4,5},{5,6},{6,7},{7,4},{8,9},{9,10},{10,1... | collective-permute-start | bytes 1277960 | tf_op jit(solution)/shard_map/ppermute | solution.py:264
  82.7 19.7 %collective-permute-start.2 = (bf16[128,1664]{1,0:T(8,128)(2,1)}, bf16[128,1664]{1,0:T(8,128)(2,1)}, u32[]{:S(2)}, u32[]{:S(2)}) collective-permute-start(bf16[128,1664]{1,0:T(8,128)(2,1)} %get-tuple-element.30), channel_id=1, source_target_pairs={{0,3},{1,0},{2,1},{3,2},{4,7},{5,4},{6,5},{7,6},{8,11},{9,8},{10,9... | collective-permute-start | bytes 1277960 | tf_op jit(solution)/shard_map/ppermute | solution.py:264
  96.4 1.4 copy-start.3
  97.8 1.4 copy-start.5
  102.4 20.3 %copy-start.1 = (bf16[1,768,1024]{2,1,0:T(8,128)(2,1)S(1)}, bf16[1,768,1024]{2,1,0:T(8,128)(2,1)}, u32[]{:S(2)}) copy-start(bf16[1,768,1024]{2,1,0:T(8,128)(2,1)} %param.19) | copy-start | bytes 4718596
  103.9 9.4 %collective-permute-start.6 = (bf16[128,768]{1,0:T(8,128)(2,1)S(1)}, bf16[128,768]{1,0:T(8,128)(2,1)S(1)}, u32[]{:S(2)}, u32[]{:S(2)}) collective-permute-start(bf16[128,768]{1,0:T(8,128)(2,1)S(1)} %shard_map.102.refs_0_), channel_id=1, source_target_pairs={{0,3},{1,0},{2,1},{3,2},{4,7},{5,4},{6,5},{7,6},{8,11},{9,8},{10,9... | collective-permute-start | bytes 589832 | tf_op jit(solution)/shard_map/ppermute | solution.py:268
  108.3 9.0 %collective-permute-start.5 = (bf16[128,768]{1,0:T(8,128)(2,1)S(1)}, bf16[128,768]{1,0:T(8,128)(2,1)S(1)}, u32[]{:S(2)}, u32[]{:S(2)}) collective-permute-start(bf16[128,768]{1,0:T(8,128)(2,1)S(1)} %shard_map.102.refs_0_), channel_id=1, source_target_pairs={{0,2},{1,3},{2,0},{3,1},{4,6},{5,7},{6,4},{7,5},{8,10},{9,11},{10,... | collective-permute-start | bytes 589832 | tf_op jit(solution)/shard_map/ppermute | solution.py:268
  110.7 9.7 %collective-permute-start.4 = (bf16[128,768]{1,0:T(8,128)(2,1)S(1)}, bf16[128,768]{1,0:T(8,128)(2,1)S(1)}, u32[]{:S(2)}, u32[]{:S(2)}) collective-permute-start(bf16[128,768]{1,0:T(8,128)(2,1)S(1)} %shard_map.102.refs_0_), channel_id=1, source_target_pairs={{0,1},{1,2},{2,3},{3,0},{4,5},{5,6},{6,7},{7,4},{8,9},{9,10},{10,1... | collective-permute-start | bytes 589832 | tf_op jit(solution)/shard_map/ppermute | solution.py:268
  113.3 24.6 %collective-permute-start.9 = (bf16[128,1664]{1,0:T(8,128)(2,1)}, bf16[128,1664]{1,0:T(8,128)(2,1)}, u32[]{:S(2)}, u32[]{:S(2)}) collective-permute-start(bf16[128,1664]{1,0:T(8,128)(2,1)} %get-tuple-element.48), channel_id=1, source_target_pairs={{0,3},{1,0},{2,1},{3,2},{4,7},{5,4},{6,5},{7,6},{8,11},{9,8},{10,9... | collective-permute-start | bytes 1277960 | tf_op jit(solution)/shard_map/ppermute | solution.py:264
  117.3 20.6 %collective-permute-start.8 = (bf16[128,1664]{1,0:T(8,128)(2,1)}, bf16[128,1664]{1,0:T(8,128)(2,1)}, u32[]{:S(2)}, u32[]{:S(2)}) collective-permute-start(bf16[128,1664]{1,0:T(8,128)(2,1)} %get-tuple-element.47), channel_id=1, source_target_pairs={{0,2},{1,3},{2,0},{3,1},{4,6},{5,7},{6,4},{7,5},{8,10},{9,11},{10,... | collective-permute-start | bytes 1277960 | tf_op jit(solution)/shard_map/ppermute | solution.py:264
  120.4 17.8 %collective-permute-start.7 = (bf16[128,1664]{1,0:T(8,128)(2,1)}, bf16[128,1664]{1,0:T(8,128)(2,1)}, u32[]{:S(2)}, u32[]{:S(2)}) collective-permute-start(bf16[128,1664]{1,0:T(8,128)(2,1)} %get-tuple-element.46), channel_id=1, source_target_pairs={{0,1},{1,2},{2,3},{3,0},{4,5},{5,6},{6,7},{7,4},{8,9},{9,10},{10,1... | collective-permute-start | bytes 1277960 | tf_op jit(solution)/shard_map/ppermute | solution.py:264
  124.9 39.2 %all-to-all-start.3 = ((bf16[64,8,1024]{2,1,0:T(8,128)(2,1)}), bf16[64,8,1024]{2,1,0:T(8,128)(2,1)S(1)}, u32[]{:S(2)}, u32[]{:S(2)}) async-start(bf16[64,8,1024]{2,1,0:T(8,128)(2,1)} %bitcast.21), calls=%async_computation.3 | async-start | bytes 2097152 | tf_op jit(solution)/shard_map/all_to_all | solution.py:203
  140.1 9.9 %collective-permute-start.10 = (bf16[128,768]{1,0:T(8,128)(2,1)S(1)}, bf16[128,768]{1,0:T(8,128)(2,1)S(1)}, u32[]{:S(2)}, u32[]{:S(2)}) collective-permute-start(bf16[128,768]{1,0:T(8,128)(2,1)S(1)} %fusion.20.refs_0_), channel_id=1, source_target_pairs={{0,1},{1,2},{2,3},{3,0},{4,5},{5,6},{6,7},{7,4},{8,9},{9,10},{10,1... | collective-permute-start | bytes 589832 | tf_op jit(solution)/shard_map/ppermute | solution.py:268
  143.7 10.2 %collective-permute-start.11 = (bf16[128,768]{1,0:T(8,128)(2,1)S(1)}, bf16[128,768]{1,0:T(8,128)(2,1)S(1)}, u32[]{:S(2)}, u32[]{:S(2)}) collective-permute-start(bf16[128,768]{1,0:T(8,128)(2,1)S(1)} %fusion.20.refs_0_), channel_id=1, source_target_pairs={{0,2},{1,3},{2,0},{3,1},{4,6},{5,7},{6,4},{7,5},{8,10},{9,11},{10,... | collective-permute-start | bytes 589832 | tf_op jit(solution)/shard_map/ppermute | solution.py:268
  146.8 7.1 %collective-permute-start.12 = (bf16[128,768]{1,0:T(8,128)(2,1)S(1)}, bf16[128,768]{1,0:T(8,128)(2,1)S(1)}, u32[]{:S(2)}, u32[]{:S(2)}) collective-permute-start(bf16[128,768]{1,0:T(8,128)(2,1)S(1)} %fusion.20.refs_0_), channel_id=1, source_target_pairs={{0,3},{1,0},{2,1},{3,2},{4,7},{5,4},{6,5},{7,6},{8,11},{9,8},{10,9... | collective-permute-start | bytes 589832 | tf_op jit(solution)/shard_map/ppermute | solution.py:268
  155.3 25.3 %copy-start.10 = (s32[64,8]{0,1:T(8,128)S(1)}, s32[64,8]{0,1:T(8,128)}, u32[]{:S(2)}) copy-start(s32[64,8]{0,1:T(8,128)} %param.15) | copy-start | bytes 6148
  155.4 25.3 %copy-start.11 = (f32[64,8]{0,1:T(8,128)S(1)}, f32[64,8]{0,1:T(8,128)}, u32[]{:S(2)}) copy-start(f32[64,8]{0,1:T(8,128)} %param.16) | copy-start | bytes 6148
  155.4 25.6 %copy-start.9 = (s32[64,64]{1,0:T(8,128)S(1)}, s32[64,64]{1,0:T(8,128)}, u32[]{:S(2)}) copy-start(s32[64,64]{1,0:T(8,128)} %copy-done.8) | copy-start | bytes 49156
  155.4 8.7 %collective-permute-start.13 = (bf16[512,1024]{1,0:T(8,128)(2,1)S(1)}, bf16[512,1024]{1,0:T(8,128)(2,1)}, u32[]{:S(2)}, u32[]{:S(2)}) collective-permute-start(bf16[512,1024]{1,0:T(8,128)(2,1)S(1)} %shard_map.104), channel_id=1, source_target_pairs={{0,32},{32,0},{1,33},{33,1},{2,34},{34,2},{3,35},{35,3},{4,36},{36... | collective-permute-start | bytes 3145736 | tf_op jit(solution)/shard_map/ppermute | solution.py:207
  164.1 43.5 %all-to-all-start.4 = ((bf16[64,8,1024]{2,1,0:T(8,128)(2,1)}), bf16[64,8,1024]{2,1,0:T(8,128)(2,1)S(1)}, u32[]{:S(2)}, u32[]{:S(2)}) async-start(bf16[64,8,1024]{2,1,0:T(8,128)(2,1)} %bitcast.23), calls=%async_computation.4 | async-start | bytes 2097152 | tf_op jit(solution)/shard_map/all_to_all | solution.py:203
  181.1 27.0 %copy-start.7 = (bf16[8,8,8,128]{3,2,1,0:T(8,128)(2,1)S(1)}, bf16[8,8,8,128]{3,2,1,0:T(8,128)(2,1)}, u32[]{:S(2)}) copy-start(bf16[8,8,8,128]{3,2,1,0:T(8,128)(2,1)} %copy-done.6) | copy-start | bytes 393220

commit v3 on v2

--- a/solution.py
+++ b/solution.py
@@ -13,6 +13,7 @@
 CAP = 8
 LANES = 128
 VMEM_LIMIT = 32 * 1024 * 1024
+WIDE_LIMIT = 50 * 1024 * 1024
 BF = jnp.bfloat16
 F32 = jnp.float32
 GROUP = ("y", "expert")
@@ -55,59 +56,70 @@
     return jnp.transpose(result, (1, 0, 2)).reshape(tok_rows, heads_here * head_size).astype(BF)
 
 
+def move(source, target, sem):
+    copy = pltpu.make_async_copy(source, target, sem)
+    copy.start()
+    return copy
+
+
 def gate_up_kernel(here, rows, gain, gate, up, *rest, size, waits):
-    outs, scaled = rest[waits : waits + size], rest[waits + size]
-    block = rows.shape[0] // size
+    outs = rest[waits : waits + size]
+    scaled, gate_held, up_held, sems = rest[waits + size :]
+    count, feat = rows.shape
     hidden = gate.shape[1]
-    step = pl.program_id(0)
-
-    @pl.when(step == 0)
-    def _():
-        lane = lax.broadcasted_iota(jnp.int32, (block, LANES), 1)
+    block, slab = count // size, feat // size
+    copies = []
+    for source, target in ((gate, gate_held), (up, up_held)):
         for k in range(size):
-            at = lax.rem(here[0] + k, size) * block
-            wide = rows[pl.ds(pl.multiple_of(at, block), block), :].astype(F32)
-            squares = jnp.sum(wide * wide, axis=1, keepdims=True)
-            high = squares.astype(BF).astype(F32)
-            extra = jnp.where(lane == 0, high, jnp.where(lane == 1, squares - high, 0.0))
-            outs[k][:, 2 * hidden :] = extra.astype(BF)
-            scaled[pl.ds(k * block, block), :] = (wide * gain[...].astype(F32)).astype(BF)
+            part = pl.ds(k * slab, slab)
+            copies.append(move(source.at[part, :], target.at[part, :], sems.at[len(copies)]))
+
+    lane = lax.broadcasted_iota(jnp.int32, (block, LANES), 1)
+    for k in range(size):
+        at = pl.multiple_of(lax.rem(here[0] + k, size) * block, block)
+        wide = rows[pl.ds(at, block), :].astype(F32)
+        squares = jnp.sum(wide * wide, axis=1, keepdims=True)
+        high = squares.astype(BF).astype(F32)
+        extra = jnp.where(lane == 0, high, jnp.where(lane == 1, squares - high, 0.0))
+        outs[k][:, 2 * hidden :] = extra.astype(BF)
+        scaled[k * block : (k + 1) * block, :] = (wide * gain[...].astype(F32)).astype(BF)
 
     def product(weight, low):
         part = jnp.dot(scaled[...], weight[...], preferred_element_type=F32).astype(BF)
         for k in range(size):
             outs[k][:, low : low + hidden] = part[k * block : (k + 1) * block, :]
 
-    @pl.when(step == 0)
-    def _():
-        product(gate, 0)
-
-    @pl.when(step == 1)
-    def _():
-        product(up, hidden)
+    for copy in copies[:size]:
+        copy.wait()
+    product(gate_held, 0)
+    for copy in copies[size:]:
+        copy.wait()
+    product(up_held, hidden)
 
 
 def gate_up(here, rows, gain, gate, up, after):
     size = lax.axis_size("tensor")
     feat, hidden = gate.shape
-    block = rows.shape[0] // size
+    count = rows.shape[0]
+    block = count // size
     width = 2 * hidden + LANES
-    kernel = functools.partial(gate_up_kernel, size=size, waits=len(after))
+    near, far = pl.BlockSpec(memory_space=pltpu.VMEM), pl.BlockSpec(memory_space=pl.ANY)
     return pl.pallas_call(
-        kernel,
-        grid_spec=pltpu.PrefetchScalarGridSpec(
-            num_scalar_prefetch=1,
-            grid=(2,),
-            in_specs=[whole(rows.shape), whole((1, feat)), whole(gate.shape), whole(up.shape)]
-            + [pl.BlockSpec(memory_space=pl.ANY)] * len(after),
-            out_specs=[whole((block, width))] * size,
-            scratch_shapes=[pltpu.VMEM(rows.shape, BF)],
-        ),
+        functools.partial(gate_up_kernel, size=size, waits=len(after)),
+        in_specs=[pl.BlockSpec(memory_space=pltpu.SMEM), near, near, far, far]
+        + [pl.BlockSpec(memory_space=pl.ANY)] * len(after),
+        out_specs=[near] * size,
+        scratch_shapes=[
+            pltpu.VMEM(rows.shape, BF),
+            pltpu.VMEM(gate.shape, BF),
+            pltpu.VMEM(up.shape, BF),
+            pltpu.SemaphoreType.DMA((2 * size,)),
+        ],
         out_shape=[jax.ShapeDtypeStruct((block, width), BF)] * size,
-        compiler_params=pltpu.CompilerParams(vmem_limit_bytes=VMEM_LIMIT),
+        compiler_params=pltpu.CompilerParams(vmem_limit_bytes=WIDE_LIMIT),
         cost_estimate=pl.CostEstimate(
-            flops=4 * rows.shape[0] * feat * hidden,
-            bytes_accessed=2 * (rows.size + 2 * gate.size + rows.shape[0] * width),
+            flops=4 * count * feat * hidden,
+            bytes_accessed=2 * (rows.size + 2 * gate.size + count * width),
             transcendentals=0,
         ),
     )(here, rows, gain, gate, up, *after)
@@ -259,13 +271,14 @@
     def blocks(flat):
         return flat.reshape(peers, CAP, feat)
 
+    steps = sorted(range(1, size), key=lambda step: -min(step, size - step))
+
     def fetch_parts(parts):
-        return [parts[0]] + [
-            lax.ppermute(parts[step], "tensor", ring(size, step)) for step in range(1, size)
-        ]
+        got = {step: lax.ppermute(parts[step], "tensor", ring(size, step)) for step in steps}
+        return [parts[0]] + [got[step] for step in range(1, size)]
 
     def spread(piece):
-        return [piece] + [lax.ppermute(piece, "tensor", ring(size, k)) for k in range(1, size)]
+        return fetch_parts([piece] * size)
 
     def combine(mix, returned):
         both = lax.dot_general(
@@ -281,11 +294,10 @@
 
     near_parts = gate_up(here, near, gain, gate_rows, up_rows, [])
     near_got = fetch_parts(near_parts)
-    far_parts = gate_up(here, far, gain, gate_rows, up_rows, [near_got[size // 2]])
-    near_got, far_parts = lax.optimization_barrier((near_got, far_parts))
-    far_parts = list(far_parts)
-    near_pieces = spread(silu_call(near_got, hidden_size))
-    for step in range(1, size):
+    early = near_got[0].astype(F32) + near_got.pop(size // 2).astype(F32)
+    near_pieces = spread(silu_call([early] + near_got[1:], hidden_size))
+    far_parts = list(gate_up(here, far, gain, gate_rows, up_rows, [near_pieces[0]]))
+    for step in steps:
         near_pieces[step], far_parts[step] = lax.optimization_barrier(
             (near_pieces[step], far_parts[step])
         )

time: 213 us -> 211 us (level)
  waiting for transfers between devices: 72.6 us -> 83.6 us
  starting transfers between devices: 108 us -> 97.9 us
  local copies, waits for them, and re-layouts: 6.39 us -> 0.75 us
  Pallas kernels: 11.3 us -> 14.1 us
    ppermute x6 -> x12, waiting for transfers between devices: 2.72 us -> 24.7 us  [fetch_parts(): lax.ppermute(parts[step], 'tensor', ring(size, step))]
    ppermute x6 -> x0, starting transfers between devices: 19.2 us -> none  [spread(): lax.ppermute(piece, 'tensor', ring(size, k))]
    ppermute x6 -> x12, starting transfers between devices: 20.5 us -> 37.5 us  [fetch_parts(): lax.ppermute(parts[step], 'tensor', ring(size, step))]
    all_to_all x4, waiting for transfers between devices: 53.2 us -> 46.2 us  [exchange(): return lax.all_to_all(block, GROUP, split_axis=0, concat_axis=0, tiled=True)]
    unnamed x26 -> x14, local copies, waits for them, and re-layouts: 5.67 us -> 0.04 us
    all_to_all x4, starting transfers between devices: 47.7 us -> 42.6 us  [exchange(): return lax.all_to_all(block, GROUP, split_axis=0, concat_axis=0, tiled=True)]
    ppermute x6 -> x0, waiting for transfers between devices: 4 us -> none  [spread(): lax.ppermute(piece, 'tensor', ring(size, k))]
    pallas_call x2, Pallas kernels: 6.14 us -> 9.05 us  [gate_up(): pl.pallas_call(functools.partial(gate_up_kernel, size=size, waits=len(aft...]
  transfers between devices with their start and end apart: 19 -> 19, of which waited for: 9 -> 10; matrix products, arithmetic and copies ran while one was open for 3% -> 3% of each run, Pallas kernels for 5% -> 7%
where the time goes in v3:
time: 211 us; the launch traced here: 207 us
  starting transfers between devices  97.9 us (46%)
  waiting for transfers between devices  83.6 us (40%)
  Pallas kernels  14.1 us (7%)
  other arithmetic  6.57 us (3%)
  matrix products  3.61 us (2%)
    all_to_all x4, waiting for transfers between devices, exchange(): return lax.all_to_all(block, GROUP, split_axis=0, concat_axis=0, tiled=True)  46.2 us
    all_to_all x4, starting transfers between devices, exchange(): return lax.all_to_all(block, GROUP, split_axis=0, concat_axis=0, tiled=True)  42.6 us
    ppermute x12, starting transfers between devices, fetch_parts(): lax.ppermute(parts[step], 'tensor', ring(size, step))  37.5 us
    ppermute x12, waiting for transfers between devices, fetch_parts(): lax.ppermute(parts[step], 'tensor', ring(size, step))  24.7 us
    all_to_all x1, starting transfers between devices, attention(): lax.all_to_all(copies, 'expert', split_axis=0, concat_axis=0, tiled=True)  10.9 us
    pallas_call x2, Pallas kernels, gate_up(): pl.pallas_call(functools.partial(gate_up_kernel, size=size, waits=len(aft...  9.05 us
    all_to_all x1, waiting for transfers between devices, attention(): lax.all_to_all(copies, 'expert', split_axis=0, concat_axis=0, tiled=True)  7.9 us
    ppermute x2, starting transfers between devices, swap(): return lax.ppermute(block, 'core', [(0, 1), (1, 0)])  7.01 us
  transfers between devices with their start and end apart: 19, of which 10 were waited for; matrix products, arithmetic and copies ran while one was open for 3% of the time, Pallas kernels for 7%

profile of v3, /device:TPU:1, one launch (start us, length us, event | category | flops | bytes accessed | tf_op | source)
XLA Modules:
  0.0 206.9 jit_solution(13000040386686658824)
XLA Ops:
  0.0 0.8 pad_maximum_fusion
  0.8 0.7 broadcast_in_dim.106
  1.5 10.9 %all-to-all-start = ((bf16[8,64,256]{2,1,0:T(8,128)(2,1)}), bf16[8,64,256]{2,1,0:T(8,128)(2,1)S(1)}, u32[]{:S(2)}, u32[]{:S(2)}) async-start(bf16[8,64,256]{2,1,0:T(8,128)(2,1)} %broadcast_in_dim.106), calls=%async_computation | async-start | bytes 524288 | tf_op jit(solution)/shard_map/all_to_all | solution.py:44
  12.4 0.7 add_bitcast_fusion.1
  13.0 0.8 compare_reduce_fusion
  13.9 0.7 select_reduce_fusion.1
  14.6 0.1 iota_compare_fusion.2
  14.7 0.1 fusion.15
  14.8 7.9 %all-to-all-done = bf16[8,64,256]{2,1,0:T(8,128)(2,1)S(1)} async-done(((bf16[8,64,256]{2,1,0:T(8,128)(2,1)}), bf16[8,64,256]{2,1,0:T(8,128)(2,1)S(1)}, u32[]{:S(2)}, u32[]{:S(2)}) %all-to-all-start) | async-done | bytes 262176 | tf_op jit(solution)/shard_map/all_to_all | solution.py:44
  22.7 0.3 fusion.10
  23.0 0.4 fusion.50
  23.4 0.3 fusion.13
  23.7 1.4 fusion.1
  25.1 9.0 %all-to-all-start.1 = ((bf16[64,8,1024]{2,1,0:T(8,128)(2,1)}), bf16[64,8,1024]{2,1,0:T(8,128)(2,1)S(1)}, u32[]{:S(2)}, u32[]{:S(2)}) async-start(bf16[64,8,1024]{2,1,0:T(8,128)(2,1)} %fusion.1), calls=%async_computation.1 | async-start | bytes 2097152 | tf_op jit(solution)/shard_map/all_to_all | solution.py:215
  34.2 0.1 fusion.14
  34.3 0.4 convolution_convert_fusion
  34.7 3.4 %collective-permute-start.4 = (bf16[512,1024]{1,0:T(8,128)(2,1)S(1)}, bf16[512,1024]{1,0:T(8,128)(2,1)}, u32[]{:S(2)}, u32[]{:S(2)}) collective-permute-start(bf16[512,1024]{1,0:T(8,128)(2,1)S(1)} %convolution_convert_fusion), channel_id=1, source_target_pairs={{0,32},{32,0},{1,33},{33,1},{2,34},{34,2},{3,35},{35,3},{4,36},{36... | collective-permute-start | bytes 3145736 | tf_op jit(solution)/shard_map/ppermute | solution.py:219
  38.2 2.4 %collective-permute-done.4 = bf16[512,1024]{1,0:T(8,128)(2,1)} collective-permute-done((bf16[512,1024]{1,0:T(8,128)(2,1)S(1)}, bf16[512,1024]{1,0:T(8,128)(2,1)}, u32[]{:S(2)}, u32[]{:S(2)}) %collective-permute-start.4) | collective-permute-done | bytes 1048608 | tf_op jit(solution)/shard_map/ppermute | solution.py:219
  40.6 20.1 %all-to-all-done.1 = bf16[64,8,1024]{2,1,0:T(8,128)(2,1)S(1)} async-done(((bf16[64,8,1024]{2,1,0:T(8,128)(2,1)}), bf16[64,8,1024]{2,1,0:T(8,128)(2,1)S(1)}, u32[]{:S(2)}, u32[]{:S(2)}) %all-to-all-start.1) | async-done | bytes 1048608 | tf_op jit(solution)/shard_map/all_to_all | solution.py:215
  60.7 9.3 %all-to-all-start.2 = ((bf16[64,8,1024]{2,1,0:T(8,128)(2,1)}), bf16[64,8,1024]{2,1,0:T(8,128)(2,1)S(1)}, u32[]{:S(2)}, u32[]{:S(2)}) async-start(bf16[64,8,1024]{2,1,0:T(8,128)(2,1)} %bitcast.18), calls=%async_computation.2 | async-start | bytes 2097152 | tf_op jit(solution)/shard_map/all_to_all | solution.py:215
  70.0 4.0 %shard_map.100 = (bf16[128,1664]{1,0:T(8,128)(2,1)S(1)}, bf16[128,1664]{1,0:T(8,128)(2,1)S(1)}, bf16[128,1664]{1,0:T(8,128)(2,1)S(1)}, bf16[128,1664]{1,0:T(8,128)(2,1)S(1)}) custom-call(s32[1]{0:T(128)} %bitcast.11.here, bf16[512,1024]{1,0:T(8,128)(2,1)S(1)} %bitcast.69, bf16[1,1024]{1,0:T(2,128)(2,1)S(1)} %broadcast_in_dim.115.gain, ...), custom_call_target="tpu_custom_call" | custom-call | flops 1610612736 | bytes 5898240 | tf_op jit(solution)/shard_map/pallas_call | solution.py:107
  74.0 4.7 %collective-permute-start = (bf16[128,1664]{1,0:T(8,128)(2,1)S(1)}, bf16[128,1664]{1,0:T(8,128)(2,1)S(1)}, u32[]{:S(2)}, u32[]{:S(2)}) collective-permute-start(bf16[128,1664]{1,0:T(8,128)(2,1)S(1)} %get-tuple-element.20), channel_id=1, source_target_pairs={{0,2},{1,3},{2,0},{3,1},{4,6},{5,7},{6,4},{7,5},{8,10},{9,11},{10,... | collective-permute-start | bytes 1277960 | tf_op jit(solution)/shard_map/ppermute | solution.py:277
  78.7 2.2 %collective-permute-start.1 = (bf16[128,1664]{1,0:T(8,128)(2,1)S(1)}, bf16[128,1664]{1,0:T(8,128)(2,1)S(1)}, u32[]{:S(2)}, u32[]{:S(2)}) collective-permute-start(bf16[128,1664]{1,0:T(8,128)(2,1)S(1)} %get-tuple-element.21), channel_id=1, source_target_pairs={{0,1},{1,2},{2,3},{3,0},{4,5},{5,6},{6,7},{7,4},{8,9},{9,10},{10,1... | collective-permute-start | bytes 1277960 | tf_op jit(solution)/shard_map/ppermute | solution.py:277
  80.9 4.3 %collective-permute-start.2 = (bf16[128,1664]{1,0:T(8,128)(2,1)S(1)}, bf16[128,1664]{1,0:T(8,128)(2,1)S(1)}, u32[]{:S(2)}, u32[]{:S(2)}) collective-permute-start(bf16[128,1664]{1,0:T(8,128)(2,1)S(1)} %get-tuple-element.22), channel_id=1, source_target_pairs={{0,3},{1,0},{2,1},{3,2},{4,7},{5,4},{6,5},{7,6},{8,11},{9,8},{10,9... | collective-permute-start | bytes 1277960 | tf_op jit(solution)/shard_map/ppermute | solution.py:277
  85.2 2.3 %collective-permute-done = bf16[128,1664]{1,0:T(8,128)(2,1)S(1)} collective-permute-done((bf16[128,1664]{1,0:T(8,128)(2,1)S(1)}, bf16[128,1664]{1,0:T(8,128)(2,1)S(1)}, u32[]{:S(2)}, u32[]{:S(2)}) %collective-permute-start) | collective-permute-done | bytes 426016 | tf_op jit(solution)/shard_map/ppermute | solution.py:277
  87.5 0.1 convert_add_fusion.1.refs_0_
  87.6 10.7 %collective-permute-done.1.refs_1_ = bf16[128,1664]{1,0:T(8,128)(2,1)S(1)} collective-permute-done((bf16[128,1664]{1,0:T(8,128)(2,1)S(1)}, bf16[128,1664]{1,0:T(8,128)(2,1)S(1)}, u32[]{:S(2)}, u32[]{:S(2)}) %collective-permute-start.1) | collective-permute-done | bytes 426016 | tf_op jit(solution)/shard_map/ppermute | solution.py:277
  98.3 0.3 shard_map.101.rest_0_.refs_0_
  98.6 3.7 %collective-permute-start.6 = (bf16[128,768]{1,0:T(8,128)(2,1)S(1)}, bf16[128,768]{1,0:T(8,128)(2,1)}, u32[]{:S(2)}, u32[]{:S(2)}) collective-permute-start(bf16[128,768]{1,0:T(8,128)(2,1)S(1)} %shard_map.101.rest_0_.refs_0_), channel_id=1, source_target_pairs={{0,3},{1,0},{2,1},{3,2},{4,7},{5,4},{6,5},{7,6},{8,11},{9,8},{10,9... | collective-permute-start | bytes 589832 | tf_op jit(solution)/shard_map/ppermute | solution.py:277
  102.4 3.1 %collective-permute-start.5 = (bf16[128,768]{1,0:T(8,128)(2,1)S(1)}, bf16[128,768]{1,0:T(8,128)(2,1)}, u32[]{:S(2)}, u32[]{:S(2)}) collective-permute-start(bf16[128,768]{1,0:T(8,128)(2,1)S(1)} %shard_map.101.rest_0_.refs_0_), channel_id=1, source_target_pairs={{0,2},{1,3},{2,0},{3,1},{4,6},{5,7},{6,4},{7,5},{8,10},{9,11},{10,... | collective-permute-start | bytes 589832 | tf_op jit(solution)/shard_map/ppermute | solution.py:277
  105.5 2.5 %collective-permute-start.3 = (bf16[128,768]{1,0:T(8,128)(2,1)S(1)}, bf16[128,768]{1,0:T(8,128)(2,1)}, u32[]{:S(2)}, u32[]{:S(2)}) collective-permute-start(bf16[128,768]{1,0:T(8,128)(2,1)S(1)} %shard_map.101.rest_0_.refs_0_), channel_id=1, source_target_pairs={{0,1},{1,2},{2,3},{3,0},{4,5},{5,6},{6,7},{7,4},{8,9},{9,10},{10,1... | collective-permute-start | bytes 589832 | tf_op jit(solution)/shard_map/ppermute | solution.py:277
  108.0 0.0 all-to-all-done.2
  108.0 0.0 copy-start.1
  108.0 5.1 %shard_map.102 = (bf16[128,1664]{1,0:T(8,128)(2,1)S(1)}, bf16[128,1664]{1,0:T(8,128)(2,1)}, bf16[128,1664]{1,0:T(8,128)(2,1)}, bf16[128,1664]{1,0:T(8,128)(2,1)}) custom-call(s32[1]{0:T(128)} %bitcast.11.here, bf16[512,1024]{1,0:T(8,128)(2,1)S(1)} %bitcast.68, bf16[1,1024]{1,0:T(2,128)(2,1)S(1)} %broadcast_in_dim.115.gain, bf16[1024,768]{1,0:T(8,128)(2,1)} %bitcast.77, ...), custom_call_target="tpu_custom_call" | custom-call | flops 1610612736 | bytes 5898240 | tf_op jit(solution)/shard_map/pallas_call | solution.py:107
  113.1 0.0 collective-permute-done.6.refs_3_
  113.1 4.0 %collective-permute-start.9 = (bf16[128,1664]{1,0:T(8,128)(2,1)}, bf16[128,1664]{1,0:T(8,128)(2,1)}, u32[]{:S(2)}, u32[]{:S(2)}) collective-permute-start(bf16[128,1664]{1,0:T(8,128)(2,1)} %get-tuple-element.32), channel_id=1, source_target_pairs={{0,3},{1,0},{2,1},{3,2},{4,7},{5,4},{6,5},{7,6},{8,11},{9,8},{10,9... | collective-permute-start | bytes 1277960 | tf_op jit(solution)/shard_map/ppermute | solution.py:277
  117.1 0.0 collective-permute-done.5.refs_2_
  117.1 2.5 %collective-permute-start.8 = (bf16[128,1664]{1,0:T(8,128)(2,1)}, bf16[128,1664]{1,0:T(8,128)(2,1)}, u32[]{:S(2)}, u32[]{:S(2)}) collective-permute-start(bf16[128,1664]{1,0:T(8,128)(2,1)} %get-tuple-element.31), channel_id=1, source_target_pairs={{0,2},{1,3},{2,0},{3,1},{4,6},{5,7},{6,4},{7,5},{8,10},{9,11},{10,... | collective-permute-start | bytes 1277960 | tf_op jit(solution)/shard_map/ppermute | solution.py:277
  119.6 1.9 collective-permute-start.7
  121.5 3.3 %shard_map.103 = bf16[512,1024]{1,0:T(8,128)(2,1)} custom-call(s32[1]{0:T(128)} %bitcast.11.here, bf16[128,768]{1,0:T(8,128)(2,1)S(1)} %shard_map.101.rest_0_.refs_0_, bf16[128,768]{1,0:T(8,128)(2,1)} %collective-permute-done.3.refs_1_, bf16[128,768]{1,0:T(8,128)(2,1)} %collective-permute-done.5.refs_2_, bf16[128,768]{1,0:T(8,128)(2,1)} %collective-permute-done.6.refs_3_, ...), custom_call_target="tpu_custom_call" | custom-call | flops 805306368 | bytes 3407872 | tf_op jit(solution)/shard_map/pallas_call | solution.py:148
  124.8 12.1 %all-to-all-start.3 = ((bf16[64,8,1024]{2,1,0:T(8,128)(2,1)}), bf16[64,8,1024]{2,1,0:T(8,128)(2,1)S(1)}, u32[]{:S(2)}, u32[]{:S(2)}) async-start(bf16[64,8,1024]{2,1,0:T(8,128)(2,1)} %bitcast.21), calls=%async_computation.3 | async-start | bytes 2097152 | tf_op jit(solution)/shard_map/all_to_all | solution.py:215
  137.0 4.7 %collective-permute-done.7 = bf16[128,1664]{1,0:T(8,128)(2,1)} collective-permute-done((bf16[128,1664]{1,0:T(8,128)(2,1)}, bf16[128,1664]{1,0:T(8,128)(2,1)}, u32[]{:S(2)}, u32[]{:S(2)}) %collective-permute-start.7) | collective-permute-done | bytes 426016 | tf_op jit(solution)/shard_map/ppermute | solution.py:277
  141.7 1.5 convert_add_fusion
  143.2 0.2 fusion.41
  143.3 0.2 fusion.20.refs_0_
  143.6 1.9 collective-permute-start.10
  145.5 2.5 %collective-permute-start.11 = (bf16[128,768]{1,0:T(8,128)(2,1)S(1)}, bf16[128,768]{1,0:T(8,128)(2,1)S(1)}, u32[]{:S(2)}, u32[]{:S(2)}) collective-permute-start(bf16[128,768]{1,0:T(8,128)(2,1)S(1)} %fusion.20.refs_0_), channel_id=1, source_target_pairs={{0,2},{1,3},{2,0},{3,1},{4,6},{5,7},{6,4},{7,5},{8,10},{9,11},{10,... | collective-permute-start | bytes 589832 | tf_op jit(solution)/shard_map/ppermute | solution.py:277
  148.0 4.2 %collective-permute-start.12 = (bf16[128,768]{1,0:T(8,128)(2,1)S(1)}, bf16[128,768]{1,0:T(8,128)(2,1)S(1)}, u32[]{:S(2)}, u32[]{:S(2)}) collective-permute-start(bf16[128,768]{1,0:T(8,128)(2,1)S(1)} %fusion.20.refs_0_), channel_id=1, source_target_pairs={{0,3},{1,0},{2,1},{3,2},{4,7},{5,4},{6,5},{7,6},{8,11},{9,8},{10,9... | collective-permute-start | bytes 589832 | tf_op jit(solution)/shard_map/ppermute | solution.py:277
  152.2 4.7 %collective-permute-done.10.refs_1_ = bf16[128,768]{1,0:T(8,128)(2,1)S(1)} collective-permute-done((bf16[128,768]{1,0:T(8,128)(2,1)S(1)}, bf16[128,768]{1,0:T(8,128)(2,1)S(1)}, u32[]{:S(2)}, u32[]{:S(2)}) %collective-permute-start.10) | collective-permute-done | bytes 196640 | tf_op jit(solution)/shard_map/ppermute | solution.py:277
  156.9 2.3 %collective-permute-done.12.refs_3_ = bf16[128,768]{1,0:T(8,128)(2,1)S(1)} collective-permute-done((bf16[128,768]{1,0:T(8,128)(2,1)S(1)}, bf16[128,768]{1,0:T(8,128)(2,1)S(1)}, u32[]{:S(2)}, u32[]{:S(2)}) %collective-permute-start.12) | collective-permute-done | bytes 196640 | tf_op jit(solution)/shard_map/ppermute | solution.py:277
  159.2 1.4 shard_map.104
  160.6 0.0 copy-start.4
  160.6 0.0 copy-start.5
  160.6 0.0 copy-start.3
  160.6 3.6 %collective-permute-start.13 = (bf16[512,1024]{1,0:T(8,128)(2,1)S(1)}, bf16[512,1024]{1,0:T(8,128)(2,1)}, u32[]{:S(2)}, u32[]{:S(2)}) collective-permute-start(bf16[512,1024]{1,0:T(8,128)(2,1)S(1)} %shard_map.104), channel_id=1, source_target_pairs={{0,32},{32,0},{1,33},{33,1},{2,34},{34,2},{3,35},{35,3},{4,36},{36... | collective-permute-start | bytes 3145736 | tf_op jit(solution)/shard_map/ppermute | solution.py:219
  164.2 2.4 %collective-permute-done.13 = bf16[512,1024]{1,0:T(8,128)(2,1)} collective-permute-done((bf16[512,1024]{1,0:T(8,128)(2,1)S(1)}, bf16[512,1024]{1,0:T(8,128)(2,1)}, u32[]{:S(2)}, u32[]{:S(2)}) %collective-permute-start.13) | collective-permute-done | bytes 1048608 | tf_op jit(solution)/shard_map/ppermute | solution.py:219
  166.6 12.1 %all-to-all-start.4 = ((bf16[64,8,1024]{2,1,0:T(8,128)(2,1)}), bf16[64,8,1024]{2,1,0:T(8,128)(2,1)S(1)}, u32[]{:S(2)}, u32[]{:S(2)}) async-start(bf16[64,8,1024]{2,1,0:T(8,128)(2,1)} %bitcast.23), calls=%async_computation.4 | async-start | bytes 2097152 | tf_op jit(solution)/shard_map/all_to_all | solution.py:215
  178.7 0.1 fusion.21
  178.9 0.1 pad_maximum_fusion.2
  179.0 0.1 pad_maximum_fusion.1
  179.2 0.5 convolution_bitcast_fusion.1
  179.7 26.0 %all-to-all-done.4 = bf16[64,8,1024]{2,1,0:T(8,128)(2,1)S(1)} async-done(((bf16[64,8,1024]{2,1,0:T(8,128)(2,1)}), bf16[64,8,1024]{2,1,0:T(8,128)(2,1)S(1)}, u32[]{:S(2)}, u32[]{:S(2)}) %all-to-all-start.4) | async-done | bytes 1048608 | tf_op jit(solution)/shard_map/all_to_all | solution.py:215
  205.7 0.5 convolution_bitcast_fusion
  206.2 0.7 fusion.24
  (23 shorter events, 0.2 us)
Async XLA Ops:
  0.0 22.7 %copy-start = (bf16[64,1024]{1,0:T(8,128)(2,1)S(1)}, bf16[64,1024]{1,0:T(8,128)(2,1)}, u32[]{:S(2)}) copy-start(bf16[64,1024]{1,0:T(8,128)(2,1)} %param.10) | copy-start | bytes 393220
  1.5 21.2 %all-to-all-start = ((bf16[8,64,256]{2,1,0:T(8,128)(2,1)}), bf16[8,64,256]{2,1,0:T(8,128)(2,1)S(1)}, u32[]{:S(2)}, u32[]{:S(2)}) async-start(bf16[8,64,256]{2,1,0:T(8,128)(2,1)} %broadcast_in_dim.106), calls=%async_computation | async-start | bytes 524288 | tf_op jit(solution)/shard_map/all_to_all | solution.py:44
  25.1 35.6 %all-to-all-start.1 = ((bf16[64,8,1024]{2,1,0:T(8,128)(2,1)}), bf16[64,8,1024]{2,1,0:T(8,128)(2,1)S(1)}, u32[]{:S(2)}, u32[]{:S(2)}) async-start(bf16[64,8,1024]{2,1,0:T(8,128)(2,1)} %fusion.1), calls=%async_computation.1 | async-start | bytes 2097152 | tf_op jit(solution)/shard_map/all_to_all | solution.py:215
  34.3 26.4 %copy-start.2 = (s32[64,64]{1,0:T(8,128)}, s32[64,64]{1,0:T(8,128)S(1)}, u32[]{:S(2)}) copy-start(s32[64,64]{1,0:T(8,128)S(1)} %fusion.14) | copy-start | bytes 49156
  34.3 35.7 %copy-start.6 = (bf16[1024]{0:T(1024)(128)(2,1)S(1)}, bf16[1024]{0:T(1024)(128)(2,1)}, u32[]{:S(2)}) copy-start(bf16[1024]{0:T(1024)(128)(2,1)} %param.14) | copy-start | bytes 6148
  34.7 5.9 %collective-permute-start.4 = (bf16[512,1024]{1,0:T(8,128)(2,1)S(1)}, bf16[512,1024]{1,0:T(8,128)(2,1)}, u32[]{:S(2)}, u32[]{:S(2)}) collective-permute-start(bf16[512,1024]{1,0:T(8,128)(2,1)S(1)} %convolution_convert_fusion), channel_id=1, source_target_pairs={{0,32},{32,0},{1,33},{33,1},{2,34},{34,2},{3,35},{35,3},{4,36},{36... | collective-permute-start | bytes 3145736 | tf_op jit(solution)/shard_map/ppermute | solution.py:219
  60.7 47.3 %all-to-all-start.2 = ((bf16[64,8,1024]{2,1,0:T(8,128)(2,1)}), bf16[64,8,1024]{2,1,0:T(8,128)(2,1)S(1)}, u32[]{:S(2)}, u32[]{:S(2)}) async-start(bf16[64,8,1024]{2,1,0:T(8,128)(2,1)} %bitcast.18), calls=%async_computation.2 | async-start | bytes 2097152 | tf_op jit(solution)/shard_map/all_to_all | solution.py:215
  74.0 13.5 %collective-permute-start = (bf16[128,1664]{1,0:T(8,128)(2,1)S(1)}, bf16[128,1664]{1,0:T(8,128)(2,1)S(1)}, u32[]{:S(2)}, u32[]{:S(2)}) collective-permute-start(bf16[128,1664]{1,0:T(8,128)(2,1)S(1)} %get-tuple-element.20), channel_id=1, source_target_pairs={{0,2},{1,3},{2,0},{3,1},{4,6},{5,7},{6,4},{7,5},{8,10},{9,11},{10,... | collective-permute-start | bytes 1277960 | tf_op jit(solution)/shard_map/ppermute | solution.py:277
  78.7 19.6 %collective-permute-start.1 = (bf16[128,1664]{1,0:T(8,128)(2,1)S(1)}, bf16[128,1664]{1,0:T(8,128)(2,1)S(1)}, u32[]{:S(2)}, u32[]{:S(2)}) collective-permute-start(bf16[128,1664]{1,0:T(8,128)(2,1)S(1)} %get-tuple-element.21), channel_id=1, source_target_pairs={{0,1},{1,2},{2,3},{3,0},{4,5},{5,6},{6,7},{7,4},{8,9},{9,10},{10,1... | collective-permute-start | bytes 1277960 | tf_op jit(solution)/shard_map/ppermute | solution.py:277
  80.9 17.4 %collective-permute-start.2 = (bf16[128,1664]{1,0:T(8,128)(2,1)S(1)}, bf16[128,1664]{1,0:T(8,128)(2,1)S(1)}, u32[]{:S(2)}, u32[]{:S(2)}) collective-permute-start(bf16[128,1664]{1,0:T(8,128)(2,1)S(1)} %get-tuple-element.22), channel_id=1, source_target_pairs={{0,3},{1,0},{2,1},{3,2},{4,7},{5,4},{6,5},{7,6},{8,11},{9,8},{10,9... | collective-permute-start | bytes 1277960 | tf_op jit(solution)/shard_map/ppermute | solution.py:277
  98.6 14.4 %collective-permute-start.6 = (bf16[128,768]{1,0:T(8,128)(2,1)S(1)}, bf16[128,768]{1,0:T(8,128)(2,1)}, u32[]{:S(2)}, u32[]{:S(2)}) collective-permute-start(bf16[128,768]{1,0:T(8,128)(2,1)S(1)} %shard_map.101.rest_0_.refs_0_), channel_id=1, source_target_pairs={{0,3},{1,0},{2,1},{3,2},{4,7},{5,4},{6,5},{7,6},{8,11},{9,8},{10,9... | collective-permute-start | bytes 589832 | tf_op jit(solution)/shard_map/ppermute | solution.py:277
  102.4 14.7 %collective-permute-start.5 = (bf16[128,768]{1,0:T(8,128)(2,1)S(1)}, bf16[128,768]{1,0:T(8,128)(2,1)}, u32[]{:S(2)}, u32[]{:S(2)}) collective-permute-start(bf16[128,768]{1,0:T(8,128)(2,1)S(1)} %shard_map.101.rest_0_.refs_0_), channel_id=1, source_target_pairs={{0,2},{1,3},{2,0},{3,1},{4,6},{5,7},{6,4},{7,5},{8,10},{9,11},{10,... | collective-permute-start | bytes 589832 | tf_op jit(solution)/shard_map/ppermute | solution.py:277
  105.5 14.1 %collective-permute-start.3 = (bf16[128,768]{1,0:T(8,128)(2,1)S(1)}, bf16[128,768]{1,0:T(8,128)(2,1)}, u32[]{:S(2)}, u32[]{:S(2)}) collective-permute-start(bf16[128,768]{1,0:T(8,128)(2,1)S(1)} %shard_map.101.rest_0_.refs_0_), channel_id=1, source_target_pairs={{0,1},{1,2},{2,3},{3,0},{4,5},{5,6},{6,7},{7,4},{8,9},{9,10},{10,1... | collective-permute-start | bytes 589832 | tf_op jit(solution)/shard_map/ppermute | solution.py:277
  108.0 13.5 %copy-start.1 = (bf16[1,768,1024]{2,1,0:T(8,128)(2,1)S(1)}, bf16[1,768,1024]{2,1,0:T(8,128)(2,1)}, u32[]{:S(2)}) copy-start(bf16[1,768,1024]{2,1,0:T(8,128)(2,1)} %param.19) | copy-start | bytes 4718596
  113.1 23.9 %collective-permute-start.9 = (bf16[128,1664]{1,0:T(8,128)(2,1)}, bf16[128,1664]{1,0:T(8,128)(2,1)}, u32[]{:S(2)}, u32[]{:S(2)}) collective-permute-start(bf16[128,1664]{1,0:T(8,128)(2,1)} %get-tuple-element.32), channel_id=1, source_target_pairs={{0,3},{1,0},{2,1},{3,2},{4,7},{5,4},{6,5},{7,6},{8,11},{9,8},{10,9... | collective-permute-start | bytes 1277960 | tf_op jit(solution)/shard_map/ppermute | solution.py:277
  117.1 19.9 %collective-permute-start.8 = (bf16[128,1664]{1,0:T(8,128)(2,1)}, bf16[128,1664]{1,0:T(8,128)(2,1)}, u32[]{:S(2)}, u32[]{:S(2)}) collective-permute-start(bf16[128,1664]{1,0:T(8,128)(2,1)} %get-tuple-element.31), channel_id=1, source_target_pairs={{0,2},{1,3},{2,0},{3,1},{4,6},{5,7},{6,4},{7,5},{8,10},{9,11},{10,... | collective-permute-start | bytes 1277960 | tf_op jit(solution)/shard_map/ppermute | solution.py:277
  119.6 22.1 %collective-permute-start.7 = (bf16[128,1664]{1,0:T(8,128)(2,1)}, bf16[128,1664]{1,0:T(8,128)(2,1)}, u32[]{:S(2)}, u32[]{:S(2)}) collective-permute-start(bf16[128,1664]{1,0:T(8,128)(2,1)} %get-tuple-element.30), channel_id=1, source_target_pairs={{0,1},{1,2},{2,3},{3,0},{4,5},{5,6},{6,7},{7,4},{8,9},{9,10},{10,1... | collective-permute-start | bytes 1277960 | tf_op jit(solution)/shard_map/ppermute | solution.py:277
  124.8 41.7 %all-to-all-start.3 = ((bf16[64,8,1024]{2,1,0:T(8,128)(2,1)}), bf16[64,8,1024]{2,1,0:T(8,128)(2,1)S(1)}, u32[]{:S(2)}, u32[]{:S(2)}) async-start(bf16[64,8,1024]{2,1,0:T(8,128)(2,1)} %bitcast.21), calls=%async_computation.3 | async-start | bytes 2097152 | tf_op jit(solution)/shard_map/all_to_all | solution.py:215
  143.6 13.3 %collective-permute-start.10 = (bf16[128,768]{1,0:T(8,128)(2,1)S(1)}, bf16[128,768]{1,0:T(8,128)(2,1)S(1)}, u32[]{:S(2)}, u32[]{:S(2)}) collective-permute-start(bf16[128,768]{1,0:T(8,128)(2,1)S(1)} %fusion.20.refs_0_), channel_id=1, source_target_pairs={{0,1},{1,2},{2,3},{3,0},{4,5},{5,6},{6,7},{7,4},{8,9},{9,10},{10,1... | collective-permute-start | bytes 589832 | tf_op jit(solution)/shard_map/ppermute | solution.py:277
  145.5 11.4 %collective-permute-start.11 = (bf16[128,768]{1,0:T(8,128)(2,1)S(1)}, bf16[128,768]{1,0:T(8,128)(2,1)S(1)}, u32[]{:S(2)}, u32[]{:S(2)}) collective-permute-start(bf16[128,768]{1,0:T(8,128)(2,1)S(1)} %fusion.20.refs_0_), channel_id=1, source_target_pairs={{0,2},{1,3},{2,0},{3,1},{4,6},{5,7},{6,4},{7,5},{8,10},{9,11},{10,... | collective-permute-start | bytes 589832 | tf_op jit(solution)/shard_map/ppermute | solution.py:277
  148.0 11.2 %collective-permute-start.12 = (bf16[128,768]{1,0:T(8,128)(2,1)S(1)}, bf16[128,768]{1,0:T(8,128)(2,1)S(1)}, u32[]{:S(2)}, u32[]{:S(2)}) collective-permute-start(bf16[128,768]{1,0:T(8,128)(2,1)S(1)} %fusion.20.refs_0_), channel_id=1, source_target_pairs={{0,3},{1,0},{2,1},{3,2},{4,7},{5,4},{6,5},{7,6},{8,11},{9,8},{10,9... | collective-permute-start | bytes 589832 | tf_op jit(solution)/shard_map/ppermute | solution.py:277
  160.6 18.2 %copy-start.4 = (s32[64,8]{0,1:T(8,128)S(1)}, s32[64,8]{0,1:T(8,128)}, u32[]{:S(2)}) copy-start(s32[64,8]{0,1:T(8,128)} %param.15) | copy-start | bytes 6148
  160.6 18.1 %copy-start.5 = (f32[64,8]{0,1:T(8,128)S(1)}, f32[64,8]{0,1:T(8,128)}, u32[]{:S(2)}) copy-start(f32[64,8]{0,1:T(8,128)} %param.16) | copy-start | bytes 6148
  160.6 18.5 %copy-start.3 = (s32[64,64]{1,0:T(8,128)S(1)}, s32[64,64]{1,0:T(8,128)}, u32[]{:S(2)}) copy-start(s32[64,64]{1,0:T(8,128)} %copy-done.2) | copy-start | bytes 49156
  160.6 6.0 %collective-permute-start.13 = (bf16[512,1024]{1,0:T(8,128)(2,1)S(1)}, bf16[512,1024]{1,0:T(8,128)(2,1)}, u32[]{:S(2)}, u32[]{:S(2)}) collective-permute-start(bf16[512,1024]{1,0:T(8,128)(2,1)S(1)} %shard_map.104), channel_id=1, source_target_pairs={{0,32},{32,0},{1,33},{33,1},{2,34},{34,2},{3,35},{35,3},{4,36},{36... | collective-permute-start | bytes 3145736 | tf_op jit(solution)/shard_map/ppermute | solution.py:219
  166.6 39.1 %all-to-all-start.4 = ((bf16[64,8,1024]{2,1,0:T(8,128)(2,1)}), bf16[64,8,1024]{2,1,0:T(8,128)(2,1)S(1)}, u32[]{:S(2)}, u32[]{:S(2)}) async-start(bf16[64,8,1024]{2,1,0:T(8,128)(2,1)} %bitcast.23), calls=%async_computation.4 | async-start | bytes 2097152 | tf_op jit(solution)/shard_map/all_to_all | solution.py:215

commit v4 on v3

--- a/solution.py
+++ b/solution.py
@@ -304,8 +304,9 @@
     near_made = down_product(here, near_pieces, down_rows, [far_parts[0]])
     far_got = fetch_parts(far_parts)
     near_back = exchange(blocks(near_made))
-    far_pieces = spread(silu_product(far_got, hidden_size))
-    far_made = down_product(here, far_pieces, down_rows, [])
+    far_hidden = silu_product(far_got, hidden_size)
+    far_hidden = lax.all_gather(far_hidden, "tensor", axis=0, tiled=True)
+    far_made = down_product(here, [far_hidden], down_rows, [])
     far_back = exchange(blocks(swap(far_made)))
 
     mixed = attended.astype(F32) + combine(mix_near, near_back) + combine(mix_far, far_back)

time: 211 us -> 208 us (0.986)
  blocking collectives: 0 us -> 11.4 us
  waiting for transfers between devices: 83.6 us -> 76.6 us
  starting transfers between devices: 97.9 us -> 91.3 us
    all_gather x0 -> x1, blocking collectives: none -> 11.4 us  [per_device(): far_hidden = lax.all_gather(far_hidden, 'tensor', axis=0, tiled=True)]
    ppermute x12 -> x9, starting transfers between devices: 37.5 us -> 28.9 us  [fetch_parts(): lax.ppermute(parts[step], 'tensor', ring(size, step))]
    ppermute x12 -> x9, waiting for transfers between devices: 24.7 us -> 17.7 us  [fetch_parts(): lax.ppermute(parts[step], 'tensor', ring(size, step))]
  transfers between devices with their start and end apart: 19 -> 16, of which waited for: 10 -> 8; matrix products, arithmetic and copies ran while one was open for 3% -> 3% of each run, Pallas kernels for 7% -> 7%
where the time goes in v4:
time: 208 us; the launch traced here: 205 us
  starting transfers between devices  91.3 us (44%)
  waiting for transfers between devices  76.6 us (37%)
  Pallas kernels  14.1 us (7%)
  blocking collectives  11.4 us (5%)
  other arithmetic  6.57 us (3%)
  matrix products  3.63 us (2%)
    all_to_all x4, waiting for transfers between devices, exchange(): return lax.all_to_all(block, GROUP, split_axis=0, concat_axis=0, tiled=True)  46.2 us
    all_to_all x4, starting transfers between devices, exchange(): return lax.all_to_all(block, GROUP, split_axis=0, concat_axis=0, tiled=True)  42.5 us
    ppermute x9, starting transfers between devices, fetch_parts(): lax.ppermute(parts[step], 'tensor', ring(size, step))  28.9 us
    ppermute x9, waiting for transfers between devices, fetch_parts(): lax.ppermute(parts[step], 'tensor', ring(size, step))  17.7 us
    all_gather x1, blocking collectives, per_device(): far_hidden = lax.all_gather(far_hidden, 'tensor', axis=0, tiled=True)  11.4 us
    all_to_all x1, starting transfers between devices, attention(): lax.all_to_all(copies, 'expert', split_axis=0, concat_axis=0, tiled=True)  10.9 us
    pallas_call x2, Pallas kernels, gate_up(): pl.pallas_call(functools.partial(gate_up_kernel, size=size, waits=len(aft...  9.04 us
    ppermute x2, starting transfers between devices, swap(): return lax.ppermute(block, 'core', [(0, 1), (1, 0)])  8.97 us
  transfers between devices with their start and end apart: 16, of which 8 were waited for; matrix products, arithmetic and copies ran while one was open for 3% of the time, Pallas kernels for 7%

profile of v4, /device:TPU:1, one launch (start us, length us, event | category | flops | bytes accessed | tf_op | source)
XLA Modules:
  0.0 204.7 jit_solution(11963765265148898476)
XLA Ops:
  0.0 0.8 pad_maximum_fusion
  0.8 0.7 broadcast_in_dim.106
  1.5 10.9 %all-to-all-start = ((bf16[8,64,256]{2,1,0:T(8,128)(2,1)}), bf16[8,64,256]{2,1,0:T(8,128)(2,1)S(1)}, u32[]{:S(2)}, u32[]{:S(2)}) async-start(bf16[8,64,256]{2,1,0:T(8,128)(2,1)} %broadcast_in_dim.106), calls=%async_computation | async-start | bytes 524288 | tf_op jit(solution)/shard_map/all_to_all | solution.py:44
  12.4 0.7 add_bitcast_fusion.1
  13.0 0.8 compare_reduce_fusion
  13.9 0.7 select_reduce_fusion.1
  14.6 0.1 iota_compare_fusion.2
  14.7 0.1 fusion.15
  14.8 7.9 %all-to-all-done = bf16[8,64,256]{2,1,0:T(8,128)(2,1)S(1)} async-done(((bf16[8,64,256]{2,1,0:T(8,128)(2,1)}), bf16[8,64,256]{2,1,0:T(8,128)(2,1)S(1)}, u32[]{:S(2)}, u32[]{:S(2)}) %all-to-all-start) | async-done | bytes 262176 | tf_op jit(solution)/shard_map/all_to_all | solution.py:44
  22.7 0.3 fusion.10
  23.0 0.4 fusion.50
  23.4 0.3 fusion.13
  23.7 1.4 fusion.1
  25.1 9.0 %all-to-all-start.1 = ((bf16[64,8,1024]{2,1,0:T(8,128)(2,1)}), bf16[64,8,1024]{2,1,0:T(8,128)(2,1)S(1)}, u32[]{:S(2)}, u32[]{:S(2)}) async-start(bf16[64,8,1024]{2,1,0:T(8,128)(2,1)} %fusion.1), calls=%async_computation.1 | async-start | bytes 2097152 | tf_op jit(solution)/shard_map/all_to_all | solution.py:215
  34.2 0.1 fusion.14
  34.3 0.4 convolution_convert_fusion
  34.8 3.4 %collective-permute-start.4 = (bf16[512,1024]{1,0:T(8,128)(2,1)S(1)}, bf16[512,1024]{1,0:T(8,128)(2,1)}, u32[]{:S(2)}, u32[]{:S(2)}) collective-permute-start(bf16[512,1024]{1,0:T(8,128)(2,1)S(1)} %convolution_convert_fusion), channel_id=1, source_target_pairs={{0,32},{32,0},{1,33},{33,1},{2,34},{34,2},{3,35},{35,3},{4,36},{36... | collective-permute-start | bytes 3145736 | tf_op jit(solution)/shard_map/ppermute | solution.py:219
  38.2 2.4 %collective-permute-done.4 = bf16[512,1024]{1,0:T(8,128)(2,1)} collective-permute-done((bf16[512,1024]{1,0:T(8,128)(2,1)S(1)}, bf16[512,1024]{1,0:T(8,128)(2,1)}, u32[]{:S(2)}, u32[]{:S(2)}) %collective-permute-start.4) | collective-permute-done | bytes 1048608 | tf_op jit(solution)/shard_map/ppermute | solution.py:219
  40.6 20.2 %all-to-all-done.1 = bf16[64,8,1024]{2,1,0:T(8,128)(2,1)S(1)} async-done(((bf16[64,8,1024]{2,1,0:T(8,128)(2,1)}), bf16[64,8,1024]{2,1,0:T(8,128)(2,1)S(1)}, u32[]{:S(2)}, u32[]{:S(2)}) %all-to-all-start.1) | async-done | bytes 1048608 | tf_op jit(solution)/shard_map/all_to_all | solution.py:215
  60.8 9.3 %all-to-all-start.2 = ((bf16[64,8,1024]{2,1,0:T(8,128)(2,1)}), bf16[64,8,1024]{2,1,0:T(8,128)(2,1)S(1)}, u32[]{:S(2)}, u32[]{:S(2)}) async-start(bf16[64,8,1024]{2,1,0:T(8,128)(2,1)} %bitcast.18), calls=%async_computation.2 | async-start | bytes 2097152 | tf_op jit(solution)/shard_map/all_to_all | solution.py:215
  70.1 4.0 %shard_map.100 = (bf16[128,1664]{1,0:T(8,128)(2,1)S(1)}, bf16[128,1664]{1,0:T(8,128)(2,1)S(1)}, bf16[128,1664]{1,0:T(8,128)(2,1)S(1)}, bf16[128,1664]{1,0:T(8,128)(2,1)S(1)}) custom-call(s32[1]{0:T(128)} %bitcast.11.here, bf16[512,1024]{1,0:T(8,128)(2,1)S(1)} %bitcast.69, bf16[1,1024]{1,0:T(2,128)(2,1)S(1)} %broadcast_in_dim.115.gain, ...), custom_call_target="tpu_custom_call" | custom-call | flops 1610612736 | bytes 5898240 | tf_op jit(solution)/shard_map/pallas_call | solution.py:107
  74.1 4.6 %collective-permute-start = (bf16[128,1664]{1,0:T(8,128)(2,1)S(1)}, bf16[128,1664]{1,0:T(8,128)(2,1)S(1)}, u32[]{:S(2)}, u32[]{:S(2)}) collective-permute-start(bf16[128,1664]{1,0:T(8,128)(2,1)S(1)} %get-tuple-element.20), channel_id=1, source_target_pairs={{0,2},{1,3},{2,0},{3,1},{4,6},{5,7},{6,4},{7,5},{8,10},{9,11},{10,... | collective-permute-start | bytes 1277960 | tf_op jit(solution)/shard_map/ppermute | solution.py:277
  78.7 2.2 %collective-permute-start.1 = (bf16[128,1664]{1,0:T(8,128)(2,1)S(1)}, bf16[128,1664]{1,0:T(8,128)(2,1)S(1)}, u32[]{:S(2)}, u32[]{:S(2)}) collective-permute-start(bf16[128,1664]{1,0:T(8,128)(2,1)S(1)} %get-tuple-element.21), channel_id=1, source_target_pairs={{0,1},{1,2},{2,3},{3,0},{4,5},{5,6},{6,7},{7,4},{8,9},{9,10},{10,1... | collective-permute-start | bytes 1277960 | tf_op jit(solution)/shard_map/ppermute | solution.py:277
  80.9 4.3 %collective-permute-start.2 = (bf16[128,1664]{1,0:T(8,128)(2,1)S(1)}, bf16[128,1664]{1,0:T(8,128)(2,1)S(1)}, u32[]{:S(2)}, u32[]{:S(2)}) collective-permute-start(bf16[128,1664]{1,0:T(8,128)(2,1)S(1)} %get-tuple-element.22), channel_id=1, source_target_pairs={{0,3},{1,0},{2,1},{3,2},{4,7},{5,4},{6,5},{7,6},{8,11},{9,8},{10,9... | collective-permute-start | bytes 1277960 | tf_op jit(solution)/shard_map/ppermute | solution.py:277
  85.2 2.4 %collective-permute-done = bf16[128,1664]{1,0:T(8,128)(2,1)S(1)} collective-permute-done((bf16[128,1664]{1,0:T(8,128)(2,1)S(1)}, bf16[128,1664]{1,0:T(8,128)(2,1)S(1)}, u32[]{:S(2)}, u32[]{:S(2)}) %collective-permute-start) | collective-permute-done | bytes 426016 | tf_op jit(solution)/shard_map/ppermute | solution.py:277
  87.6 0.1 convert_add_fusion.1.refs_0_
  87.7 10.7 %collective-permute-done.1.refs_1_ = bf16[128,1664]{1,0:T(8,128)(2,1)S(1)} collective-permute-done((bf16[128,1664]{1,0:T(8,128)(2,1)S(1)}, bf16[128,1664]{1,0:T(8,128)(2,1)S(1)}, u32[]{:S(2)}, u32[]{:S(2)}) %collective-permute-start.1) | collective-permute-done | bytes 426016 | tf_op jit(solution)/shard_map/ppermute | solution.py:277
  98.3 0.0 collective-permute-done.2.refs_2_
  98.3 0.3 shard_map.101.rest_0_.refs_0_
  98.7 3.7 %collective-permute-start.6 = (bf16[128,768]{1,0:T(8,128)(2,1)S(1)}, bf16[128,768]{1,0:T(8,128)(2,1)}, u32[]{:S(2)}, u32[]{:S(2)}) collective-permute-start(bf16[128,768]{1,0:T(8,128)(2,1)S(1)} %shard_map.101.rest_0_.refs_0_), channel_id=1, source_target_pairs={{0,3},{1,0},{2,1},{3,2},{4,7},{5,4},{6,5},{7,6},{8,11},{9,8},{10,9... | collective-permute-start | bytes 589832 | tf_op jit(solution)/shard_map/ppermute | solution.py:277
  102.4 3.1 %collective-permute-start.5 = (bf16[128,768]{1,0:T(8,128)(2,1)S(1)}, bf16[128,768]{1,0:T(8,128)(2,1)}, u32[]{:S(2)}, u32[]{:S(2)}) collective-permute-start(bf16[128,768]{1,0:T(8,128)(2,1)S(1)} %shard_map.101.rest_0_.refs_0_), channel_id=1, source_target_pairs={{0,2},{1,3},{2,0},{3,1},{4,6},{5,7},{6,4},{7,5},{8,10},{9,11},{10,... | collective-permute-start | bytes 589832 | tf_op jit(solution)/shard_map/ppermute | solution.py:277
  105.5 2.5 %collective-permute-start.3 = (bf16[128,768]{1,0:T(8,128)(2,1)S(1)}, bf16[128,768]{1,0:T(8,128)(2,1)}, u32[]{:S(2)}, u32[]{:S(2)}) collective-permute-start(bf16[128,768]{1,0:T(8,128)(2,1)S(1)} %shard_map.101.rest_0_.refs_0_), channel_id=1, source_target_pairs={{0,1},{1,2},{2,3},{3,0},{4,5},{5,6},{6,7},{7,4},{8,9},{9,10},{10,1... | collective-permute-start | bytes 589832 | tf_op jit(solution)/shard_map/ppermute | solution.py:277
  108.0 0.0 all-to-all-done.2
  108.0 0.0 copy-start.1
  108.0 5.0 %shard_map.102 = (bf16[128,1664]{1,0:T(8,128)(2,1)S(1)}, bf16[128,1664]{1,0:T(8,128)(2,1)}, bf16[128,1664]{1,0:T(8,128)(2,1)}, bf16[128,1664]{1,0:T(8,128)(2,1)}) custom-call(s32[1]{0:T(128)} %bitcast.11.here, bf16[512,1024]{1,0:T(8,128)(2,1)S(1)} %bitcast.68, bf16[1,1024]{1,0:T(2,128)(2,1)S(1)} %broadcast_in_dim.115.gain, bf16[1024,768]{1,0:T(8,128)(2,1)} %bitcast.77, ...), custom_call_target="tpu_custom_call" | custom-call | flops 1610612736 | bytes 5898240 | tf_op jit(solution)/shard_map/pallas_call | solution.py:107
  113.1 0.0 collective-permute-done.6.refs_3_
  113.1 4.0 %collective-permute-start.9 = (bf16[128,1664]{1,0:T(8,128)(2,1)}, bf16[128,1664]{1,0:T(8,128)(2,1)}, u32[]{:S(2)}, u32[]{:S(2)}) collective-permute-start(bf16[128,1664]{1,0:T(8,128)(2,1)} %get-tuple-element.32), channel_id=1, source_target_pairs={{0,3},{1,0},{2,1},{3,2},{4,7},{5,4},{6,5},{7,6},{8,11},{9,8},{10,9... | collective-permute-start | bytes 1277960 | tf_op jit(solution)/shard_map/ppermute | solution.py:277
  117.1 0.0 collective-permute-done.5.refs_2_
  117.1 2.5 %collective-permute-start.8 = (bf16[128,1664]{1,0:T(8,128)(2,1)}, bf16[128,1664]{1,0:T(8,128)(2,1)}, u32[]{:S(2)}, u32[]{:S(2)}) collective-permute-start(bf16[128,1664]{1,0:T(8,128)(2,1)} %get-tuple-element.31), channel_id=1, source_target_pairs={{0,2},{1,3},{2,0},{3,1},{4,6},{5,7},{6,4},{7,5},{8,10},{9,11},{10,... | collective-permute-start | bytes 1277960 | tf_op jit(solution)/shard_map/ppermute | solution.py:277
  119.6 0.0 collective-permute-done.3.refs_1_
  119.6 1.9 collective-permute-start.7
  121.6 3.3 %shard_map.103 = bf16[512,1024]{1,0:T(8,128)(2,1)} custom-call(s32[1]{0:T(128)} %bitcast.11.here, bf16[128,768]{1,0:T(8,128)(2,1)S(1)} %shard_map.101.rest_0_.refs_0_, bf16[128,768]{1,0:T(8,128)(2,1)} %collective-permute-done.3.refs_1_, bf16[128,768]{1,0:T(8,128)(2,1)} %collective-permute-done.5.refs_2_, bf16[128,768]{1,0:T(8,128)(2,1)} %collective-permute-done.6.refs_3_, ...), custom_call_target="tpu_custom_call" | custom-call | flops 805306368 | bytes 3407872 | tf_op jit(solution)/shard_map/pallas_call | solution.py:148
  124.9 12.1 %all-to-all-start.3 = ((bf16[64,8,1024]{2,1,0:T(8,128)(2,1)}), bf16[64,8,1024]{2,1,0:T(8,128)(2,1)S(1)}, u32[]{:S(2)}, u32[]{:S(2)}) async-start(bf16[64,8,1024]{2,1,0:T(8,128)(2,1)} %bitcast.21), calls=%async_computation.3 | async-start | bytes 2097152 | tf_op jit(solution)/shard_map/all_to_all | solution.py:215
  137.0 0.0 collective-permute-done.8
  137.0 4.7 %collective-permute-done.7 = bf16[128,1664]{1,0:T(8,128)(2,1)} collective-permute-done((bf16[128,1664]{1,0:T(8,128)(2,1)}, bf16[128,1664]{1,0:T(8,128)(2,1)}, u32[]{:S(2)}, u32[]{:S(2)}) %collective-permute-start.7) | collective-permute-done | bytes 426016 | tf_op jit(solution)/shard_map/ppermute | solution.py:277
  141.7 1.5 convert_add_fusion
  143.2 0.2 fusion.41
  143.4 0.2 fusion.20
  143.6 11.4 %all_gather.3.refs_0_ = bf16[512,768]{1,0:T(8,128)(2,1)S(1)} all-gather(bf16[128,768]{1,0:T(8,128)(2,1)S(1)} %fusion.20), channel_id=1, replica_groups=mesh['y'=8,'core'=2,'expert'=8,'tensor'=4] {'tensor'}, dimensions={0}, use_global_device_ids=true | all-gather | bytes 983040 | tf_op jit(solution)/shard_map/all_gather | solution.py:308
  155.0 1.4 shard_map.104
  156.4 0.0 copy-start.4
  156.4 0.0 copy-start.5
  156.4 0.0 copy-start.3
  156.4 5.5 %collective-permute-start.10 = (bf16[512,1024]{1,0:T(8,128)(2,1)S(1)}, bf16[512,1024]{1,0:T(8,128)(2,1)}, u32[]{:S(2)}, u32[]{:S(2)}) collective-permute-start(bf16[512,1024]{1,0:T(8,128)(2,1)S(1)} %shard_map.104), channel_id=1, source_target_pairs={{0,32},{32,0},{1,33},{33,1},{2,34},{34,2},{3,35},{35,3},{4,36},{36... | collective-permute-start | bytes 3145736 | tf_op jit(solution)/shard_map/ppermute | solution.py:219
  162.0 2.4 %collective-permute-done.10 = bf16[512,1024]{1,0:T(8,128)(2,1)} collective-permute-done((bf16[512,1024]{1,0:T(8,128)(2,1)S(1)}, bf16[512,1024]{1,0:T(8,128)(2,1)}, u32[]{:S(2)}, u32[]{:S(2)}) %collective-permute-start.10) | collective-permute-done | bytes 1048608 | tf_op jit(solution)/shard_map/ppermute | solution.py:219
  164.4 0.0 all-to-all-done.3
  164.4 12.1 %all-to-all-start.4 = ((bf16[64,8,1024]{2,1,0:T(8,128)(2,1)}), bf16[64,8,1024]{2,1,0:T(8,128)(2,1)S(1)}, u32[]{:S(2)}, u32[]{:S(2)}) async-start(bf16[64,8,1024]{2,1,0:T(8,128)(2,1)} %bitcast.23), calls=%async_computation.4 | async-start | bytes 2097152 | tf_op jit(solution)/shard_map/all_to_all | solution.py:215
  176.5 0.1 fusion.21
  176.7 0.1 pad_maximum_fusion.2
  176.8 0.1 pad_maximum_fusion.1
  177.0 0.5 convolution_bitcast_fusion.1
  177.4 26.0 %all-to-all-done.4 = bf16[64,8,1024]{2,1,0:T(8,128)(2,1)S(1)} async-done(((bf16[64,8,1024]{2,1,0:T(8,128)(2,1)}), bf16[64,8,1024]{2,1,0:T(8,128)(2,1)S(1)}, u32[]{:S(2)}, u32[]{:S(2)}) %all-to-all-start.4) | async-done | bytes 1048608 | tf_op jit(solution)/shard_map/all_to_all | solution.py:215
  203.5 0.5 convolution_bitcast_fusion
  203.9 0.7 fusion.24
  (18 shorter events, 0.1 us)
Async XLA Ops:
  0.0 22.7 %copy-start = (bf16[64,1024]{1,0:T(8,128)(2,1)S(1)}, bf16[64,1024]{1,0:T(8,128)(2,1)}, u32[]{:S(2)}) copy-start(bf16[64,1024]{1,0:T(8,128)(2,1)} %param.10) | copy-start | bytes 393220
  1.5 21.2 %all-to-all-start = ((bf16[8,64,256]{2,1,0:T(8,128)(2,1)}), bf16[8,64,256]{2,1,0:T(8,128)(2,1)S(1)}, u32[]{:S(2)}, u32[]{:S(2)}) async-start(bf16[8,64,256]{2,1,0:T(8,128)(2,1)} %broadcast_in_dim.106), calls=%async_computation | async-start | bytes 524288 | tf_op jit(solution)/shard_map/all_to_all | solution.py:44
  25.1 35.6 %all-to-all-start.1 = ((bf16[64,8,1024]{2,1,0:T(8,128)(2,1)}), bf16[64,8,1024]{2,1,0:T(8,128)(2,1)S(1)}, u32[]{:S(2)}, u32[]{:S(2)}) async-start(bf16[64,8,1024]{2,1,0:T(8,128)(2,1)} %fusion.1), calls=%async_computation.1 | async-start | bytes 2097152 | tf_op jit(solution)/shard_map/all_to_all | solution.py:215
  34.3 26.4 %copy-start.2 = (s32[64,64]{1,0:T(8,128)}, s32[64,64]{1,0:T(8,128)S(1)}, u32[]{:S(2)}) copy-start(s32[64,64]{1,0:T(8,128)S(1)} %fusion.14) | copy-start | bytes 49156
  34.3 35.7 %copy-start.6 = (bf16[1024]{0:T(1024)(128)(2,1)S(1)}, bf16[1024]{0:T(1024)(128)(2,1)}, u32[]{:S(2)}) copy-start(bf16[1024]{0:T(1024)(128)(2,1)} %param.14) | copy-start | bytes 6148
  34.8 5.8 %collective-permute-start.4 = (bf16[512,1024]{1,0:T(8,128)(2,1)S(1)}, bf16[512,1024]{1,0:T(8,128)(2,1)}, u32[]{:S(2)}, u32[]{:S(2)}) collective-permute-start(bf16[512,1024]{1,0:T(8,128)(2,1)S(1)} %convolution_convert_fusion), channel_id=1, source_target_pairs={{0,32},{32,0},{1,33},{33,1},{2,34},{34,2},{3,35},{35,3},{4,36},{36... | collective-permute-start | bytes 3145736 | tf_op jit(solution)/shard_map/ppermute | solution.py:219
  60.8 47.3 %all-to-all-start.2 = ((bf16[64,8,1024]{2,1,0:T(8,128)(2,1)}), bf16[64,8,1024]{2,1,0:T(8,128)(2,1)S(1)}, u32[]{:S(2)}, u32[]{:S(2)}) async-start(bf16[64,8,1024]{2,1,0:T(8,128)(2,1)} %bitcast.18), calls=%async_computation.2 | async-start | bytes 2097152 | tf_op jit(solution)/shard_map/all_to_all | solution.py:215
  74.1 13.5 %collective-permute-start = (bf16[128,1664]{1,0:T(8,128)(2,1)S(1)}, bf16[128,1664]{1,0:T(8,128)(2,1)S(1)}, u32[]{:S(2)}, u32[]{:S(2)}) collective-permute-start(bf16[128,1664]{1,0:T(8,128)(2,1)S(1)} %get-tuple-element.20), channel_id=1, source_target_pairs={{0,2},{1,3},{2,0},{3,1},{4,6},{5,7},{6,4},{7,5},{8,10},{9,11},{10,... | collective-permute-start | bytes 1277960 | tf_op jit(solution)/shard_map/ppermute | solution.py:277
  78.7 19.6 %collective-permute-start.1 = (bf16[128,1664]{1,0:T(8,128)(2,1)S(1)}, bf16[128,1664]{1,0:T(8,128)(2,1)S(1)}, u32[]{:S(2)}, u32[]{:S(2)}) collective-permute-start(bf16[128,1664]{1,0:T(8,128)(2,1)S(1)} %get-tuple-element.21), channel_id=1, source_target_pairs={{0,1},{1,2},{2,3},{3,0},{4,5},{5,6},{6,7},{7,4},{8,9},{9,10},{10,1... | collective-permute-start | bytes 1277960 | tf_op jit(solution)/shard_map/ppermute | solution.py:277
  80.9 17.4 %collective-permute-start.2 = (bf16[128,1664]{1,0:T(8,128)(2,1)S(1)}, bf16[128,1664]{1,0:T(8,128)(2,1)S(1)}, u32[]{:S(2)}, u32[]{:S(2)}) collective-permute-start(bf16[128,1664]{1,0:T(8,128)(2,1)S(1)} %get-tuple-element.22), channel_id=1, source_target_pairs={{0,3},{1,0},{2,1},{3,2},{4,7},{5,4},{6,5},{7,6},{8,11},{9,8},{10,9... | collective-permute-start | bytes 1277960 | tf_op jit(solution)/shard_map/ppermute | solution.py:277
  98.7 14.4 %collective-permute-start.6 = (bf16[128,768]{1,0:T(8,128)(2,1)S(1)}, bf16[128,768]{1,0:T(8,128)(2,1)}, u32[]{:S(2)}, u32[]{:S(2)}) collective-permute-start(bf16[128,768]{1,0:T(8,128)(2,1)S(1)} %shard_map.101.rest_0_.refs_0_), channel_id=1, source_target_pairs={{0,3},{1,0},{2,1},{3,2},{4,7},{5,4},{6,5},{7,6},{8,11},{9,8},{10,9... | collective-permute-start | bytes 589832 | tf_op jit(solution)/shard_map/ppermute | solution.py:277
  102.4 14.7 %collective-permute-start.5 = (bf16[128,768]{1,0:T(8,128)(2,1)S(1)}, bf16[128,768]{1,0:T(8,128)(2,1)}, u32[]{:S(2)}, u32[]{:S(2)}) collective-permute-start(bf16[128,768]{1,0:T(8,128)(2,1)S(1)} %shard_map.101.rest_0_.refs_0_), channel_id=1, source_target_pairs={{0,2},{1,3},{2,0},{3,1},{4,6},{5,7},{6,4},{7,5},{8,10},{9,11},{10,... | collective-permute-start | bytes 589832 | tf_op jit(solution)/shard_map/ppermute | solution.py:277
  105.5 14.1 %collective-permute-start.3 = (bf16[128,768]{1,0:T(8,128)(2,1)S(1)}, bf16[128,768]{1,0:T(8,128)(2,1)}, u32[]{:S(2)}, u32[]{:S(2)}) collective-permute-start(bf16[128,768]{1,0:T(8,128)(2,1)S(1)} %shard_map.101.rest_0_.refs_0_), channel_id=1, source_target_pairs={{0,1},{1,2},{2,3},{3,0},{4,5},{5,6},{6,7},{7,4},{8,9},{9,10},{10,1... | collective-permute-start | bytes 589832 | tf_op jit(solution)/shard_map/ppermute | solution.py:277
  108.0 13.5 %copy-start.1 = (bf16[1,768,1024]{2,1,0:T(8,128)(2,1)S(1)}, bf16[1,768,1024]{2,1,0:T(8,128)(2,1)}, u32[]{:S(2)}) copy-start(bf16[1,768,1024]{2,1,0:T(8,128)(2,1)} %param.19) | copy-start | bytes 4718596
  113.1 23.9 %collective-permute-start.9 = (bf16[128,1664]{1,0:T(8,128)(2,1)}, bf16[128,1664]{1,0:T(8,128)(2,1)}, u32[]{:S(2)}, u32[]{:S(2)}) collective-permute-start(bf16[128,1664]{1,0:T(8,128)(2,1)} %get-tuple-element.32), channel_id=1, source_target_pairs={{0,3},{1,0},{2,1},{3,2},{4,7},{5,4},{6,5},{7,6},{8,11},{9,8},{10,9... | collective-permute-start | bytes 1277960 | tf_op jit(solution)/shard_map/ppermute | solution.py:277
  117.1 19.9 %collective-permute-start.8 = (bf16[128,1664]{1,0:T(8,128)(2,1)}, bf16[128,1664]{1,0:T(8,128)(2,1)}, u32[]{:S(2)}, u32[]{:S(2)}) collective-permute-start(bf16[128,1664]{1,0:T(8,128)(2,1)} %get-tuple-element.31), channel_id=1, source_target_pairs={{0,2},{1,3},{2,0},{3,1},{4,6},{5,7},{6,4},{7,5},{8,10},{9,11},{10,... | collective-permute-start | bytes 1277960 | tf_op jit(solution)/shard_map/ppermute | solution.py:277
  119.6 22.1 %collective-permute-start.7 = (bf16[128,1664]{1,0:T(8,128)(2,1)}, bf16[128,1664]{1,0:T(8,128)(2,1)}, u32[]{:S(2)}, u32[]{:S(2)}) collective-permute-start(bf16[128,1664]{1,0:T(8,128)(2,1)} %get-tuple-element.30), channel_id=1, source_target_pairs={{0,1},{1,2},{2,3},{3,0},{4,5},{5,6},{6,7},{7,4},{8,9},{9,10},{10,1... | collective-permute-start | bytes 1277960 | tf_op jit(solution)/shard_map/ppermute | solution.py:277
  124.9 39.5 %all-to-all-start.3 = ((bf16[64,8,1024]{2,1,0:T(8,128)(2,1)}), bf16[64,8,1024]{2,1,0:T(8,128)(2,1)S(1)}, u32[]{:S(2)}, u32[]{:S(2)}) async-start(bf16[64,8,1024]{2,1,0:T(8,128)(2,1)} %bitcast.21), calls=%async_computation.3 | async-start | bytes 2097152 | tf_op jit(solution)/shard_map/all_to_all | solution.py:215
  156.4 20.1 %copy-start.4 = (s32[64,8]{0,1:T(8,128)S(1)}, s32[64,8]{0,1:T(8,128)}, u32[]{:S(2)}) copy-start(s32[64,8]{0,1:T(8,128)} %param.15) | copy-start | bytes 6148
  156.4 20.1 %copy-start.5 = (f32[64,8]{0,1:T(8,128)S(1)}, f32[64,8]{0,1:T(8,128)}, u32[]{:S(2)}) copy-start(f32[64,8]{0,1:T(8,128)} %param.16) | copy-start | bytes 6148
  156.4 20.5 %copy-start.3 = (s32[64,64]{1,0:T(8,128)S(1)}, s32[64,64]{1,0:T(8,128)}, u32[]{:S(2)}) copy-start(s32[64,64]{1,0:T(8,128)} %copy-done.2) | copy-start | bytes 49156
  156.4 7.9 %collective-permute-start.10 = (bf16[512,1024]{1,0:T(8,128)(2,1)S(1)}, bf16[512,1024]{1,0:T(8,128)(2,1)}, u32[]{:S(2)}, u32[]{:S(2)}) collective-permute-start(bf16[512,1024]{1,0:T(8,128)(2,1)S(1)} %shard_map.104), channel_id=1, source_target_pairs={{0,32},{32,0},{1,33},{33,1},{2,34},{34,2},{3,35},{35,3},{4,36},{36... | collective-permute-start | bytes 3145736 | tf_op jit(solution)/shard_map/ppermute | solution.py:219
  164.4 39.1 %all-to-all-start.4 = ((bf16[64,8,1024]{2,1,0:T(8,128)(2,1)}), bf16[64,8,1024]{2,1,0:T(8,128)(2,1)S(1)}, u32[]{:S(2)}, u32[]{:S(2)}) async-start(bf16[64,8,1024]{2,1,0:T(8,128)(2,1)} %bitcast.23), calls=%async_computation.4 | async-start | bytes 2097152 | tf_op jit(solution)/shard_map/all_to_all | solution.py:215

commit v5 on v4

--- a/solution.py
+++ b/solution.py
@@ -303,6 +303,7 @@
         )
     near_made = down_product(here, near_pieces, down_rows, [far_parts[0]])
     far_got = fetch_parts(far_parts)
+    far_got = [far_got[0].astype(F32) + far_got.pop(size // 2).astype(F32)] + far_got[1:]
     near_back = exchange(blocks(near_made))
     far_hidden = silu_product(far_got, hidden_size)
     far_hidden = lax.all_gather(far_hidden, "tensor", axis=0, tiled=True)

time: 208 us -> 207 us (level)
  waiting for transfers between devices: 76.6 us -> 72.4 us
  starting transfers between devices: 91.3 us -> 93.8 us
    ppermute x9, waiting for transfers between devices: 17.7 us -> 13.2 us  [fetch_parts(): lax.ppermute(parts[step], 'tensor', ring(size, step))]
    ppermute x2, starting transfers between devices: 8.97 us -> 11.3 us  [swap(): return lax.ppermute(block, 'core', [(0, 1), (1, 0)])]
  transfers between devices with their start and end apart: 16 -> 16, of which waited for: 8 -> 9; matrix products, arithmetic and copies ran while one was open for 3% -> 3% of each run, Pallas kernels for 7% -> 7%
where the time goes in v5:
time: 207 us; the launch traced here: 203 us
  starting transfers between devices  93.8 us (45%)
  waiting for transfers between devices  72.4 us (35%)
  Pallas kernels  14.1 us (7%)
  blocking collectives  11.3 us (5%)
  other arithmetic  6.57 us (3%)
  matrix products  3.63 us (2%)
    all_to_all x4, waiting for transfers between devices, exchange(): return lax.all_to_all(block, GROUP, split_axis=0, concat_axis=0, tiled=True)  46.5 us
    all_to_all x4, starting transfers between devices, exchange(): return lax.all_to_all(block, GROUP, split_axis=0, concat_axis=0, tiled=True)  42.2 us
    ppermute x9, starting transfers between devices, fetch_parts(): lax.ppermute(parts[step], 'tensor', ring(size, step))  29.5 us
    ppermute x9, waiting for transfers between devices, fetch_parts(): lax.ppermute(parts[step], 'tensor', ring(size, step))  13.2 us
    ppermute x2, starting transfers between devices, swap(): return lax.ppermute(block, 'core', [(0, 1), (1, 0)])  11.3 us
    all_gather x1, blocking collectives, per_device(): far_hidden = lax.all_gather(far_hidden, 'tensor', axis=0, tiled=True)  11.3 us
    all_to_all x1, starting transfers between devices, attention(): lax.all_to_all(copies, 'expert', split_axis=0, concat_axis=0, tiled=True)  10.9 us
    pallas_call x2, Pallas kernels, gate_up(): pl.pallas_call(functools.partial(gate_up_kernel, size=size, waits=len(aft...  9.04 us
  transfers between devices with their start and end apart: 16, of which 9 were waited for; matrix products, arithmetic and copies ran while one was open for 3% of the time, Pallas kernels for 7%

profile of v5, /device:TPU:1, one launch (start us, length us, event | category | flops | bytes accessed | tf_op | source)
XLA Modules:
  0.0 202.9 jit_solution(10115298176827201359)
XLA Ops:
  0.0 0.8 pad_maximum_fusion
  0.8 0.7 broadcast_in_dim.106
  1.5 10.9 %all-to-all-start = ((bf16[8,64,256]{2,1,0:T(8,128)(2,1)}), bf16[8,64,256]{2,1,0:T(8,128)(2,1)S(1)}, u32[]{:S(2)}, u32[]{:S(2)}) async-start(bf16[8,64,256]{2,1,0:T(8,128)(2,1)} %broadcast_in_dim.106), calls=%async_computation | async-start | bytes 524288 | tf_op jit(solution)/shard_map/all_to_all | solution.py:44
  12.4 0.7 add_bitcast_fusion.1
  13.0 0.8 compare_reduce_fusion
  13.9 0.7 select_reduce_fusion.1
  14.6 0.1 iota_compare_fusion.2
  14.7 0.1 fusion.15
  14.8 7.9 %all-to-all-done = bf16[8,64,256]{2,1,0:T(8,128)(2,1)S(1)} async-done(((bf16[8,64,256]{2,1,0:T(8,128)(2,1)}), bf16[8,64,256]{2,1,0:T(8,128)(2,1)S(1)}, u32[]{:S(2)}, u32[]{:S(2)}) %all-to-all-start) | async-done | bytes 262176 | tf_op jit(solution)/shard_map/all_to_all | solution.py:44
  22.7 0.3 fusion.10
  23.0 0.4 fusion.50
  23.4 0.3 fusion.13
  23.7 1.4 fusion.1
  25.1 9.0 %all-to-all-start.1 = ((bf16[64,8,1024]{2,1,0:T(8,128)(2,1)}), bf16[64,8,1024]{2,1,0:T(8,128)(2,1)S(1)}, u32[]{:S(2)}, u32[]{:S(2)}) async-start(bf16[64,8,1024]{2,1,0:T(8,128)(2,1)} %fusion.1), calls=%async_computation.1 | async-start | bytes 2097152 | tf_op jit(solution)/shard_map/all_to_all | solution.py:215
  34.2 0.1 fusion.14
  34.3 0.4 convolution_convert_fusion
  34.8 3.4 %collective-permute-start.4 = (bf16[512,1024]{1,0:T(8,128)(2,1)S(1)}, bf16[512,1024]{1,0:T(8,128)(2,1)}, u32[]{:S(2)}, u32[]{:S(2)}) collective-permute-start(bf16[512,1024]{1,0:T(8,128)(2,1)S(1)} %convolution_convert_fusion), channel_id=1, source_target_pairs={{0,32},{32,0},{1,33},{33,1},{2,34},{34,2},{3,35},{35,3},{4,36},{36... | collective-permute-start | bytes 3145736 | tf_op jit(solution)/shard_map/ppermute | solution.py:219
  38.2 2.4 %collective-permute-done.4 = bf16[512,1024]{1,0:T(8,128)(2,1)} collective-permute-done((bf16[512,1024]{1,0:T(8,128)(2,1)S(1)}, bf16[512,1024]{1,0:T(8,128)(2,1)}, u32[]{:S(2)}, u32[]{:S(2)}) %collective-permute-start.4) | collective-permute-done | bytes 1048608 | tf_op jit(solution)/shard_map/ppermute | solution.py:219
  40.6 20.2 %all-to-all-done.1 = bf16[64,8,1024]{2,1,0:T(8,128)(2,1)S(1)} async-done(((bf16[64,8,1024]{2,1,0:T(8,128)(2,1)}), bf16[64,8,1024]{2,1,0:T(8,128)(2,1)S(1)}, u32[]{:S(2)}, u32[]{:S(2)}) %all-to-all-start.1) | async-done | bytes 1048608 | tf_op jit(solution)/shard_map/all_to_all | solution.py:215
  60.8 9.3 %all-to-all-start.2 = ((bf16[64,8,1024]{2,1,0:T(8,128)(2,1)}), bf16[64,8,1024]{2,1,0:T(8,128)(2,1)S(1)}, u32[]{:S(2)}, u32[]{:S(2)}) async-start(bf16[64,8,1024]{2,1,0:T(8,128)(2,1)} %bitcast.18), calls=%async_computation.2 | async-start | bytes 2097152 | tf_op jit(solution)/shard_map/all_to_all | solution.py:215
  70.1 4.0 %shard_map.100 = (bf16[128,1664]{1,0:T(8,128)(2,1)S(1)}, bf16[128,1664]{1,0:T(8,128)(2,1)S(1)}, bf16[128,1664]{1,0:T(8,128)(2,1)S(1)}, bf16[128,1664]{1,0:T(8,128)(2,1)S(1)}) custom-call(s32[1]{0:T(128)} %bitcast.11.here, bf16[512,1024]{1,0:T(8,128)(2,1)S(1)} %bitcast.69, bf16[1,1024]{1,0:T(2,128)(2,1)S(1)} %broadcast_in_dim.115.gain, ...), custom_call_target="tpu_custom_call" | custom-call | flops 1610612736 | bytes 5898240 | tf_op jit(solution)/shard_map/pallas_call | solution.py:107
  74.1 4.6 %collective-permute-start = (bf16[128,1664]{1,0:T(8,128)(2,1)S(1)}, bf16[128,1664]{1,0:T(8,128)(2,1)S(1)}, u32[]{:S(2)}, u32[]{:S(2)}) collective-permute-start(bf16[128,1664]{1,0:T(8,128)(2,1)S(1)} %get-tuple-element.20), channel_id=1, source_target_pairs={{0,2},{1,3},{2,0},{3,1},{4,6},{5,7},{6,4},{7,5},{8,10},{9,11},{10,... | collective-permute-start | bytes 1277960 | tf_op jit(solution)/shard_map/ppermute | solution.py:277
  78.7 2.2 %collective-permute-start.1 = (bf16[128,1664]{1,0:T(8,128)(2,1)S(1)}, bf16[128,1664]{1,0:T(8,128)(2,1)S(1)}, u32[]{:S(2)}, u32[]{:S(2)}) collective-permute-start(bf16[128,1664]{1,0:T(8,128)(2,1)S(1)} %get-tuple-element.21), channel_id=1, source_target_pairs={{0,1},{1,2},{2,3},{3,0},{4,5},{5,6},{6,7},{7,4},{8,9},{9,10},{10,1... | collective-permute-start | bytes 1277960 | tf_op jit(solution)/shard_map/ppermute | solution.py:277
  80.9 4.3 %collective-permute-start.2 = (bf16[128,1664]{1,0:T(8,128)(2,1)S(1)}, bf16[128,1664]{1,0:T(8,128)(2,1)S(1)}, u32[]{:S(2)}, u32[]{:S(2)}) collective-permute-start(bf16[128,1664]{1,0:T(8,128)(2,1)S(1)} %get-tuple-element.22), channel_id=1, source_target_pairs={{0,3},{1,0},{2,1},{3,2},{4,7},{5,4},{6,5},{7,6},{8,11},{9,8},{10,9... | collective-permute-start | bytes 1277960 | tf_op jit(solution)/shard_map/ppermute | solution.py:277
  85.2 2.4 %collective-permute-done = bf16[128,1664]{1,0:T(8,128)(2,1)S(1)} collective-permute-done((bf16[128,1664]{1,0:T(8,128)(2,1)S(1)}, bf16[128,1664]{1,0:T(8,128)(2,1)S(1)}, u32[]{:S(2)}, u32[]{:S(2)}) %collective-permute-start) | collective-permute-done | bytes 426016 | tf_op jit(solution)/shard_map/ppermute | solution.py:277
  87.6 0.1 convert_add_fusion.1.refs_0_
  87.7 10.7 %collective-permute-done.1.refs_1_ = bf16[128,1664]{1,0:T(8,128)(2,1)S(1)} collective-permute-done((bf16[128,1664]{1,0:T(8,128)(2,1)S(1)}, bf16[128,1664]{1,0:T(8,128)(2,1)S(1)}, u32[]{:S(2)}, u32[]{:S(2)}) %collective-permute-start.1) | collective-permute-done | bytes 426016 | tf_op jit(solution)/shard_map/ppermute | solution.py:277
  98.3 0.0 collective-permute-done.2.refs_2_
  98.3 0.3 shard_map.101.rest_0_.refs_0_
  98.7 3.7 %collective-permute-start.6 = (bf16[128,768]{1,0:T(8,128)(2,1)S(1)}, bf16[128,768]{1,0:T(8,128)(2,1)}, u32[]{:S(2)}, u32[]{:S(2)}) collective-permute-start(bf16[128,768]{1,0:T(8,128)(2,1)S(1)} %shard_map.101.rest_0_.refs_0_), channel_id=1, source_target_pairs={{0,3},{1,0},{2,1},{3,2},{4,7},{5,4},{6,5},{7,6},{8,11},{9,8},{10,9... | collective-permute-start | bytes 589832 | tf_op jit(solution)/shard_map/ppermute | solution.py:277
  102.4 1.9 collective-permute-start.3
  104.3 4.3 %collective-permute-start.5 = (bf16[128,768]{1,0:T(8,128)(2,1)S(1)}, bf16[128,768]{1,0:T(8,128)(2,1)}, u32[]{:S(2)}, u32[]{:S(2)}) collective-permute-start(bf16[128,768]{1,0:T(8,128)(2,1)S(1)} %shard_map.101.rest_0_.refs_0_), channel_id=1, source_target_pairs={{0,2},{1,3},{2,0},{3,1},{4,6},{5,7},{6,4},{7,5},{8,10},{9,11},{10,... | collective-permute-start | bytes 589832 | tf_op jit(solution)/shard_map/ppermute | solution.py:277
  108.6 0.0 all-to-all-done.2
  108.6 0.0 copy-start.1
  108.6 5.0 %shard_map.102 = (bf16[128,1664]{1,0:T(8,128)(2,1)S(1)}, bf16[128,1664]{1,0:T(8,128)(2,1)}, bf16[128,1664]{1,0:T(8,128)(2,1)}, bf16[128,1664]{1,0:T(8,128)(2,1)}) custom-call(s32[1]{0:T(128)} %bitcast.11.here, bf16[512,1024]{1,0:T(8,128)(2,1)S(1)} %bitcast.68, bf16[1,1024]{1,0:T(2,128)(2,1)S(1)} %broadcast_in_dim.115.gain, bf16[1024,768]{1,0:T(8,128)(2,1)} %bitcast.77, ...), custom_call_target="tpu_custom_call" | custom-call | flops 1610612736 | bytes 5898240 | tf_op jit(solution)/shard_map/pallas_call | solution.py:107
  113.7 0.0 collective-permute-done.6.refs_3_
  113.7 2.8 %collective-permute-start.9 = (bf16[128,1664]{1,0:T(8,128)(2,1)}, bf16[128,1664]{1,0:T(8,128)(2,1)}, u32[]{:S(2)}, u32[]{:S(2)}) collective-permute-start(bf16[128,1664]{1,0:T(8,128)(2,1)} %get-tuple-element.32), channel_id=1, source_target_pairs={{0,3},{1,0},{2,1},{3,2},{4,7},{5,4},{6,5},{7,6},{8,11},{9,8},{10,9... | collective-permute-start | bytes 1277960 | tf_op jit(solution)/shard_map/ppermute | solution.py:277
  116.5 0.0 collective-permute-done.3.refs_1_
  116.5 2.5 %collective-permute-start.8 = (bf16[128,1664]{1,0:T(8,128)(2,1)}, bf16[128,1664]{1,0:T(8,128)(2,1)}, u32[]{:S(2)}, u32[]{:S(2)}) collective-permute-start(bf16[128,1664]{1,0:T(8,128)(2,1)} %get-tuple-element.31), channel_id=1, source_target_pairs={{0,1},{1,2},{2,3},{3,0},{4,5},{5,6},{6,7},{7,4},{8,9},{9,10},{10,1... | collective-permute-start | bytes 1277960 | tf_op jit(solution)/shard_map/ppermute | solution.py:277
  119.0 0.0 collective-permute-done.5.refs_2_
  119.0 3.1 %collective-permute-start.7 = (bf16[128,1664]{1,0:T(8,128)(2,1)}, bf16[128,1664]{1,0:T(8,128)(2,1)}, u32[]{:S(2)}, u32[]{:S(2)}) collective-permute-start(bf16[128,1664]{1,0:T(8,128)(2,1)} %get-tuple-element.30), channel_id=1, source_target_pairs={{0,2},{1,3},{2,0},{3,1},{4,6},{5,7},{6,4},{7,5},{8,10},{9,11},{10,... | collective-permute-start | bytes 1277960 | tf_op jit(solution)/shard_map/ppermute | solution.py:277
  122.2 3.3 %shard_map.103 = bf16[512,1024]{1,0:T(8,128)(2,1)} custom-call(s32[1]{0:T(128)} %bitcast.11.here, bf16[128,768]{1,0:T(8,128)(2,1)S(1)} %shard_map.101.rest_0_.refs_0_, bf16[128,768]{1,0:T(8,128)(2,1)} %collective-permute-done.3.refs_1_, bf16[128,768]{1,0:T(8,128)(2,1)} %collective-permute-done.5.refs_2_, bf16[128,768]{1,0:T(8,128)(2,1)} %collective-permute-done.6.refs_3_, ...), custom_call_target="tpu_custom_call" | custom-call | flops 805306368 | bytes 3407872 | tf_op jit(solution)/shard_map/pallas_call | solution.py:148
  125.5 11.9 %all-to-all-start.3 = ((bf16[64,8,1024]{2,1,0:T(8,128)(2,1)}), bf16[64,8,1024]{2,1,0:T(8,128)(2,1)S(1)}, u32[]{:S(2)}, u32[]{:S(2)}) async-start(bf16[64,8,1024]{2,1,0:T(8,128)(2,1)} %bitcast.21), calls=%async_computation.3 | async-start | bytes 2097152 | tf_op jit(solution)/shard_map/all_to_all | solution.py:215
  137.3 0.0 collective-permute-done.8
  137.4 0.2 collective-permute-done.7
  137.5 1.5 convert_add_fusion
  139.0 0.2 fusion.41
  139.2 0.2 fusion.20
  139.4 11.3 %all_gather.3.refs_0_ = bf16[512,768]{1,0:T(8,128)(2,1)S(1)} all-gather(bf16[128,768]{1,0:T(8,128)(2,1)S(1)} %fusion.20), channel_id=1, replica_groups=mesh['y'=8,'core'=2,'expert'=8,'tensor'=4] {'tensor'}, dimensions={0}, use_global_device_ids=true | all-gather | bytes 983040 | tf_op jit(solution)/shard_map/all_gather | solution.py:309
  150.7 1.4 shard_map.104
  152.1 0.0 copy-start.4
  152.2 0.0 copy-start.5
  152.2 0.0 copy-start.3
  152.2 7.9 %collective-permute-start.10 = (bf16[512,1024]{1,0:T(8,128)(2,1)S(1)}, bf16[512,1024]{1,0:T(8,128)(2,1)}, u32[]{:S(2)}, u32[]{:S(2)}) collective-permute-start(bf16[512,1024]{1,0:T(8,128)(2,1)S(1)} %shard_map.104), channel_id=1, source_target_pairs={{0,32},{32,0},{1,33},{33,1},{2,34},{34,2},{3,35},{35,3},{4,36},{36... | collective-permute-start | bytes 3145736 | tf_op jit(solution)/shard_map/ppermute | solution.py:219
  160.1 2.4 %collective-permute-done.10 = bf16[512,1024]{1,0:T(8,128)(2,1)} collective-permute-done((bf16[512,1024]{1,0:T(8,128)(2,1)S(1)}, bf16[512,1024]{1,0:T(8,128)(2,1)}, u32[]{:S(2)}, u32[]{:S(2)}) %collective-permute-start.10) | collective-permute-done | bytes 1048608 | tf_op jit(solution)/shard_map/ppermute | solution.py:219
  162.5 0.3 all-to-all-done.3
  162.7 12.0 %all-to-all-start.4 = ((bf16[64,8,1024]{2,1,0:T(8,128)(2,1)}), bf16[64,8,1024]{2,1,0:T(8,128)(2,1)S(1)}, u32[]{:S(2)}, u32[]{:S(2)}) async-start(bf16[64,8,1024]{2,1,0:T(8,128)(2,1)} %bitcast.23), calls=%async_computation.4 | async-start | bytes 2097152 | tf_op jit(solution)/shard_map/all_to_all | solution.py:215
  174.8 0.1 fusion.21
  174.9 0.1 pad_maximum_fusion.2
  175.0 0.1 pad_maximum_fusion.1
  175.2 0.5 convolution_bitcast_fusion.1
  175.7 26.0 %all-to-all-done.4 = bf16[64,8,1024]{2,1,0:T(8,128)(2,1)S(1)} async-done(((bf16[64,8,1024]{2,1,0:T(8,128)(2,1)}), bf16[64,8,1024]{2,1,0:T(8,128)(2,1)S(1)}, u32[]{:S(2)}, u32[]{:S(2)}) %all-to-all-start.4) | async-done | bytes 1048608 | tf_op jit(solution)/shard_map/all_to_all | solution.py:215
  201.7 0.5 convolution_bitcast_fusion
  202.2 0.7 fusion.24
  (18 shorter events, 0.1 us)
Async XLA Ops:
  0.0 22.7 %copy-start = (bf16[64,1024]{1,0:T(8,128)(2,1)S(1)}, bf16[64,1024]{1,0:T(8,128)(2,1)}, u32[]{:S(2)}) copy-start(bf16[64,1024]{1,0:T(8,128)(2,1)} %param.10) | copy-start | bytes 393220
  1.5 21.2 %all-to-all-start = ((bf16[8,64,256]{2,1,0:T(8,128)(2,1)}), bf16[8,64,256]{2,1,0:T(8,128)(2,1)S(1)}, u32[]{:S(2)}, u32[]{:S(2)}) async-start(bf16[8,64,256]{2,1,0:T(8,128)(2,1)} %broadcast_in_dim.106), calls=%async_computation | async-start | bytes 524288 | tf_op jit(solution)/shard_map/all_to_all | solution.py:44
  25.1 35.6 %all-to-all-start.1 = ((bf16[64,8,1024]{2,1,0:T(8,128)(2,1)}), bf16[64,8,1024]{2,1,0:T(8,128)(2,1)S(1)}, u32[]{:S(2)}, u32[]{:S(2)}) async-start(bf16[64,8,1024]{2,1,0:T(8,128)(2,1)} %fusion.1), calls=%async_computation.1 | async-start | bytes 2097152 | tf_op jit(solution)/shard_map/all_to_all | solution.py:215
  34.3 26.4 %copy-start.2 = (s32[64,64]{1,0:T(8,128)}, s32[64,64]{1,0:T(8,128)S(1)}, u32[]{:S(2)}) copy-start(s32[64,64]{1,0:T(8,128)S(1)} %fusion.14) | copy-start | bytes 49156
  34.3 35.7 %copy-start.6 = (bf16[1024]{0:T(1024)(128)(2,1)S(1)}, bf16[1024]{0:T(1024)(128)(2,1)}, u32[]{:S(2)}) copy-start(bf16[1024]{0:T(1024)(128)(2,1)} %param.14) | copy-start | bytes 6148
  34.8 5.8 %collective-permute-start.4 = (bf16[512,1024]{1,0:T(8,128)(2,1)S(1)}, bf16[512,1024]{1,0:T(8,128)(2,1)}, u32[]{:S(2)}, u32[]{:S(2)}) collective-permute-start(bf16[512,1024]{1,0:T(8,128)(2,1)S(1)} %convolution_convert_fusion), channel_id=1, source_target_pairs={{0,32},{32,0},{1,33},{33,1},{2,34},{34,2},{3,35},{35,3},{4,36},{36... | collective-permute-start | bytes 3145736 | tf_op jit(solution)/shard_map/ppermute | solution.py:219
  60.8 47.9 %all-to-all-start.2 = ((bf16[64,8,1024]{2,1,0:T(8,128)(2,1)}), bf16[64,8,1024]{2,1,0:T(8,128)(2,1)S(1)}, u32[]{:S(2)}, u32[]{:S(2)}) async-start(bf16[64,8,1024]{2,1,0:T(8,128)(2,1)} %bitcast.18), calls=%async_computation.2 | async-start | bytes 2097152 | tf_op jit(solution)/shard_map/all_to_all | solution.py:215
  74.1 13.5 %collective-permute-start = (bf16[128,1664]{1,0:T(8,128)(2,1)S(1)}, bf16[128,1664]{1,0:T(8,128)(2,1)S(1)}, u32[]{:S(2)}, u32[]{:S(2)}) collective-permute-start(bf16[128,1664]{1,0:T(8,128)(2,1)S(1)} %get-tuple-element.20), channel_id=1, source_target_pairs={{0,2},{1,3},{2,0},{3,1},{4,6},{5,7},{6,4},{7,5},{8,10},{9,11},{10,... | collective-permute-start | bytes 1277960 | tf_op jit(solution)/shard_map/ppermute | solution.py:277
  78.7 19.6 %collective-permute-start.1 = (bf16[128,1664]{1,0:T(8,128)(2,1)S(1)}, bf16[128,1664]{1,0:T(8,128)(2,1)S(1)}, u32[]{:S(2)}, u32[]{:S(2)}) collective-permute-start(bf16[128,1664]{1,0:T(8,128)(2,1)S(1)} %get-tuple-element.21), channel_id=1, source_target_pairs={{0,1},{1,2},{2,3},{3,0},{4,5},{5,6},{6,7},{7,4},{8,9},{9,10},{10,1... | collective-permute-start | bytes 1277960 | tf_op jit(solution)/shard_map/ppermute | solution.py:277
  80.9 17.4 %collective-permute-start.2 = (bf16[128,1664]{1,0:T(8,128)(2,1)S(1)}, bf16[128,1664]{1,0:T(8,128)(2,1)S(1)}, u32[]{:S(2)}, u32[]{:S(2)}) collective-permute-start(bf16[128,1664]{1,0:T(8,128)(2,1)S(1)} %get-tuple-element.22), channel_id=1, source_target_pairs={{0,3},{1,0},{2,1},{3,2},{4,7},{5,4},{6,5},{7,6},{8,11},{9,8},{10,9... | collective-permute-start | bytes 1277960 | tf_op jit(solution)/shard_map/ppermute | solution.py:277
  98.7 15.0 %collective-permute-start.6 = (bf16[128,768]{1,0:T(8,128)(2,1)S(1)}, bf16[128,768]{1,0:T(8,128)(2,1)}, u32[]{:S(2)}, u32[]{:S(2)}) collective-permute-start(bf16[128,768]{1,0:T(8,128)(2,1)S(1)} %shard_map.101.rest_0_.refs_0_), channel_id=1, source_target_pairs={{0,3},{1,0},{2,1},{3,2},{4,7},{5,4},{6,5},{7,6},{8,11},{9,8},{10,9... | collective-permute-start | bytes 589832 | tf_op jit(solution)/shard_map/ppermute | solution.py:277
  102.4 14.1 %collective-permute-start.3 = (bf16[128,768]{1,0:T(8,128)(2,1)S(1)}, bf16[128,768]{1,0:T(8,128)(2,1)}, u32[]{:S(2)}, u32[]{:S(2)}) collective-permute-start(bf16[128,768]{1,0:T(8,128)(2,1)S(1)} %shard_map.101.rest_0_.refs_0_), channel_id=1, source_target_pairs={{0,1},{1,2},{2,3},{3,0},{4,5},{5,6},{6,7},{7,4},{8,9},{9,10},{10,1... | collective-permute-start | bytes 589832 | tf_op jit(solution)/shard_map/ppermute | solution.py:277
  104.3 14.7 %collective-permute-start.5 = (bf16[128,768]{1,0:T(8,128)(2,1)S(1)}, bf16[128,768]{1,0:T(8,128)(2,1)}, u32[]{:S(2)}, u32[]{:S(2)}) collective-permute-start(bf16[128,768]{1,0:T(8,128)(2,1)S(1)} %shard_map.101.rest_0_.refs_0_), channel_id=1, source_target_pairs={{0,2},{1,3},{2,0},{3,1},{4,6},{5,7},{6,4},{7,5},{8,10},{9,11},{10,... | collective-permute-start | bytes 589832 | tf_op jit(solution)/shard_map/ppermute | solution.py:277
  108.6 13.5 %copy-start.1 = (bf16[1,768,1024]{2,1,0:T(8,128)(2,1)S(1)}, bf16[1,768,1024]{2,1,0:T(8,128)(2,1)}, u32[]{:S(2)}) copy-start(bf16[1,768,1024]{2,1,0:T(8,128)(2,1)} %param.19) | copy-start | bytes 4718596
  113.7 23.6 %collective-permute-start.9 = (bf16[128,1664]{1,0:T(8,128)(2,1)}, bf16[128,1664]{1,0:T(8,128)(2,1)}, u32[]{:S(2)}, u32[]{:S(2)}) collective-permute-start(bf16[128,1664]{1,0:T(8,128)(2,1)} %get-tuple-element.32), channel_id=1, source_target_pairs={{0,3},{1,0},{2,1},{3,2},{4,7},{5,4},{6,5},{7,6},{8,11},{9,8},{10,9... | collective-permute-start | bytes 1277960 | tf_op jit(solution)/shard_map/ppermute | solution.py:277
  116.5 20.9 %collective-permute-start.8 = (bf16[128,1664]{1,0:T(8,128)(2,1)}, bf16[128,1664]{1,0:T(8,128)(2,1)}, u32[]{:S(2)}, u32[]{:S(2)}) collective-permute-start(bf16[128,1664]{1,0:T(8,128)(2,1)} %get-tuple-element.31), channel_id=1, source_target_pairs={{0,1},{1,2},{2,3},{3,0},{4,5},{5,6},{6,7},{7,4},{8,9},{9,10},{10,1... | collective-permute-start | bytes 1277960 | tf_op jit(solution)/shard_map/ppermute | solution.py:277
  119.0 18.5 %collective-permute-start.7 = (bf16[128,1664]{1,0:T(8,128)(2,1)}, bf16[128,1664]{1,0:T(8,128)(2,1)}, u32[]{:S(2)}, u32[]{:S(2)}) collective-permute-start(bf16[128,1664]{1,0:T(8,128)(2,1)} %get-tuple-element.30), channel_id=1, source_target_pairs={{0,2},{1,3},{2,0},{3,1},{4,6},{5,7},{6,4},{7,5},{8,10},{9,11},{10,... | collective-permute-start | bytes 1277960 | tf_op jit(solution)/shard_map/ppermute | solution.py:277
  125.5 37.3 %all-to-all-start.3 = ((bf16[64,8,1024]{2,1,0:T(8,128)(2,1)}), bf16[64,8,1024]{2,1,0:T(8,128)(2,1)S(1)}, u32[]{:S(2)}, u32[]{:S(2)}) async-start(bf16[64,8,1024]{2,1,0:T(8,128)(2,1)} %bitcast.21), calls=%async_computation.3 | async-start | bytes 2097152 | tf_op jit(solution)/shard_map/all_to_all | solution.py:215
  152.1 22.6 %copy-start.4 = (s32[64,8]{0,1:T(8,128)S(1)}, s32[64,8]{0,1:T(8,128)}, u32[]{:S(2)}) copy-start(s32[64,8]{0,1:T(8,128)} %param.15) | copy-start | bytes 6148
  152.2 22.6 %copy-start.5 = (f32[64,8]{0,1:T(8,128)S(1)}, f32[64,8]{0,1:T(8,128)}, u32[]{:S(2)}) copy-start(f32[64,8]{0,1:T(8,128)} %param.16) | copy-start | bytes 6148
  152.2 23.0 %copy-start.3 = (s32[64,64]{1,0:T(8,128)S(1)}, s32[64,64]{1,0:T(8,128)}, u32[]{:S(2)}) copy-start(s32[64,64]{1,0:T(8,128)} %copy-done.2) | copy-start | bytes 49156
  152.2 10.3 %collective-permute-start.10 = (bf16[512,1024]{1,0:T(8,128)(2,1)S(1)}, bf16[512,1024]{1,0:T(8,128)(2,1)}, u32[]{:S(2)}, u32[]{:S(2)}) collective-permute-start(bf16[512,1024]{1,0:T(8,128)(2,1)S(1)} %shard_map.104), channel_id=1, source_target_pairs={{0,32},{32,0},{1,33},{33,1},{2,34},{34,2},{3,35},{35,3},{4,36},{36... | collective-permute-start | bytes 3145736 | tf_op jit(solution)/shard_map/ppermute | solution.py:219
  162.7 39.0 %all-to-all-start.4 = ((bf16[64,8,1024]{2,1,0:T(8,128)(2,1)}), bf16[64,8,1024]{2,1,0:T(8,128)(2,1)S(1)}, u32[]{:S(2)}, u32[]{:S(2)}) async-start(bf16[64,8,1024]{2,1,0:T(8,128)(2,1)} %bitcast.23), calls=%async_computation.4 | async-start | bytes 2097152 | tf_op jit(solution)/shard_map/all_to_all | solution.py:215
